TPU v7x, 1024 devices: a whole 8x8x8 slice. The times are simulated.
1024 devices in a mesh: dp: 16 (over y, core), expert: 64 (over x, z).
Axes of the slice: x: 8, y: 8, z: 8, core: 2. Of those that a mesh axis runs over, the one named last changes fastest.
Arguments:
- layer_input: bfloat16 [32768, 4096], P(('dp', 'expert')), may hold values from -6 to 6
- out_grad: bfloat16 [32768, 4096], P(('dp', 'expert')), may hold values from -6 to 6
- expert_ids: int32 [131072, 2], P(('dp', 'expert')), may hold values from 0 to 63, all different within a row; in each aligned block of 128 rows (0 to 127, 128 to 255, ...) at most 5 rows name the same one
- gates: bfloat16 [131072, 2], P(('dp', 'expert')), may hold values from 0.099609375 to 0.8984375
- up_weight: bfloat16 [64, 1024, 1024], P('expert'), may hold values from -0.1875 to 0.1875
- down_weight: bfloat16 [64, 1024, 1024], P('expert'), may hold values from -0.1875 to 0.1875
Outputs:
- input_grad: bfloat16 [32768, 4096], P(('dp', 'expert'))
- gate_grad: bfloat16 [131072, 2], P(('dp', 'expert'))
- up_grad: float32 [64, 1024, 1024], P('expert', 'dp')
- down_grad: float32 [64, 1024, 1024], P('expert', 'dp')
Inputs may be any that keep to these rules, and one draw needn't show every extreme that they name: `expert_ids`: within the 128 sub-tokens of one device, each expert is chosen by at most 5 of them, and some expert reaches 5 in some device's rows; the 2 experts of a sub-token differ.
All inputs are finite; a program needn't handle non-finite values.
Results may differ from a plain program's by a relative error of at most 0.023.
Values may be sent and summed in bfloat16 or wider, within the bound.
No kernel may reach another device: no remote copies, remote signals or barrier semaphores. Data moves between devices by JAX's collectives and lax.ppermute only.
A program may use at most 32 MiB of HBM per device.

v0:
```python
import jax
import jax.numpy as jnp
from jax import lax
from jax.sharding import PartitionSpec as P

TOP = 2


def silu_slope(pre_act):
    sig_val = jax.nn.sigmoid(pre_act)
    return sig_val * (1.0 + pre_act * (1.0 - sig_val))


def outer_sum(left, right):
    return lax.dot_general(
        left, right, (((0,), (0,)), ((), ())), preferred_element_type=jnp.float32
    )


def body(layer_input, out_grad, expert_ids, gates, up_weight, down_weight):
    width = up_weight.shape[1]
    sub_in = layer_input.reshape(-1, width)
    sub_grad = out_grad.reshape(-1, width)
    block = sub_in.shape[0]
    assigns = block * TOP
    experts = lax.axis_size("expert") * up_weight.shape[0]
    capacity = max(2, 5 * assigns // (4 * experts))
    flat_ids = expert_ids.reshape(-1)
    onehot = (flat_ids[:, None] == jnp.arange(experts, dtype=jnp.int32)[None, :]).astype(jnp.int32)
    before = jnp.cumsum(onehot, axis=0) - onehot
    slots = jnp.sum(before * onehot, axis=1)
    dest = flat_ids * capacity + slots
    source_rows = jnp.arange(assigns, dtype=jnp.int32) // TOP
    send_in = jnp.zeros((experts * capacity, width), jnp.bfloat16).at[dest].set(sub_in[source_rows])
    send_grad = (
        jnp.zeros((experts * capacity, width), jnp.bfloat16).at[dest].set(sub_grad[source_rows])
    )
    send_gate = jnp.zeros((experts * capacity,), jnp.bfloat16).at[dest].set(gates.reshape(-1))
    recv_in, recv_grad, recv_gate = (
        lax.all_to_all(
            send_in.reshape(experts, capacity, width),
            "expert",
            split_axis=0,
            concat_axis=0,
            tiled=True,
        ),
        lax.all_to_all(
            send_grad.reshape(experts, capacity, width),
            "expert",
            split_axis=0,
            concat_axis=0,
            tiled=True,
        ),
        lax.all_to_all(
            send_gate.reshape(experts, capacity), "expert", split_axis=0, concat_axis=0, tiled=True
        ),
    )
    features = recv_in.reshape(-1, width)
    upstream = recv_grad.reshape(-1, width)
    gate_vals = recv_gate.reshape(-1).astype(jnp.float32)[:, None]
    w_up = up_weight[0]
    w_down = down_weight[0]
    pre_act = jnp.dot(features, w_up, preferred_element_type=jnp.float32)
    hidden = jax.nn.silu(pre_act).astype(jnp.bfloat16)
    back_proj = jnp.dot(upstream, w_down.T, preferred_element_type=jnp.float32)
    gate_part = jnp.sum(hidden.astype(jnp.float32) * back_proj, axis=1).astype(jnp.bfloat16)
    scaled = (gate_vals * upstream.astype(jnp.float32)).astype(jnp.bfloat16)
    hidden_grad = (gate_vals * back_proj * silu_slope(pre_act)).astype(jnp.bfloat16)
    pieces = jnp.dot(hidden_grad, w_up.T, preferred_element_type=jnp.float32).astype(jnp.bfloat16)
    back_pieces, back_gate = (
        lax.all_to_all(
            pieces.reshape(experts, capacity, width),
            "expert",
            split_axis=0,
            concat_axis=0,
            tiled=True,
        ),
        lax.all_to_all(
            gate_part.reshape(experts, capacity), "expert", split_axis=0, concat_axis=0, tiled=True
        ),
    )
    up_share, down_share = (
        lax.psum_scatter(
            outer_sum(features, hidden_grad).astype(jnp.bfloat16),
            "dp",
            scatter_dimension=0,
            tiled=True,
        ).astype(jnp.float32),
        lax.psum_scatter(
            outer_sum(hidden, scaled).astype(jnp.bfloat16), "dp", scatter_dimension=0, tiled=True
        ).astype(jnp.float32),
    )
    chosen = back_pieces.reshape(experts * capacity, width)[dest].astype(jnp.float32)
    input_grad = jnp.sum(chosen.reshape(block, TOP, width), axis=1).astype(jnp.bfloat16)
    gate_grad = back_gate.reshape(-1)[dest].reshape(block, TOP)
    return (input_grad.reshape(layer_input.shape), gate_grad, up_share[None], down_share[None])


def solution(mesh):
    placed = (
        P(("dp", "expert"), None),
        P(("dp", "expert"), None),
        P(("dp", "expert"), None),
        P(("dp", "expert"), None),
        P("expert", None, None),
        P("expert", None, None),
    )
    return jax.shard_map(
        body,
        mesh=mesh,
        in_specs=placed,
        out_specs=(
            P(("dp", "expert"), None),
            P(("dp", "expert"), None),
            P("expert", "dp", None),
            P("expert", "dp", None),
        ),
        check_vma=False,
    )
```

profile of v0, /device:TPU:1, one launch (start us, length us, event | category | flops | bytes accessed | tf_op | source)
XLA Modules:
  0.0 266.0 jit_solution(3244774150637629760)
XLA Ops:
  11.2 2.2 scatter_custom_fusion
  14.2 23.2 %all-to-all-start = ((bf16[64,1,5]{2,1,0:T(2,128)(2,1)}), bf16[64,1,5]{2,1,0:T(2,128)(2,1)S(1)}, u32[]{:S(2)}, u32[]{:S(2)}) async-start(bf16[64,1,5]{2,1,0:T(2,128)(2,1)} %all_to_all.25), calls=%async_computation | async-start | bytes 65536 | tf_op jit(solution)/shard_map/all_to_all | solution.py:54
  38.5 3.6 %scatter_custom_fusion.2 = bf16[320,1024]{1,0:T(8,128)(2,1)S(1)} fusion(s32[256]{0:T(256)S(1)} %bitcast.47, bf16[128,1024]{1,0:T(8,128)(2,1)S(1)} %reshape.171, s32[1024]{0:T(1024)S(1)} %pad_clamp_fusion.1, bf16[]{:T(256)} %constant.28.clone.1), kind=kCustom, calls=%fused_computation.22 | custom fusion | bytes 655362 | tf_op jit(solution)/shard_map/scatter | solution.py:34
  43.5 4.7 %all-to-all-done = bf16[64,1,5]{2,1,0:T(2,128)(2,1)S(1)} async-done(((bf16[64,1,5]{2,1,0:T(2,128)(2,1)}), bf16[64,1,5]{2,1,0:T(2,128)(2,1)S(1)}, u32[]{:S(2)}, u32[]{:S(2)}) %all-to-all-start) | async-done | bytes 672 | tf_op jit(solution)/shard_map/all_to_all | solution.py:54
  48.1 7.6 %all-to-all-start.2 = ((bf16[64,5,1024]{2,1,0:T(8,128)(2,1)}), bf16[64,5,1024]{2,1,0:T(8,128)(2,1)S(1)}, u32[]{:S(2)}, u32[]{:S(2)}) async-start(bf16[64,5,1024]{2,1,0:T(8,128)(2,1)} %reshape.172), calls=%async_computation.2 | async-start | bytes 2097152 | tf_op jit(solution)/shard_map/all_to_all | solution.py:40
  56.6 5.1 %scatter_custom_fusion.1 = bf16[320,1024]{1,0:T(8,128)(2,1)} fusion(s32[256]{0:T(256)S(1)} %bitcast.48, bf16[128,1024]{1,0:T(8,128)(2,1)} %reshape.168, s32[1024]{0:T(1024)S(1)} %pad_clamp_fusion.1, bf16[]{:T(256)} %constant.28.clone.1), kind=kCustom, calls=%fused_computation.24 | custom fusion | bytes 655872 | tf_op jit(solution)/shard_map/scatter | solution.py:36
  61.8 2.2 reshape.169
  63.9 18.4 %all-to-all-done.2 = bf16[64,5,1024]{2,1,0:T(8,128)(2,1)S(1)} async-done(((bf16[64,5,1024]{2,1,0:T(8,128)(2,1)}), bf16[64,5,1024]{2,1,0:T(8,128)(2,1)S(1)}, u32[]{:S(2)}, u32[]{:S(2)}) %all-to-all-start.2) | async-done | bytes 655392 | tf_op jit(solution)/shard_map/all_to_all | solution.py:40
  82.3 9.5 %all-to-all-start.1 = ((bf16[64,5,1024]{2,1,0:T(8,128)(2,1)}), bf16[64,5,1024]{2,1,0:T(8,128)(2,1)}, u32[]{:S(2)}, u32[]{:S(2)}) async-start(bf16[64,5,1024]{2,1,0:T(8,128)(2,1)} %reshape.169), calls=%async_computation.1 | async-start | bytes 2097152 | tf_op jit(solution)/shard_map/all_to_all | solution.py:47
  93.2 3.0 %fusion.2 = f32[320,1024]{1,0:T(8,128)} fusion(bf16[320,1024]{1,0:T(8,128)(2,1)} %reshape.173, bf16[1,1024,1024]{2,1,0:T(8,128)(2,1)S(1)} %copy-done), kind=kOutput, calls=%fused_computation.9 | convolution fusion | flops 671088640 | bytes 4063232 | tf_op jit(solution)/shard_map/dot_general | solution.py:63
  96.2 22.0 %all-to-all-done.1 = bf16[64,5,1024]{2,1,0:T(8,128)(2,1)} async-done(((bf16[64,5,1024]{2,1,0:T(8,128)(2,1)}), bf16[64,5,1024]{2,1,0:T(8,128)(2,1)}, u32[]{:S(2)}, u32[]{:S(2)}) %all-to-all-start.1) | async-done | bytes 655392 | tf_op jit(solution)/shard_map/all_to_all | solution.py:47
  119.6 3.4 %multiply_reduce_fusion = (bf16[320]{0:T(512)(128)(2,1)S(1)}, bf16[320,1024]{1,0:T(8,128)(2,1)S(1)}) fusion(f32[320,1024]{1,0:T(8,128)} %fusion.2, f32[320]{0:T(512)S(1)} %reshape.178, bf16[320,1024]{1,0:T(8,128)(2,1)S(1)} %reshape.170, bf16[1,1024,1024]{2,1,0:T(8,128)(2,1)} %param.11), kind=kOutput, calls=%fused_computation.17 | convolution fusion | flops 676003520 | bytes 4720512 | tf_op jit(solution)/shard_map/dot_general | solution.py:65
  123.9 2.6 convolution_convert_fusion.1
  126.6 4.0 %convolution_convert_fusion = bf16[1024,1024]{1,0:T(8,128)(2,1)} fusion(bf16[320,1024]{1,0:T(8,128)(2,1)S(1)} %reshape.170, f32[320]{0:T(512)S(1)} %reshape.178, f32[320,1024]{1,0:T(8,128)} %fusion.2), kind=kOutput, calls=%fused_computation.13 | convolution fusion | flops 674758656 | bytes 4064512 | tf_op jit(solution)/shard_map/dot_general | solution.py:15
  131.5 9.3 %all-to-all-start.4 = ((bf16[64,1,5]{2,1,0:T(2,128)(2,1)}), bf16[64,1,5]{2,1,0:T(2,128)(2,1)S(1)}, u32[]{:S(2)}, u32[]{:S(2)}) async-start(bf16[64,1,5]{2,1,0:T(2,128)(2,1)} %convert_element_type.90), calls=%async_computation.4 | async-start | bytes 65536 | tf_op jit(solution)/shard_map/all_to_all | solution.py:78
  140.8 2.0 fusion.6
  144.0 7.5 %all-to-all-done.4 = bf16[64,1,5]{2,1,0:T(2,128)(2,1)S(1)} async-done(((bf16[64,1,5]{2,1,0:T(2,128)(2,1)}), bf16[64,1,5]{2,1,0:T(2,128)(2,1)S(1)}, u32[]{:S(2)}, u32[]{:S(2)}) %all-to-all-start.4) | async-done | bytes 672 | tf_op jit(solution)/shard_map/all_to_all | solution.py:78
  151.5 5.7 %all-to-all-start.3 = ((bf16[64,5,1024]{2,1,0:T(8,128)(2,1)}), bf16[64,5,1024]{2,1,0:T(8,128)(2,1)}, u32[]{:S(2)}, u32[]{:S(2)}) async-start(bf16[64,5,1024]{2,1,0:T(8,128)(2,1)} %reshape.174), calls=%async_computation.3 | async-start | bytes 2097152 | tf_op jit(solution)/shard_map/all_to_all | solution.py:71
  157.5 1.9 gather_fusion.1
  160.2 22.8 %all-to-all-done.3 = bf16[64,5,1024]{2,1,0:T(8,128)(2,1)} async-done(((bf16[64,5,1024]{2,1,0:T(8,128)(2,1)}), bf16[64,5,1024]{2,1,0:T(8,128)(2,1)}, u32[]{:S(2)}, u32[]{:S(2)}) %all-to-all-start.3) | async-done | bytes 655392 | tf_op jit(solution)/shard_map/all_to_all | solution.py:71
  188.1 2.3 reduce-scatter.3.cloned.1.call-done
  190.5 1.6 bitcast_convert_fusion.1
  192.1 65.4 %reduce-scatter.5.cloned.1.call-done = bf16[64,1024]{1,0:T(8,128)(2,1)} async-done(((bf16[1024,1024]{1,0:T(8,128)(2,1)}), bf16[64,1024]{1,0:T(8,128)(2,1)}) %reduce-scatter.5.cloned.1.call-update) | async-done | bytes 131088 | tf_op jit(solution)/shard_map/reduce_scatter | solution.py:89
  257.5 1.6 bitcast_convert_fusion
  (49 shorter events, 19.9 us)
Async XLA Ops:
  7.2 86.1 %copy-start = (bf16[1,1024,1024]{2,1,0:T(8,128)(2,1)S(1)}, bf16[1,1024,1024]{2,1,0:T(8,128)(2,1)}, u32[]{:S(2)}) copy-start(bf16[1,1024,1024]{2,1,0:T(8,128)(2,1)} %param.10) | copy-start | bytes 6291460
  14.2 33.9 %all-to-all-start = ((bf16[64,1,5]{2,1,0:T(2,128)(2,1)}), bf16[64,1,5]{2,1,0:T(2,128)(2,1)S(1)}, u32[]{:S(2)}, u32[]{:S(2)}) async-start(bf16[64,1,5]{2,1,0:T(2,128)(2,1)} %all_to_all.25), calls=%async_computation | async-start | bytes 65536 | tf_op jit(solution)/shard_map/all_to_all | solution.py:54
  43.5 12.3 %copy-start.2 = (bf16[32,4096]{1,0:T(8,128)(2,1)S(1)}, bf16[32,4096]{1,0:T(8,128)(2,1)}, u32[]{:S(2)}) copy-start(bf16[32,4096]{1,0:T(8,128)(2,1)} %param.7) | copy-start | bytes 786436
  48.1 34.2 %all-to-all-start.2 = ((bf16[64,5,1024]{2,1,0:T(8,128)(2,1)}), bf16[64,5,1024]{2,1,0:T(8,128)(2,1)S(1)}, u32[]{:S(2)}, u32[]{:S(2)}) async-start(bf16[64,5,1024]{2,1,0:T(8,128)(2,1)} %reshape.172), calls=%async_computation.2 | async-start | bytes 2097152 | tf_op jit(solution)/shard_map/all_to_all | solution.py:40
  82.3 35.9 %all-to-all-start.1 = ((bf16[64,5,1024]{2,1,0:T(8,128)(2,1)}), bf16[64,5,1024]{2,1,0:T(8,128)(2,1)}, u32[]{:S(2)}, u32[]{:S(2)}) async-start(bf16[64,5,1024]{2,1,0:T(8,128)(2,1)} %reshape.169), calls=%async_computation.1 | async-start | bytes 2097152 | tf_op jit(solution)/shard_map/all_to_all | solution.py:47
  91.8 98.6 %reduce-scatter.3.cloned.1.call-start = ((), (), s32[]{:S(2)}) async-start(), calls=%async_computation.7 | async-start | bytes 2228224 | tf_op jit(solution)/shard_map/reduce_scatter | solution.py:83
  119.6 4.3 %copy-start.1 = (bf16[320,1024]{1,0:T(8,128)(2,1)S(1)}, bf16[320,1024]{1,0:T(8,128)(2,1)}, u32[]{:S(2)}) copy-start(bf16[320,1024]{1,0:T(8,128)(2,1)} %reshape.173) | copy-start | bytes 1966084
  123.0 0.9 copy-start.3
  126.6 131.0 %reduce-scatter.5.cloned.1.call-start = ((), (), s32[]{:S(2)}) async-start(), calls=%async_computation.8 | async-start | bytes 2228224 | tf_op jit(solution)/shard_map/reduce_scatter | solution.py:89
  131.5 20.1 %all-to-all-start.4 = ((bf16[64,1,5]{2,1,0:T(2,128)(2,1)}), bf16[64,1,5]{2,1,0:T(2,128)(2,1)S(1)}, u32[]{:S(2)}, u32[]{:S(2)}) async-start(bf16[64,1,5]{2,1,0:T(2,128)(2,1)} %convert_element_type.90), calls=%async_computation.4 | async-start | bytes 65536 | tf_op jit(solution)/shard_map/all_to_all | solution.py:78
  151.5 31.5 %all-to-all-start.3 = ((bf16[64,5,1024]{2,1,0:T(8,128)(2,1)}), bf16[64,5,1024]{2,1,0:T(8,128)(2,1)}, u32[]{:S(2)}, u32[]{:S(2)}) async-start(bf16[64,5,1024]{2,1,0:T(8,128)(2,1)} %reshape.174), calls=%async_computation.3 | async-start | bytes 2097152 | tf_op jit(solution)/shard_map/all_to_all | solution.py:71
Sparse Core Ops, SparseCore 0:
  126.7 63.7 reduce-scatter.2
  193.9 63.6 reduce-scatter.4
where the time goes:
time: 267 us; the launch traced here: 266 us
  waiting for transfers between devices  143 us (54%)
  starting transfers between devices  55.4 us (21%)
  local copies, waits for them, and re-layouts  31.8 us (12%)
  matrix products  15 us (6%)
  between operations  14.3 us (5%)
  other arithmetic  6.29 us (2%)
    reduce_scatter x1, waiting for transfers between devices, body(): lax.psum_scatter(outer_sum(hidden, scaled).astype(jnp.bfloat16), 'dp', sc...  65.4 us
    all_to_all x1, starting transfers between devices, body(): lax.all_to_all(send_gate.reshape(experts, capacity), 'expert', split_axis...  23.2 us
    all_to_all x1, waiting for transfers between devices, body(): lax.all_to_all(pieces.reshape(experts, capacity, width), 'expert', split_...  22.8 us
    all_to_all x1, waiting for transfers between devices, body(): lax.all_to_all(send_grad.reshape(experts, capacity, width), 'expert', spl...  22 us
    all_to_all x1, waiting for transfers between devices, body(): lax.all_to_all(send_in.reshape(experts, capacity, width), 'expert', split...  18.4 us
    all_to_all x1, starting transfers between devices, body(): lax.all_to_all(send_grad.reshape(experts, capacity, width), 'expert', spl...  9.54 us
    all_to_all x1, starting transfers between devices, body(): lax.all_to_all(gate_part.reshape(experts, capacity), 'expert', split_axis...  9.3 us
    scatter x2, local copies, waits for them, and re-layouts, body(): jnp.zeros((experts * capacity, width), jnp.bfloat16).at[dest]  8.79 us
  transfers between devices with their start and end apart: 7, of which 7 were waited for; matrix products, arithmetic and copies ran while one was open for 14% of the time, Pallas kernels for 0%

commit v1 on v0

v1 whole, which is shorter than its diff:
```python
import functools

import jax
import jax.numpy as jnp
from jax import lax
from jax.experimental import pallas as pl
from jax.experimental.pallas import tpu as pltpu
from jax.sharding import PartitionSpec as P

TOP = 2
SUB = 4
CAP = 5
LANE = 128
ROWS8 = 8
F32 = jnp.float32
BF16 = jnp.bfloat16
VMEM = pl.BlockSpec(memory_space=pltpu.VMEM)
SMEM = pl.BlockSpec(memory_space=pltpu.SMEM)


def iota(shape, dim):
    return lax.broadcasted_iota(jnp.int32, shape, dim)


def one_hot(mask):
    return jnp.where(mask, 1.0, 0.0).astype(BF16)


def mm(left, right):
    return jnp.dot(left, right, preferred_element_type=F32)


def mm_tr(left, right):
    return lax.dot_general(left, right, (((1,), (1,)), ((), ())), preferred_element_type=F32)


def tr_mm(left, right):
    return lax.dot_general(left, right, (((0,), (0,)), ((), ())), preferred_element_type=F32)


def by_sublane(peers):
    size = peers * ROWS8
    row, col = iota((size, size), 0), iota((size, size), 1)
    return one_hot(col == lax.rem(row, peers) * ROWS8 + lax.div(row, peers))


def by_peer(peers):
    size = peers * ROWS8
    row, col = iota((size, size), 0), iota((size, size), 1)
    return one_hot(col == lax.rem(row, ROWS8) * peers + lax.div(row, ROWS8))


def natural_order(block):
    tokens = block // SUB
    row, col = iota((block, block), 0), iota((block, block), 1)
    return one_hot(row == lax.rem(col, tokens) * SUB + lax.div(col, tokens))


def dispatch_kernel(x_ref, g_ref, ids_ref, gates_ref, out_ref, s_ref, rows, picks, packed):
    tokens = x_ref.shape[0]
    block = ids_ref.shape[1]
    peers = out_ref.shape[0] // ROWS8
    width = rows.shape[1]
    chunks = width // LANE
    top = jnp.concatenate(
        [ids_ref[...].astype(F32), gates_ref[...].astype(F32), jnp.zeros((4, block), F32)], axis=0
    ).astype(BF16)
    top = mm(top, natural_order(block))
    expert = iota((peers, block), 0).astype(F32)
    hot = [expert == top[k : k + 1] for k in range(TOP)]
    chosen = one_hot(hot[0] | hot[1])
    earlier = one_hot(iota((block, block), 0) < iota((block, block), 1))
    before = mm(chosen, earlier)
    weight = jnp.where(hot[0], top[2:3], jnp.where(hot[1], top[3:4], 0.0))
    for c in range(CAP):
        slot = pl.ds(c * peers, peers)
        here = before == float(c)
        for k in range(TOP):
            s_ref[k, slot, :] = one_hot(hot[k] & here)
        picks[0, slot, :] = one_hot((hot[0] | hot[1]) & here)
        picks[1, slot, :] = jnp.where(here, weight, 0.0).astype(BF16)
    for a, ref in enumerate((x_ref, g_ref)):
        for j in range(SUB):
            rows[j * tokens : (j + 1) * tokens, :] = ref[:, j * width : (j + 1) * width]
        sent = mm(picks[a], rows[...]).astype(BF16)
        for c in range(CAP):
            for j in range(chunks):
                packed[j * peers : (j + 1) * peers, (a * CAP + c) * LANE : (a * CAP + c + 1) * LANE] = (
                    sent[c * peers : (c + 1) * peers, j * LANE : (j + 1) * LANE]
                )
    out_ref[...] = mm(by_peer(peers), packed[...]).astype(BF16)


def unpack(source, target, peers, base):
    chunks = target.shape[1] // LANE
    for c in range(CAP):
        for j in range(chunks):
            target[c * peers : (c + 1) * peers, j * LANE : (j + 1) * LANE] = source[
                j * peers : (j + 1) * peers, (base + c) * LANE : (base + c + 1) * LANE
            ]


def expert_kernel(
    order, place_ref, in_ref, up_ref, down_ref, hg_ref, gate_ref, *rest
):
    n_chip = len(order)
    mine, theirs = rest[:n_chip], rest[n_chip : n_chip + 2]
    feat, scal, hid, left = rest[n_chip + 2 :]
    peers = in_ref.shape[0] // ROWS8
    width = up_ref.shape[0]
    chip, core = place_ref[0], place_ref[1]
    moved = mm(by_sublane(peers), in_ref[...]).astype(BF16)
    unpack(moved, feat, peers, 0)
    unpack(moved, scal, peers, CAP)
    pre = mm(feat[...], up_ref[...])
    sig = jax.nn.sigmoid(pre)
    hidden = (pre * sig).astype(BF16)
    hid[...] = hidden
    back = mm_tr(scal[...], down_ref[...])
    part = jnp.sum(hidden.astype(F32) * back, axis=1, keepdims=True)
    gate_ref[...] = jnp.broadcast_to(part, gate_ref.shape).astype(BF16)
    hg_ref[...] = (back * (sig * (1.0 + pre * (1.0 - sig)))).astype(BF16)
    piece = width // n_chip
    half = piece // 2
    first = core == 0
    for a, (source, right) in enumerate(((feat, hg_ref), (hid, scal))):
        for i, p in enumerate(order):
            at = lax.rem(chip + p, n_chip) * piece
            left[:, i * piece : (i + 1) * piece] = source[:, pl.ds(pl.multiple_of(at, piece), piece)]
        lanes = slice(a * width, (a + 1) * width)
        for i in range(0, n_chip, 2):
            total = tr_mm(left[:, i * piece : (i + 2) * piece], right[...]).astype(BF16)
            for h in range(2):
                low = total[h * piece : h * piece + half]
                high = total[h * piece + half : (h + 1) * piece]
                mine[order[i + h]][:, lanes] = jnp.where(first, low, high)
                other = jnp.where(first, high, low)
                if i == 0:
                    theirs[0][h * half : (h + 1) * half, lanes] = other
                else:
                    row = (i - 2 + h) * half
                    theirs[1][row : row + half, lanes] = other


def piece_kernel(hg_ref, up_ref, gate_ref, out_ref, packed):
    peers = out_ref.shape[0] // ROWS8
    width = up_ref.shape[0]
    chunks = width // LANE
    piece = mm_tr(hg_ref[...], up_ref[...]).astype(BF16)
    for c in range(CAP):
        for j in range(chunks):
            packed[j * peers : (j + 1) * peers, c * LANE : (c + 1) * LANE] = piece[
                c * peers : (c + 1) * peers, j * LANE : (j + 1) * LANE
            ]
    packed[: CAP * peers, CAP * LANE :] = gate_ref[...]
    packed[CAP * peers :, CAP * LANE :] = jnp.zeros((packed.shape[0] - CAP * peers, LANE), BF16)
    out_ref[...] = mm(by_peer(peers), packed[...]).astype(BF16)


def combine_kernel(in_ref, s_ref, gates_ref, grad_ref, gate_ref, pieces):
    peers = in_ref.shape[0] // ROWS8
    tokens = grad_ref.shape[0]
    width = pieces.shape[1]
    block = s_ref.shape[2]
    moved = mm(by_sublane(peers), in_ref[...]).astype(BF16)
    unpack(moved, pieces, peers, 0)
    picks = s_ref[0] + s_ref[1]
    total = tr_mm(picks, pieces[...]).astype(BF16)
    for j in range(SUB):
        grad_ref[:, j * width : (j + 1) * width] = total[j * tokens : (j + 1) * tokens, :]
    gates = moved[: CAP * peers, CAP * LANE :]
    rows = [tr_mm(gates, s_ref[k])[0:1] for k in range(TOP)]
    rows = jnp.concatenate(rows + [jnp.zeros((8 - TOP, block), F32)], axis=0).astype(BF16)
    rows = mm_tr(rows, natural_order(block))
    gate_ref[...] = (rows[:TOP] / gates_ref[...].astype(F32)).astype(BF16)


def call(kernel, out, ins, scratch, flops=0, moved=0):
    return pl.pallas_call(
        kernel,
        out_shape=out,
        in_specs=ins,
        out_specs=jax.tree.map(lambda _: VMEM, out),
        scratch_shapes=scratch,
        compiler_params=pltpu.CompilerParams(vmem_limit_bytes=40 << 20),
        cost_estimate=pl.CostEstimate(flops=flops, bytes_accessed=moved, transcendentals=0),
    )


def shape(*dims, dtype=BF16):
    return jax.ShapeDtypeStruct(dims, dtype)


def dispatch(layer_input, out_grad, ids, gates, peers, width):
    tokens = layer_input.shape[0]
    block = tokens * SUB
    rows = peers * CAP
    return call(
        dispatch_kernel,
        (shape(peers * ROWS8, 2 * CAP * LANE), shape(TOP, rows, block)),
        [VMEM] * 4,
        [
            pltpu.VMEM((block, width), BF16),
            pltpu.VMEM((2, rows, block), BF16),
            pltpu.VMEM((peers * ROWS8, 2 * CAP * LANE), BF16),
        ],
        flops=10**9,
        moved=4 << 20,
    )(layer_input, out_grad, ids, gates)


def expert(place, received, w_up, w_down, order):
    peers = received.shape[0] // ROWS8
    width = w_up.shape[0]
    rows = peers * CAP
    n_chip = len(order)
    half = width // n_chip // 2
    outs = (
        (shape(rows, width), shape(rows, LANE))
        + tuple(shape(half, 2 * width) for _ in order)
        + (shape(2 * half, 2 * width), shape((n_chip - 2) * half, 2 * width))
    )
    out = call(
        functools.partial(expert_kernel, order),
        outs,
        [SMEM, VMEM, VMEM, VMEM],
        [pltpu.VMEM((rows, width), BF16)] * 4,
        flops=4 * 10**9,
        moved=10 << 20,
    )(place, received, w_up, w_down)
    return out[0], out[1], out[2 : 2 + n_chip], out[2 + n_chip], out[3 + n_chip]


def give_back(hidden_grad, w_up, gate_part):
    rows, width = hidden_grad.shape
    peers = rows // CAP
    size = (peers * ROWS8, (CAP + 1) * LANE)
    return call(
        piece_kernel,
        shape(*size),
        [VMEM] * 3,
        [pltpu.VMEM(size, BF16)],
        flops=10**9,
        moved=4 << 20,
    )(hidden_grad, w_up, gate_part)


def combine(returned, picks, gates, tokens, width):
    return call(
        combine_kernel,
        (shape(tokens, SUB * width), shape(TOP, tokens * SUB)),
        [VMEM] * 3,
        [pltpu.VMEM((picks.shape[1], width), BF16)],
        flops=10**9,
        moved=2 << 20,
    )(returned, picks, gates)


def added(*terms):
    total = terms[0].astype(F32)
    for term in terms[1:]:
        total = total + term.astype(F32)
    return total


def body(n_dp, layer_input, out_grad, expert_ids, gates, up_weight, down_weight):
    tokens = layer_input.shape[0]
    width = up_weight.shape[1]
    peers = lax.axis_size("expert")
    n_chip = n_dp // 2
    at = lax.axis_index("dp")
    place = jnp.stack([at // 2, at % 2]).astype(jnp.int32)
    gates_t = gates.T
    w_up, w_down = up_weight[0], down_weight[0]

    def exchange(array):
        moved = lax.all_to_all(
            array.reshape(peers, ROWS8, -1), "expert", split_axis=0, concat_axis=0, tiled=True
        )
        return moved.reshape(array.shape)

    def hop(array, step):
        return lax.ppermute(array, "dp", [(i, (i + 2 * step) % n_dp) for i in range(n_dp)])

    def swap(array):
        return lax.ppermute(array, "dp", [(i, i ^ 1) for i in range(n_dp)])

    sent, picks = dispatch(layer_input, out_grad, expert_ids.T, gates_t, peers, width)
    received = exchange(sent)
    half_way = n_chip // 2
    order = [half_way]
    for step in range(half_way - 1, 0, -1):
        order += [n_chip - step, step]
    order.append(0)
    hidden_grad, gate_part, mine, theirs_first, theirs = expert(
        place, received, w_up, w_down, order
    )
    returned = exchange(give_back(hidden_grad, w_up, gate_part))
    got_first, got = swap(theirs_first), swap(theirs)
    half = theirs_first.shape[0] // 2

    def own(offset):
        i = order.index(offset)
        if i < 2:
            return [mine[i_of[offset]], got_first[i * half : (i + 1) * half]]
        return [mine[i_of[offset]], got[(i - 2) * half : (i - 1) * half]]

    i_of = {p: p for p in order}
    up, down = None, None
    for step in range(half_way, 0, -1):
        terms = own(step) + ([] if up is None else [up])
        up = hop(added(*terms).astype(BF16), 1)
        if step > 1:
            terms = own(n_chip - step + 1) + ([] if down is None else [down])
            down = hop(added(*terms).astype(BF16), -1)
    total = added(*own(0), up, down)
    input_grad, gate_grad = combine(returned, picks, gates_t, tokens, width)
    return (input_grad, gate_grad.T, total[None, :, :width], total[None, :, width:])


def solution(mesh):
    placed = (
        P(("dp", "expert"), None),
        P(("dp", "expert"), None),
        P(("dp", "expert"), None),
        P(("dp", "expert"), None),
        P("expert", None, None),
        P("expert", None, None),
    )
    return jax.shard_map(
        functools.partial(body, mesh.shape["dp"]),
        mesh=mesh,
        in_specs=placed,
        out_specs=(
            P(("dp", "expert"), None),
            P(("dp", "expert"), None),
            P("expert", "dp", None),
            P("expert", "dp", None),
        ),
        check_vma=False,
    )
```

time: 267 us -> 144 us (0.54)
  the two profiles are of different devices: /device:TPU:1 before, /device:TPU:52 now
where the time goes in v1:
time: 144 us; the launch traced here: 143 us
  starting transfers between devices  61 us (42%)
  waiting for transfers between devices  58.2 us (40%)
  Pallas kernels  12.1 us (8%)
  local copies, waits for them, and re-layouts  7.25 us (5%)
  other arithmetic  3.78 us (3%)
    all_to_all x2, waiting for transfers between devices, exchange(): lax.all_to_all(array.reshape(peers, ROWS8, -1), 'expert', split_axis=0, c...  45 us
    all_to_all x2, starting transfers between devices, exchange(): lax.all_to_all(array.reshape(peers, ROWS8, -1), 'expert', split_axis=0, c...  29.6 us
    ppermute x7, starting transfers between devices, hop(): lax.ppermute(array, 'dp', [(i, (i + 2 * step) % n_dp) for i in range(n_dp)])  27 us
    ppermute x7, waiting for transfers between devices, hop(): lax.ppermute(array, 'dp', [(i, (i + 2 * step) % n_dp) for i in range(n_dp)])  11.4 us
    unnamed x18, local copies, waits for them, and re-layouts  6.42 us
    pallas_call x1, Pallas kernels, expert(): call(functools.partial(expert_kernel, order), outs, [SMEM, VMEM, VMEM, VM...  5.59 us
    ppermute x2, starting transfers between devices, swap(): return lax.ppermute(array, 'dp', [(i, i ^ 1) for i in range(n_dp)])  4.33 us
  transfers between devices with their start and end apart: 11, of which 6 were waited for; matrix products, arithmetic and copies ran while one was open for 2% of the time, Pallas kernels for 3%

profile of v1, /device:TPU:52, one launch (start us, length us, event | category | flops | bytes accessed | tf_op | source)
XLA Modules:
  0.0 143.2 jit_solution(6286694212969475364)
XLA Ops:
  3.9 2.6 %shard_map.93 = (bf16[512,1280]{1,0:T(8,128)(2,1)}, bf16[2,320,128]{2,1,0:T(8,128)(2,1)S(1)}) custom-call(bf16[32,4096]{1,0:T(8,128)(2,1)S(1)} %copy-done.3, bf16[32,4096]{1,0:T(8,128)(2,1)S(1)} %copy-done.4, s32[2,128]{1,0:T(2,128)S(1)} %bitcast.20, bf16[2,128]{1,0:T(2,128)(2,1)S(1)} %bitcast.21), custom_call_target="tpu_custom_call" | custom-call | flops 1000000000 | bytes 4194304 | tf_op jit(solution)/shard_map/pallas_call | solution.py:198
  6.4 22.7 %all-to-all-start = ((bf16[64,8,1280]{2,1,0:T(8,128)(2,1)}), bf16[64,8,1280]{2,1,0:T(8,128)(2,1)S(1)}, u32[]{:S(2)}, u32[]{:S(2)}) async-start(bf16[64,8,1280]{2,1,0:T(8,128)(2,1)} %bitcast.4), calls=%async_computation | async-start | bytes 2621440 | tf_op jit(solution)/shard_map/all_to_all | solution.py:277
  29.2 35.6 %all-to-all-done = bf16[64,8,1280]{2,1,0:T(8,128)(2,1)S(1)} async-done(((bf16[64,8,1280]{2,1,0:T(8,128)(2,1)}), bf16[64,8,1280]{2,1,0:T(8,128)(2,1)S(1)}, u32[]{:S(2)}, u32[]{:S(2)}) %all-to-all-start) | async-done | bytes 1310752 | tf_op jit(solution)/shard_map/all_to_all | solution.py:277
  64.8 1.6 %copy-done = bf16[1,1024,1024]{2,1,0:T(8,128)(2,1)S(1)} copy-done((bf16[1,1024,1024]{2,1,0:T(8,128)(2,1)S(1)}, bf16[1,1024,1024]{2,1,0:T(8,128)(2,1)}, u32[]{:S(2)}) %copy-start) | copy-done | bytes 2097176
  66.4 1.6 %copy-done.1 = bf16[1,1024,1024]{2,1,0:T(8,128)(2,1)S(1)} copy-done((bf16[1,1024,1024]{2,1,0:T(8,128)(2,1)S(1)}, bf16[1,1024,1024]{2,1,0:T(8,128)(2,1)}, u32[]{:S(2)}) %copy-start.1) | copy-done | bytes 2097176
  68.0 5.6 %shard_map.94 = (bf16[320,1024]{1,0:T(8,128)(2,1)S(1)}, bf16[320,128]{1,0:T(8,128)(2,1)S(1)}, bf16[64,2048]{1,0:T(8,128)(2,1)S(1)}, bf16[64,2048]{1,0:T(8,128)(2...) custom-call(s32[2]{0:T(128)S(1)} %pad_add_fusion.place_ref, ...), custom_call_target="tpu_custom_call" | custom-call | flops 4000000000 | bytes 10485760 | tf_op jit(solution)/shard_map/pallas_call | solution.py:223
  73.6 1.9 %collective-permute-start = (bf16[384,2048]{1,0:T(8,128)(2,1)S(1)}, bf16[384,2048]{1,0:T(8,128)(2,1)S(1)}, u32[]{:S(2)}, u32[]{:S(2)}) collective-permute-start(bf16[384,2048]{1,0:T(8,128)(2,1)S(1)} %get-tuple-element.27), channel_id=1, source_target_pairs={{0,64},{64,0},{128,192},{192,128},{256,320},{320,256},{384,448},{4... | collective-permute-start | bytes 4718600 | tf_op jit(solution)/shard_map/ppermute | solution.py:286
  75.5 2.4 %collective-permute-start.1 = (bf16[128,2048]{1,0:T(8,128)(2,1)S(1)}, bf16[128,2048]{1,0:T(8,128)(2,1)S(1)}, u32[]{:S(2)}, u32[]{:S(2)}) collective-permute-start(bf16[128,2048]{1,0:T(8,128)(2,1)S(1)} %get-tuple-element.32), channel_id=1, source_target_pairs={{0,64},{64,0},{128,192},{192,128},{256,320},{320,256},{384,448},{4... | collective-permute-start | bytes 1572872 | tf_op jit(solution)/shard_map/ppermute | solution.py:286
  78.0 1.7 %collective-permute-done.1 = bf16[128,2048]{1,0:T(8,128)(2,1)S(1)} collective-permute-done((bf16[128,2048]{1,0:T(8,128)(2,1)S(1)}, bf16[128,2048]{1,0:T(8,128)(2,1)S(1)}, u32[]{:S(2)}, u32[]{:S(2)}) %collective-permute-start.1) | collective-permute-done | bytes 524320 | tf_op jit(solution)/shard_map/ppermute | solution.py:286
  79.8 4.9 %collective-permute-start.2 = (bf16[64,2048]{1,0:T(8,128)(2,1)S(1)}, bf16[64,2048]{1,0:T(8,128)(2,1)S(1)}, u32[]{:S(2)}, u32[]{:S(2)}) collective-permute-start(bf16[64,2048]{1,0:T(8,128)(2,1)S(1)} %get-tuple-element.40), channel_id=1, source_target_pairs={{0,128},{64,192},{128,256},{192,320},{256,384},{320,448},{384,512}... | collective-permute-start | bytes 786440 | tf_op jit(solution)/shard_map/ppermute | solution.py:283
  84.8 5.9 %collective-permute-done.2 = bf16[64,2048]{1,0:T(8,128)(2,1)S(1)} collective-permute-done((bf16[64,2048]{1,0:T(8,128)(2,1)S(1)}, bf16[64,2048]{1,0:T(8,128)(2,1)S(1)}, u32[]{:S(2)}, u32[]{:S(2)}) %collective-permute-start.2) | collective-permute-done | bytes 262176 | tf_op jit(solution)/shard_map/ppermute | solution.py:283
  90.7 5.6 %collective-permute-start.3 = (bf16[64,2048]{1,0:T(8,128)(2,1)S(1)}, bf16[64,2048]{1,0:T(8,128)(2,1)S(1)}, u32[]{:S(2)}, u32[]{:S(2)}) collective-permute-start(bf16[64,2048]{1,0:T(8,128)(2,1)S(1)} %add_convert_fusion.5), channel_id=1, source_target_pairs={{0,128},{64,192},{128,256},{192,320},{256,384},{320,448},{384,512}... | collective-permute-start | bytes 786440 | tf_op jit(solution)/shard_map/ppermute | solution.py:283
  96.4 1.9 %collective-permute-start.6 = (bf16[64,2048]{1,0:T(8,128)(2,1)S(1)}, bf16[64,2048]{1,0:T(8,128)(2,1)S(1)}, u32[]{:S(2)}, u32[]{:S(2)}) collective-permute-start(bf16[64,2048]{1,0:T(8,128)(2,1)S(1)} %get-tuple-element.41), channel_id=1, source_target_pairs={{0,896},{64,960},{128,0},{192,64},{256,128},{320,192},{384,256},{4... | collective-permute-start | bytes 786440 | tf_op jit(solution)/shard_map/ppermute | solution.py:283
  98.3 3.1 %collective-permute-done.3 = bf16[64,2048]{1,0:T(8,128)(2,1)S(1)} collective-permute-done((bf16[64,2048]{1,0:T(8,128)(2,1)S(1)}, bf16[64,2048]{1,0:T(8,128)(2,1)S(1)}, u32[]{:S(2)}, u32[]{:S(2)}) %collective-permute-start.3) | collective-permute-done | bytes 262176 | tf_op jit(solution)/shard_map/ppermute | solution.py:283
  101.5 5.6 %collective-permute-start.4 = (bf16[64,2048]{1,0:T(8,128)(2,1)S(1)}, bf16[64,2048]{1,0:T(8,128)(2,1)S(1)}, u32[]{:S(2)}, u32[]{:S(2)}) collective-permute-start(bf16[64,2048]{1,0:T(8,128)(2,1)S(1)} %add_convert_fusion.4), channel_id=1, source_target_pairs={{0,128},{64,192},{128,256},{192,320},{256,384},{320,448},{384,512}... | collective-permute-start | bytes 786440 | tf_op jit(solution)/shard_map/ppermute | solution.py:283
  107.1 2.3 %shard_map.95 = bf16[512,768]{1,0:T(8,128)(2,1)} custom-call(bf16[320,1024]{1,0:T(8,128)(2,1)S(1)} %get-tuple-element.21.hg_ref, bf16[1024,1024]{1,0:T(8,128)(2,1)S(1)} %bitcast.19, bf16[320,128]{1,0:T(8,128)(2,1)S(1)} %get-tuple-element.22.gate_ref), custom_call_target="tpu_custom_call" | custom-call | flops 1000000000 | bytes 4194304 | tf_op jit(solution)/shard_map/pallas_call | solution.py:238
  109.4 7.0 %all-to-all-start.1 = ((bf16[64,8,768]{2,1,0:T(8,128)(2,1)}), bf16[64,8,768]{2,1,0:T(8,128)(2,1)S(1)}, u32[]{:S(2)}, u32[]{:S(2)}) async-start(bf16[64,8,768]{2,1,0:T(8,128)(2,1)} %bitcast.8), calls=%async_computation.1 | async-start | bytes 1572864 | tf_op jit(solution)/shard_map/all_to_all | solution.py:277
  116.4 1.3 add_convert_fusion.3
  117.7 1.9 %collective-permute-start.7 = (bf16[64,2048]{1,0:T(8,128)(2,1)S(1)}, bf16[64,2048]{1,0:T(8,128)(2,1)S(1)}, u32[]{:S(2)}, u32[]{:S(2)}) collective-permute-start(bf16[64,2048]{1,0:T(8,128)(2,1)S(1)} %get-tuple-element.37), channel_id=1, source_target_pairs={{0,896},{64,960},{128,0},{192,64},{256,128},{320,192},{384,256},{4... | collective-permute-start | bytes 786440 | tf_op jit(solution)/shard_map/ppermute | solution.py:283
  119.6 5.1 %collective-permute-start.5 = (bf16[64,2048]{1,0:T(8,128)(2,1)S(1)}, bf16[64,2048]{1,0:T(8,128)(2,1)S(1)}, u32[]{:S(2)}, u32[]{:S(2)}) collective-permute-start(bf16[64,2048]{1,0:T(8,128)(2,1)S(1)} %get-tuple-element.36), channel_id=1, source_target_pairs={{0,128},{64,192},{128,256},{192,320},{256,384},{320,448},{384,512}... | collective-permute-start | bytes 786440 | tf_op jit(solution)/shard_map/ppermute | solution.py:283
  124.8 2.4 %collective-permute-done.7 = bf16[64,2048]{1,0:T(8,128)(2,1)S(1)} collective-permute-done((bf16[64,2048]{1,0:T(8,128)(2,1)S(1)}, bf16[64,2048]{1,0:T(8,128)(2,1)S(1)}, u32[]{:S(2)}, u32[]{:S(2)}) %collective-permute-start.7) | collective-permute-done | bytes 262176 | tf_op jit(solution)/shard_map/ppermute | solution.py:283
  128.2 1.9 %collective-permute-start.8 = (bf16[64,2048]{1,0:T(8,128)(2,1)S(1)}, bf16[64,2048]{1,0:T(8,128)(2,1)S(1)}, u32[]{:S(2)}, u32[]{:S(2)}) collective-permute-start(bf16[64,2048]{1,0:T(8,128)(2,1)S(1)} %add_convert_fusion), channel_id=1, source_target_pairs={{0,896},{64,960},{128,0},{192,64},{256,128},{320,192},{384,256},{4... | collective-permute-start | bytes 786440 | tf_op jit(solution)/shard_map/ppermute | solution.py:283
  130.2 9.4 %all-to-all-done.1 = bf16[64,8,768]{2,1,0:T(8,128)(2,1)S(1)} async-done(((bf16[64,8,768]{2,1,0:T(8,128)(2,1)}), bf16[64,8,768]{2,1,0:T(8,128)(2,1)S(1)}, u32[]{:S(2)}, u32[]{:S(2)}) %all-to-all-start.1) | async-done | bytes 786464 | tf_op jit(solution)/shard_map/all_to_all | solution.py:277
  139.6 1.7 %shard_map.96 = (bf16[32,4096]{1,0:T(8,128)(2,1)}, bf16[2,128]{1,0:T(2,128)(2,1)}) custom-call(bf16[512,768]{1,0:T(8,128)(2,1)S(1)} %bitcast.16, bf16[2,320,128]{2,1,0:T(8,128)(2,1)S(1)} %get-tuple-element.23.s_ref, bf16[2,128]{1,0:T(2,128)(2,1)S(1)} %bitcast.22), custom_call_target="tpu_custom_call" | custom-call | flops 1000000000 | bytes 2097152 | tf_op jit(solution)/shard_map/pallas_call | solution.py:249
  (28 shorter events, 6.6 us)
Async XLA Ops:
  0.6 1.0 copy-start.3
  1.6 0.9 copy-start.4
  2.5 0.7 copy-start.5
  3.2 0.7 copy-start.6
  6.4 58.4 %all-to-all-start = ((bf16[64,8,1280]{2,1,0:T(8,128)(2,1)}), bf16[64,8,1280]{2,1,0:T(8,128)(2,1)S(1)}, u32[]{:S(2)}, u32[]{:S(2)}) async-start(bf16[64,8,1280]{2,1,0:T(8,128)(2,1)} %bitcast.4), calls=%async_computation | async-start | bytes 2621440 | tf_op jit(solution)/shard_map/all_to_all | solution.py:277
  64.8 1.6 %copy-start = (bf16[1,1024,1024]{2,1,0:T(8,128)(2,1)S(1)}, bf16[1,1024,1024]{2,1,0:T(8,128)(2,1)}, u32[]{:S(2)}) copy-start(bf16[1,1024,1024]{2,1,0:T(8,128)(2,1)} %param.11) | copy-start | bytes 6291460
  66.4 1.6 %copy-start.1 = (bf16[1,1024,1024]{2,1,0:T(8,128)(2,1)S(1)}, bf16[1,1024,1024]{2,1,0:T(8,128)(2,1)}, u32[]{:S(2)}) copy-start(bf16[1,1024,1024]{2,1,0:T(8,128)(2,1)} %param.10) | copy-start | bytes 6291460
  73.6 17.0 %collective-permute-start = (bf16[384,2048]{1,0:T(8,128)(2,1)S(1)}, bf16[384,2048]{1,0:T(8,128)(2,1)S(1)}, u32[]{:S(2)}, u32[]{:S(2)}) collective-permute-start(bf16[384,2048]{1,0:T(8,128)(2,1)S(1)} %get-tuple-element.27), channel_id=1, source_target_pairs={{0,64},{64,0},{128,192},{192,128},{256,320},{320,256},{384,448},{4... | collective-permute-start | bytes 4718600 | tf_op jit(solution)/shard_map/ppermute | solution.py:286
  75.5 4.1 %collective-permute-start.1 = (bf16[128,2048]{1,0:T(8,128)(2,1)S(1)}, bf16[128,2048]{1,0:T(8,128)(2,1)S(1)}, u32[]{:S(2)}, u32[]{:S(2)}) collective-permute-start(bf16[128,2048]{1,0:T(8,128)(2,1)S(1)} %get-tuple-element.32), channel_id=1, source_target_pairs={{0,64},{64,0},{128,192},{192,128},{256,320},{320,256},{384,448},{4... | collective-permute-start | bytes 1572872 | tf_op jit(solution)/shard_map/ppermute | solution.py:286
  79.7 27.5 %copy-start.2 = (bf16[1,1024,1024]{2,1,0:T(8,128)(2,1)S(1)}, bf16[1,1024,1024]{2,1,0:T(8,128)(2,1)}, u32[]{:S(2)}) copy-start(bf16[1,1024,1024]{2,1,0:T(8,128)(2,1)} %param.10) | copy-start | bytes 6291460
  79.8 10.8 %collective-permute-start.2 = (bf16[64,2048]{1,0:T(8,128)(2,1)S(1)}, bf16[64,2048]{1,0:T(8,128)(2,1)S(1)}, u32[]{:S(2)}, u32[]{:S(2)}) collective-permute-start(bf16[64,2048]{1,0:T(8,128)(2,1)S(1)} %get-tuple-element.40), channel_id=1, source_target_pairs={{0,128},{64,192},{128,256},{192,320},{256,384},{320,448},{384,512}... | collective-permute-start | bytes 786440 | tf_op jit(solution)/shard_map/ppermute | solution.py:283
  90.6 18.8 %copy-start.8 = (bf16[384,2048]{1,0:T(8,128)(2,1)}, bf16[384,2048]{1,0:T(8,128)(2,1)S(1)}, u32[]{:S(2)}) copy-start(bf16[384,2048]{1,0:T(8,128)(2,1)S(1)} %collective-permute-done) | copy-start | bytes 4718596
  90.7 10.7 %collective-permute-start.3 = (bf16[64,2048]{1,0:T(8,128)(2,1)S(1)}, bf16[64,2048]{1,0:T(8,128)(2,1)S(1)}, u32[]{:S(2)}, u32[]{:S(2)}) collective-permute-start(bf16[64,2048]{1,0:T(8,128)(2,1)S(1)} %add_convert_fusion.5), channel_id=1, source_target_pairs={{0,128},{64,192},{128,256},{192,320},{256,384},{320,448},{384,512}... | collective-permute-start | bytes 786440 | tf_op jit(solution)/shard_map/ppermute | solution.py:283
  96.4 20.1 %collective-permute-start.6 = (bf16[64,2048]{1,0:T(8,128)(2,1)S(1)}, bf16[64,2048]{1,0:T(8,128)(2,1)S(1)}, u32[]{:S(2)}, u32[]{:S(2)}) collective-permute-start(bf16[64,2048]{1,0:T(8,128)(2,1)S(1)} %get-tuple-element.41), channel_id=1, source_target_pairs={{0,896},{64,960},{128,0},{192,64},{256,128},{320,192},{384,256},{4... | collective-permute-start | bytes 786440 | tf_op jit(solution)/shard_map/ppermute | solution.py:283
  101.5 14.9 %collective-permute-start.4 = (bf16[64,2048]{1,0:T(8,128)(2,1)S(1)}, bf16[64,2048]{1,0:T(8,128)(2,1)S(1)}, u32[]{:S(2)}, u32[]{:S(2)}) collective-permute-start(bf16[64,2048]{1,0:T(8,128)(2,1)S(1)} %add_convert_fusion.4), channel_id=1, source_target_pairs={{0,128},{64,192},{128,256},{192,320},{256,384},{320,448},{384,512}... | collective-permute-start | bytes 786440 | tf_op jit(solution)/shard_map/ppermute | solution.py:283
  109.4 30.2 %all-to-all-start.1 = ((bf16[64,8,768]{2,1,0:T(8,128)(2,1)}), bf16[64,8,768]{2,1,0:T(8,128)(2,1)S(1)}, u32[]{:S(2)}, u32[]{:S(2)}) async-start(bf16[64,8,768]{2,1,0:T(8,128)(2,1)} %bitcast.8), calls=%async_computation.1 | async-start | bytes 1572864 | tf_op jit(solution)/shard_map/all_to_all | solution.py:277
  116.4 23.1 %copy-start.7 = (bf16[128,2]{0,1:T(2,128)(2,1)S(1)}, bf16[128,2]{0,1:T(2,128)(2,1)}, u32[]{:S(2)}) copy-start(bf16[128,2]{0,1:T(2,128)(2,1)} %param.9) | copy-start | bytes 1540
  117.7 9.5 %collective-permute-start.7 = (bf16[64,2048]{1,0:T(8,128)(2,1)S(1)}, bf16[64,2048]{1,0:T(8,128)(2,1)S(1)}, u32[]{:S(2)}, u32[]{:S(2)}) collective-permute-start(bf16[64,2048]{1,0:T(8,128)(2,1)S(1)} %get-tuple-element.37), channel_id=1, source_target_pairs={{0,896},{64,960},{128,0},{192,64},{256,128},{320,192},{384,256},{4... | collective-permute-start | bytes 786440 | tf_op jit(solution)/shard_map/ppermute | solution.py:283
  119.6 21.6 %collective-permute-start.5 = (bf16[64,2048]{1,0:T(8,128)(2,1)S(1)}, bf16[64,2048]{1,0:T(8,128)(2,1)S(1)}, u32[]{:S(2)}, u32[]{:S(2)}) collective-permute-start(bf16[64,2048]{1,0:T(8,128)(2,1)S(1)} %get-tuple-element.36), channel_id=1, source_target_pairs={{0,128},{64,192},{128,256},{192,320},{256,384},{320,448},{384,512}... | collective-permute-start | bytes 786440 | tf_op jit(solution)/shard_map/ppermute | solution.py:283
  128.2 13.1 %collective-permute-start.8 = (bf16[64,2048]{1,0:T(8,128)(2,1)S(1)}, bf16[64,2048]{1,0:T(8,128)(2,1)S(1)}, u32[]{:S(2)}, u32[]{:S(2)}) collective-permute-start(bf16[64,2048]{1,0:T(8,128)(2,1)S(1)} %add_convert_fusion), channel_id=1, source_target_pairs={{0,896},{64,960},{128,0},{192,64},{256,128},{320,192},{384,256},{4... | collective-permute-start | bytes 786440 | tf_op jit(solution)/shard_map/ppermute | solution.py:283

commit v2 on v1

v2 whole, which is shorter than its diff:
```python
import functools

import jax
import jax.numpy as jnp
from jax import lax
from jax.experimental import pallas as pl
from jax.experimental.pallas import tpu as pltpu
from jax.sharding import PartitionSpec as P

TOP = 2
SUB = 4
CAP = 5
LANE = 128
ROWS8 = 8
N_CHIP = 8
F32 = jnp.float32
BF16 = jnp.bfloat16
VMEM = pl.BlockSpec(memory_space=pltpu.VMEM)
SMEM = pl.BlockSpec(memory_space=pltpu.SMEM)
HBM = pl.BlockSpec(memory_space=pltpu.HBM)
ANY = pl.BlockSpec(memory_space=pl.ANY)


def iota(shape, dim):
    return lax.broadcasted_iota(jnp.int32, shape, dim)


def one_hot(mask):
    return jnp.where(mask, 1.0, 0.0).astype(BF16)


def mm(left, right):
    return jnp.dot(left, right, preferred_element_type=F32)


def mm_tr(left, right):
    return lax.dot_general(left, right, (((1,), (1,)), ((), ())), preferred_element_type=F32)


def tr_mm(left, right):
    return lax.dot_general(left, right, (((0,), (0,)), ((), ())), preferred_element_type=F32)


def by_sublane(peers):
    size = peers * ROWS8
    row, col = iota((size, size), 0), iota((size, size), 1)
    return one_hot(col == lax.rem(row, peers) * ROWS8 + lax.div(row, peers))


def by_peer(peers):
    size = peers * ROWS8
    row, col = iota((size, size), 0), iota((size, size), 1)
    return one_hot(col == lax.rem(row, ROWS8) * peers + lax.div(row, ROWS8))


def natural_order(block):
    tokens = block // SUB
    row, col = iota((block, block), 0), iota((block, block), 1)
    return one_hot(row == lax.rem(col, tokens) * SUB + lax.div(col, tokens))


def dispatch_kernel(
    x_hbm, g_hbm, ids_hbm, gates_hbm, out_ref, s_ref,
    x_ref, g_ref, ids_ref, gates_ref, rows, picks, packed, sems,
):
    tokens = x_ref.shape[0]
    pairs = (
        (ids_hbm, ids_ref), (gates_hbm, gates_ref), (x_hbm, x_ref), (g_hbm, g_ref),
    )
    copies = [pltpu.make_async_copy(a, b, sems.at[i]) for i, (a, b) in enumerate(pairs)]
    for copy in copies:
        copy.start()
    copies[0].wait()
    copies[1].wait()
    block = ids_ref.shape[1]
    peers = out_ref.shape[0] // ROWS8
    width = rows.shape[1]
    chunks = width // LANE
    top = jnp.concatenate(
        [ids_ref[...].astype(F32), gates_ref[...].astype(F32), jnp.zeros((4, block), F32)], axis=0
    ).astype(BF16)
    top = mm(top, natural_order(block))
    expert = iota((peers, block), 0).astype(F32)
    hot = [expert == top[k : k + 1] for k in range(TOP)]
    chosen = one_hot(hot[0] | hot[1])
    earlier = one_hot(iota((block, block), 0) < iota((block, block), 1))
    before = mm(chosen, earlier)
    weight = jnp.where(hot[0], top[2:3], jnp.where(hot[1], top[3:4], 0.0))
    for c in range(CAP):
        slot = pl.ds(c * peers, peers)
        here = before == float(c)
        for k in range(TOP):
            s_ref[k, slot, :] = one_hot(hot[k] & here)
        picks[0, slot, :] = one_hot((hot[0] | hot[1]) & here)
        picks[1, slot, :] = jnp.where(here, weight, 0.0).astype(BF16)
    for a, ref in enumerate((x_ref, g_ref)):
        copies[2 + a].wait()
        for j in range(SUB):
            rows[j * tokens : (j + 1) * tokens, :] = ref[:, j * width : (j + 1) * width]
        sent = mm(picks[a], rows[...]).astype(BF16)
        for c in range(CAP):
            for j in range(chunks):
                packed[j * peers : (j + 1) * peers, (a * CAP + c) * LANE : (a * CAP + c + 1) * LANE] = (
                    sent[c * peers : (c + 1) * peers, j * LANE : (j + 1) * LANE]
                )
    out_ref[...] = mm(by_peer(peers), packed[...]).astype(BF16)


def unpack(source, target, peers, base):
    chunks = target.shape[1] // LANE
    for c in range(CAP):
        for j in range(chunks):
            target[c * peers : (c + 1) * peers, j * LANE : (j + 1) * LANE] = source[
                j * peers : (j + 1) * peers, (base + c) * LANE : (base + c + 1) * LANE
            ]


def expert_kernel(
    order, place_ref, in_hbm, up_hbm, down_hbm, back_ref, *rest
):
    (mine_first, mine, *swapped_out), rest = rest[:4], rest[4:]
    in_ref, feat, scal, hid, hg_ref, left_up, left_down, up_ref, down_ref, packed, back_v, *rest = rest
    held, other, other_later, sems = rest
    leaving = []

    def leave(source, target):
        leaving.append(pltpu.make_async_copy(source, target, sems.at[3 + len(leaving)]))
        leaving[-1].start()

    pairs = ((in_hbm, in_ref), (up_hbm, up_ref), (down_hbm, down_ref))
    copies = [pltpu.make_async_copy(a, b, sems.at[i]) for i, (a, b) in enumerate(pairs)]
    for copy in copies:
        copy.start()
    peers = in_ref.shape[0] // ROWS8
    width = up_ref.shape[0]
    to_sublane = by_sublane(peers)
    copies[0].wait()
    moved = mm(to_sublane, in_ref[...]).astype(BF16)
    unpack(moved, feat, peers, 0)
    unpack(moved, scal, peers, CAP)
    copies[1].wait()
    pre = mm(feat[...], up_ref[...])
    sig = jax.nn.sigmoid(pre)
    hidden = (pre * sig).astype(BF16)
    hid[...] = hidden
    copies[2].wait()
    back = mm_tr(scal[...], down_ref[...])
    part = jnp.sum(hidden.astype(F32) * back, axis=1, keepdims=True)
    hg_ref[...] = (back * (sig * (1.0 + pre * (1.0 - sig)))).astype(BF16)
    piece = mm_tr(hg_ref[...], up_ref[...]).astype(BF16)
    for c in range(CAP):
        for j in range(width // LANE):
            packed[j * peers : (j + 1) * peers, c * LANE : (c + 1) * LANE] = piece[
                c * peers : (c + 1) * peers, j * LANE : (j + 1) * LANE
            ]
    rows = CAP * peers
    packed[:rows, CAP * LANE :] = jnp.broadcast_to(part, (rows, LANE)).astype(BF16)
    packed[rows:, CAP * LANE :] = jnp.zeros((packed.shape[0] - rows, LANE), BF16)
    back_v[...] = mm(by_peer(peers), packed[...]).astype(BF16)
    leave(back_v, back_ref)
    first = place_ref[1] == 0
    piece = width // N_CHIP
    half = piece // 2
    for i, p in enumerate(order):
        at = pl.ds(pl.multiple_of(lax.rem(place_ref[0] + p, N_CHIP) * piece, piece), piece)
        left_up[:, i * piece : (i + 1) * piece] = feat[:, at]
        left_down[:, i * piece : (i + 1) * piece] = hid[:, at]
    for i in range(0, N_CHIP, 2):
        for a, (left, right) in enumerate(((left_up, hg_ref), (left_down, scal))):
            total = tr_mm(left[:, i * piece : (i + 2) * piece], right[...]).astype(BF16)
            lanes = slice(a * width, (a + 1) * width)
            for h in range(2):
                low = total[h * piece : h * piece + half]
                high = total[h * piece + half : (h + 1) * piece]
                held[(i + h) * half : (i + h + 1) * half, lanes] = jnp.where(first, low, high)
                swapped, row = (other, i) if i < N_CHIP // 2 else (other_later, i - N_CHIP // 2)
                row = (row + h) * half
                swapped[row : row + half, lanes] = jnp.where(first, high, low)
        if i == 0:
            leave(held.at[pl.ds(0, half)], mine_first)
            leave(held.at[pl.ds(half, half)], mine.at[pl.ds(0, half)])
        else:
            leave(held.at[pl.ds(i * half, 2 * half)], mine.at[pl.ds((i - 1) * half, 2 * half)])
        if i == N_CHIP // 2 - 2:
            leave(other, swapped_out[0])
    leave(other_later, swapped_out[1])
    for copy in leaving:
        copy.wait()


def fetch(refs, rows, held, sems):
    copies = [
        pltpu.make_async_copy(ref.at[pl.ds(row, held.shape[1])], held.at[i], sems.at[i])
        for i, (ref, row) in enumerate(zip(refs, rows))
    ]
    for copy in copies:
        copy.start()
    for copy in copies:
        copy.wait()


def step_kernel(rows, counts, *refs):
    n_in, n_out = len(rows), len(counts)
    outs, (held, sems) = refs[-2 - n_out : -2], refs[-2:]
    fetch(refs, rows, held, sems)
    at = 0
    for out, count in zip(outs, counts):
        total = held[at].astype(F32)
        for i in range(at + 1, at + count):
            total = total + held[i].astype(F32)
        out[...] = total.astype(BF16)
        at += count


def last_kernel(width, rows, *refs):
    ins, outs, (held, sems) = refs[: len(rows)], refs[len(rows) : -2], refs[-2:]
    fetch(ins, rows, held, sems)
    for a, out in enumerate(outs):
        total = held[0, :, a * width : (a + 1) * width].astype(F32)
        for i in range(1, len(rows)):
            total = total + held[i, :, a * width : (a + 1) * width].astype(F32)
        out[...] = total


def combine_kernel(in_ref, s_ref, gates_ref, grad_ref, gate_ref, pieces):
    peers = in_ref.shape[0] // ROWS8
    tokens = grad_ref.shape[0]
    width = pieces.shape[1]
    block = s_ref.shape[2]
    moved = mm(by_sublane(peers), in_ref[...]).astype(BF16)
    unpack(moved, pieces, peers, 0)
    picks = s_ref[0] + s_ref[1]
    total = tr_mm(picks, pieces[...]).astype(BF16)
    for j in range(SUB):
        grad_ref[:, j * width : (j + 1) * width] = total[j * tokens : (j + 1) * tokens, :]
    gates = moved[: CAP * peers, CAP * LANE :]
    rows = [tr_mm(gates, s_ref[k])[0:1] for k in range(TOP)]
    rows = jnp.concatenate(rows + [jnp.zeros((8 - TOP, block), F32)], axis=0).astype(BF16)
    rows = mm_tr(rows, natural_order(block))
    gate_ref[...] = (rows[:TOP] / gates_ref[...].astype(F32)).astype(BF16)


def call(kernel, out, ins, scratch, flops, moved, limit=16, place=VMEM):
    return pl.pallas_call(
        kernel,
        out_shape=out,
        in_specs=ins,
        out_specs=jax.tree.map(lambda _: place, out),
        scratch_shapes=scratch,
        compiler_params=pltpu.CompilerParams(vmem_limit_bytes=limit << 20),
        cost_estimate=pl.CostEstimate(flops=flops, bytes_accessed=moved, transcendentals=0),
    )


def shape(*dims, dtype=BF16):
    return jax.ShapeDtypeStruct(dims, dtype)


def dispatch(layer_input, out_grad, ids, gates, peers):
    tokens, depth = layer_input.shape
    block = tokens * SUB
    rows = peers * CAP
    width = depth // SUB
    size = (peers * ROWS8, 2 * CAP * LANE)
    return call(
        dispatch_kernel,
        (shape(*size), shape(TOP, rows, block)),
        [HBM] * 4,
        [
            pltpu.VMEM((tokens, depth), BF16),
            pltpu.VMEM((tokens, depth), BF16),
            pltpu.VMEM((TOP, block), jnp.int32),
            pltpu.VMEM((TOP, block), BF16),
            pltpu.VMEM((block, width), BF16),
            pltpu.VMEM((2, rows, block), BF16),
            pltpu.VMEM(size, BF16),
            pltpu.SemaphoreType.DMA((4,)),
        ],
        flops=10**9,
        moved=4 << 20,
        limit=60,
    )(layer_input, out_grad, ids, gates)


def expert(place, received, w_up, w_down, order):
    peers = received.shape[0] // ROWS8
    width = w_up.shape[0]
    rows = peers * CAP
    half = width // N_CHIP // 2
    back = (peers * ROWS8, (CAP + 1) * LANE)
    out = call(
        functools.partial(expert_kernel, order),
        (shape(*back), shape(half, 2 * width), shape(width // 2 - half, 2 * width)) + (shape(width // 4, 2 * width),) * 2,
        [SMEM, ANY, HBM, HBM],
        [pltpu.VMEM(received.shape, BF16)]
        + [pltpu.VMEM((rows, width), BF16)] * 6
        + [
            pltpu.VMEM(w_up.shape, BF16),
            pltpu.VMEM(w_down.shape, BF16),
            pltpu.VMEM(back, BF16),
            pltpu.VMEM(back, BF16),
            pltpu.VMEM((N_CHIP * half, 2 * width), BF16),
            pltpu.VMEM((width // 4, 2 * width), BF16),
            pltpu.VMEM((width // 4, 2 * width), BF16),
            pltpu.SemaphoreType.DMA((11,)),
        ],
        flops=3 * 10**9,
        moved=8 << 20,
        limit=52,
        place=ANY,
    )(place, received, w_up, w_down)
    return out


def ring_step(half, groups, after=()):
    arrays, rows = zip(*[term for group in groups for term in group])
    width = arrays[0].shape[1]
    return call(
        functools.partial(step_kernel, rows, [len(group) for group in groups]),
        (shape(half, width),) * len(groups),
        [ANY] * (len(arrays) + len(after)),
        [pltpu.VMEM((len(arrays), half, width), BF16), pltpu.SemaphoreType.DMA((len(arrays),))],
        flops=10**6,
        moved=1 << 20,
        limit=50,
    )(*arrays, *after)


def finish(half, terms):
    arrays, rows = zip(*terms)
    width = arrays[0].shape[1]
    return call(
        functools.partial(last_kernel, width // 2, rows),
        (shape(half, width // 2, dtype=F32),) * 2,
        [ANY] * len(arrays),
        [pltpu.VMEM((len(arrays), half, width), BF16), pltpu.SemaphoreType.DMA((len(arrays),))],
        flops=10**6,
        moved=1 << 20,
        limit=50,
    )(*arrays)


def combine(returned, picks, gates, tokens, width):
    return call(
        combine_kernel,
        (shape(tokens, SUB * width), shape(TOP, tokens * SUB)),
        [VMEM] * 3,
        [pltpu.VMEM((picks.shape[1], width), BF16)],
        flops=10**10,
        moved=2 << 20,
    )(returned, picks, gates)


def body(n_dp, layer_input, out_grad, expert_ids, gates, up_weight, down_weight):
    tokens = layer_input.shape[0]
    width = up_weight.shape[1]
    peers = lax.axis_size("expert")
    at = lax.axis_index("dp")
    place = jnp.stack([at // 2, at % 2]).astype(jnp.int32)
    gates_t = gates.T
    w_up, w_down = up_weight[0], down_weight[0]

    def exchange(array):
        moved = lax.all_to_all(
            array.reshape(peers, ROWS8, -1), "expert", split_axis=0, concat_axis=0, tiled=True
        )
        return moved.reshape(array.shape)

    def hop(array, step):
        return lax.ppermute(array, "dp", [(i, (i + 2 * step) % n_dp) for i in range(n_dp)])

    def swap(array):
        return lax.ppermute(array, "dp", [(i, i ^ 1) for i in range(n_dp)])

    sent, picks = dispatch(layer_input, out_grad, expert_ids.T, gates_t, peers)
    received = exchange(sent)
    order = [N_CHIP // 2]
    for far in range(N_CHIP // 2 - 1, 0, -1):
        order += [N_CHIP - far, far]
    order.append(0)
    early = N_CHIP // 2
    back, mine_first, mine, other, other_later = expert(place, received, w_up, w_down, order)
    half = mine_first.shape[0]
    got, got_later = swap(other), swap(other_later)
    returned = exchange(back)
    input_grad, gate_grad = combine(returned, picks, gates_t, tokens, width)

    def pair(offset):
        i = order.index(offset)
        own = (mine, (i - 1) * half) if i else (mine_first, 0)
        return [own, (got, i * half) if i < early else (got_later, (i - early) * half)]

    (up,) = ring_step(half, [pair(4)])
    up = hop(up, 1)
    up, down = ring_step(half, [pair(3) + [(up, 0)], pair(5)])
    up, down = hop(up, 1), hop(down, -1)
    up, down = ring_step(half, [pair(2) + [(up, 0)], pair(6) + [(down, 0)]])
    up, down = hop(up, 1), hop(down, -1)
    up, down = ring_step(half, [pair(1) + [(up, 0)], pair(7) + [(down, 0)]], [gate_grad])
    up, down = hop(up, 1), hop(down, -1)
    up_grad, down_grad = finish(half, pair(0) + [(up, 0), (down, 0)])
    return (input_grad, gate_grad.T, up_grad[None], down_grad[None])


def solution(mesh):
    placed = (
        P(("dp", "expert"), None),
        P(("dp", "expert"), None),
        P(("dp", "expert"), None),
        P(("dp", "expert"), None),
        P("expert", None, None),
        P("expert", None, None),
    )
    return jax.shard_map(
        functools.partial(body, mesh.shape["dp"]),
        mesh=mesh,
        in_specs=placed,
        out_specs=(
            P(("dp", "expert"), None),
            P(("dp", "expert"), None),
            P("expert", "dp", None),
            P("expert", "dp", None),
        ),
        check_vma=False,
    )
```

time: 144 us -> 143 us (level)
  the two profiles are of different devices: /device:TPU:52 before, /device:TPU:30 now
where the time goes in v2:
time: 143 us; the launch traced here: 142 us
  starting transfers between devices  59.6 us (42%)
  waiting for transfers between devices  58.5 us (41%)
  Pallas kernels  21.4 us (15%)
  local copies, waits for them, and re-layouts  1.76 us (1%)
    all_to_all x2, waiting for transfers between devices, exchange(): lax.all_to_all(array.reshape(peers, ROWS8, -1), 'expert', split_axis=0, c...  33.9 us
    all_to_all x2, starting transfers between devices, exchange(): lax.all_to_all(array.reshape(peers, ROWS8, -1), 'expert', split_axis=0, c...  31.7 us
    ppermute x7, waiting for transfers between devices, hop(): lax.ppermute(array, 'dp', [(i, (i + 2 * step) % n_dp) for i in range(n_dp)])  24.5 us
    ppermute x7, starting transfers between devices, hop(): lax.ppermute(array, 'dp', [(i, (i + 2 * step) % n_dp) for i in range(n_dp)])  23.9 us
    pallas_call x1, Pallas kernels, expert(): call(functools.partial(expert_kernel, order), (shape(*back), shape(half,...  10 us
    pallas_call x4, Pallas kernels, ring_step(): call(functools.partial(step_kernel, rows, [len(group) for group in groups...  4.02 us
    ppermute x2, starting transfers between devices, swap(): return lax.ppermute(array, 'dp', [(i, i ^ 1) for i in range(n_dp)])  3.97 us
    pallas_call x1, Pallas kernels, dispatch(): call(dispatch_kernel, (shape(*size), shape(TOP, rows, block)), [HBM] * 4,...  3.44 us
  transfers between devices with their start and end apart: 11, of which 7 were waited for; matrix products, arithmetic and copies ran while one was open for 0% of the time, Pallas kernels for 5%

profile of v2, /device:TPU:30, one launch (start us, length us, event | category | flops | bytes accessed | tf_op | source)
XLA Modules:
  0.0 142.2 jit_solution(8684776636526859653)
XLA Ops:
  0.6 3.4 %shard_map.93 = (bf16[512,1280]{1,0:T(8,128)(2,1)}, bf16[2,320,128]{2,1,0:T(8,128)(2,1)}) custom-call(bf16[32,4096]{1,0:T(8,128)(2,1)} %x_hbm.1, bf16[32,4096]{1,0:T(8,128)(2,1)} %g_hbm.1, s32[2,128]{1,0:T(2,128)} %bitcast.22, bf16[2,128]{1,0:T(2,128)(2,1)} %bitcast.14), custom_call_target="tpu_custom_call" | custom-call | flops 1000000000 | bytes 4194304 | tf_op jit(solution)/shard_map/pallas_call | solution.py:265
  4.1 22.8 %all-to-all-start = ((bf16[64,8,1280]{2,1,0:T(8,128)(2,1)}), bf16[64,8,1280]{2,1,0:T(8,128)(2,1)S(1)}, u32[]{:S(2)}, u32[]{:S(2)}) async-start(bf16[64,8,1280]{2,1,0:T(8,128)(2,1)} %bitcast.17), calls=%async_computation | async-start | bytes 2621440 | tf_op jit(solution)/shard_map/all_to_all | solution.py:364
  27.0 33.9 %all-to-all-done = bf16[64,8,1280]{2,1,0:T(8,128)(2,1)S(1)} async-done(((bf16[64,8,1280]{2,1,0:T(8,128)(2,1)}), bf16[64,8,1280]{2,1,0:T(8,128)(2,1)S(1)}, u32[]{:S(2)}, u32[]{:S(2)}) %all-to-all-start) | async-done | bytes 1310752 | tf_op jit(solution)/shard_map/all_to_all | solution.py:364
  60.9 1.1 copy-done.5
  62.0 10.0 %shard_map.94 = (bf16[512,768]{1,0:T(8,128)(2,1)}, bf16[64,2048]{1,0:T(8,128)(2,1)S(1)}, bf16[448,2048]{1,0:T(8,128)(2,1)}, bf16[256,2048]{1,0:T(8,128)(2,1)}, bf16[256,2048]{1,0:T(8,128)(2,1)}) custom-call(s32[2]{0:T(128)S(1)} %pad_add_fusion.place_ref, bf16[512,1280]{1,0:T(8,128)(2,1)} %bitcast.16, bf16[1024,1024]{1,0:T(8,128)(2,1)} %bitcast.18, ...), custom_call_target="tpu_custom_call" | custom-call | flops 3000000000 | bytes 8388608 | tf_op jit(solution)/shard_map/pallas_call | solution.py:291
  72.0 2.1 %collective-permute-start.1 = (bf16[256,2048]{1,0:T(8,128)(2,1)}, bf16[256,2048]{1,0:T(8,128)(2,1)}, u32[]{:S(2)}, u32[]{:S(2)}) collective-permute-start(bf16[256,2048]{1,0:T(8,128)(2,1)} %get-tuple-element.28), channel_id=1, source_target_pairs={{0,64},{64,0},{128,192},{192,128},{256,320},{320,256},{384,448},{4... | collective-permute-start | bytes 3145736 | tf_op jit(solution)/shard_map/ppermute | solution.py:373
  74.1 8.9 %all-to-all-start.1 = ((bf16[64,8,768]{2,1,0:T(8,128)(2,1)}), bf16[64,8,768]{2,1,0:T(8,128)(2,1)}, u32[]{:S(2)}, u32[]{:S(2)}) async-start(bf16[64,8,768]{2,1,0:T(8,128)(2,1)} %bitcast.8), calls=%async_computation.1 | async-start | bytes 1572864 | tf_op jit(solution)/shard_map/all_to_all | solution.py:364
  83.0 1.9 %collective-permute-start = (bf16[256,2048]{1,0:T(8,128)(2,1)}, bf16[256,2048]{1,0:T(8,128)(2,1)S(1)}, u32[]{:S(2)}, u32[]{:S(2)}) collective-permute-start(bf16[256,2048]{1,0:T(8,128)(2,1)} %get-tuple-element.27), channel_id=1, source_target_pairs={{0,64},{64,0},{128,192},{192,128},{256,320},{320,256},{384,448},{4... | collective-permute-start | bytes 3145736 | tf_op jit(solution)/shard_map/ppermute | solution.py:373
  86.0 3.6 %collective-permute-start.2 = (bf16[64,2048]{1,0:T(8,128)(2,1)S(1)}, bf16[64,2048]{1,0:T(8,128)(2,1)S(1)}, u32[]{:S(2)}, u32[]{:S(2)}) collective-permute-start(bf16[64,2048]{1,0:T(8,128)(2,1)S(1)} %shard_map.96), channel_id=1, source_target_pairs={{0,128},{64,192},{128,256},{192,320},{256,384},{320,448},{384,512}... | collective-permute-start | bytes 786440 | tf_op jit(solution)/shard_map/ppermute | solution.py:370
  89.6 7.0 %collective-permute-done.2.refs_2_ = bf16[64,2048]{1,0:T(8,128)(2,1)S(1)} collective-permute-done((bf16[64,2048]{1,0:T(8,128)(2,1)S(1)}, bf16[64,2048]{1,0:T(8,128)(2,1)S(1)}, u32[]{:S(2)}, u32[]{:S(2)}) %collective-permute-start.2) | collective-permute-done | bytes 262176 | tf_op jit(solution)/shard_map/ppermute | solution.py:370
  96.6 1.3 shard_map.97
  97.9 3.6 %collective-permute-start.3 = (bf16[64,2048]{1,0:T(8,128)(2,1)S(1)}, bf16[64,2048]{1,0:T(8,128)(2,1)S(1)}, u32[]{:S(2)}, u32[]{:S(2)}) collective-permute-start(bf16[64,2048]{1,0:T(8,128)(2,1)S(1)} %get-tuple-element.30), channel_id=1, source_target_pairs={{0,128},{64,192},{128,256},{192,320},{256,384},{320,448},{384,512}... | collective-permute-start | bytes 786440 | tf_op jit(solution)/shard_map/ppermute | solution.py:370
  101.5 3.2 %collective-permute-start.4 = (bf16[64,2048]{1,0:T(8,128)(2,1)S(1)}, bf16[64,2048]{1,0:T(8,128)(2,1)S(1)}, u32[]{:S(2)}, u32[]{:S(2)}) collective-permute-start(bf16[64,2048]{1,0:T(8,128)(2,1)S(1)} %get-tuple-element.31), channel_id=1, source_target_pairs={{0,896},{64,960},{128,0},{192,64},{256,128},{320,192},{384,256},{4... | collective-permute-start | bytes 786440 | tf_op jit(solution)/shard_map/ppermute | solution.py:370
  104.8 4.4 %collective-permute-done.3.refs_2_ = bf16[64,2048]{1,0:T(8,128)(2,1)S(1)} collective-permute-done((bf16[64,2048]{1,0:T(8,128)(2,1)S(1)}, bf16[64,2048]{1,0:T(8,128)(2,1)S(1)}, u32[]{:S(2)}, u32[]{:S(2)}) %collective-permute-start.3) | collective-permute-done | bytes 262176 | tf_op jit(solution)/shard_map/ppermute | solution.py:370
  109.2 2.4 %collective-permute-done.4.refs_5_ = bf16[64,2048]{1,0:T(8,128)(2,1)S(1)} collective-permute-done((bf16[64,2048]{1,0:T(8,128)(2,1)S(1)}, bf16[64,2048]{1,0:T(8,128)(2,1)S(1)}, u32[]{:S(2)}, u32[]{:S(2)}) %collective-permute-start.4) | collective-permute-done | bytes 262176 | tf_op jit(solution)/shard_map/ppermute | solution.py:370
  111.6 1.4 shard_map.98
  112.9 5.7 %collective-permute-start.5 = (bf16[64,2048]{1,0:T(8,128)(2,1)S(1)}, bf16[64,2048]{1,0:T(8,128)(2,1)S(1)}, u32[]{:S(2)}, u32[]{:S(2)}) collective-permute-start(bf16[64,2048]{1,0:T(8,128)(2,1)S(1)} %get-tuple-element.32), channel_id=1, source_target_pairs={{0,128},{64,192},{128,256},{192,320},{256,384},{320,448},{384,512}... | collective-permute-start | bytes 786440 | tf_op jit(solution)/shard_map/ppermute | solution.py:370
  118.6 1.9 %collective-permute-start.6 = (bf16[64,2048]{1,0:T(8,128)(2,1)S(1)}, bf16[64,2048]{1,0:T(8,128)(2,1)S(1)}, u32[]{:S(2)}, u32[]{:S(2)}) collective-permute-start(bf16[64,2048]{1,0:T(8,128)(2,1)S(1)} %get-tuple-element.33), channel_id=1, source_target_pairs={{0,896},{64,960},{128,0},{192,64},{256,128},{320,192},{384,256},{4... | collective-permute-start | bytes 786440 | tf_op jit(solution)/shard_map/ppermute | solution.py:370
  120.6 3.0 %shard_map.95 = (bf16[32,4096]{1,0:T(8,128)(2,1)}, bf16[2,128]{1,0:T(2,128)(2,1)}) custom-call(bf16[512,768]{1,0:T(8,128)(2,1)} %bitcast.9.in_ref, bf16[2,320,128]{2,1,0:T(8,128)(2,1)S(1)} %copy-done.4, bf16[2,128]{1,0:T(2,128)(2,1)S(1)} %bitcast.15), custom_call_target="tpu_custom_call" | custom-call | flops 10000000000 | bytes 2097152 | tf_op jit(solution)/shard_map/pallas_call | solution.py:344
  123.6 4.7 %collective-permute-done.6.refs_5_ = bf16[64,2048]{1,0:T(8,128)(2,1)S(1)} collective-permute-done((bf16[64,2048]{1,0:T(8,128)(2,1)S(1)}, bf16[64,2048]{1,0:T(8,128)(2,1)S(1)}, u32[]{:S(2)}, u32[]{:S(2)}) %collective-permute-start.6) | collective-permute-done | bytes 262176 | tf_op jit(solution)/shard_map/ppermute | solution.py:370
  129.3 3.6 %collective-permute-start.7 = (bf16[64,2048]{1,0:T(8,128)(2,1)S(1)}, bf16[64,2048]{1,0:T(8,128)(2,1)S(1)}, u32[]{:S(2)}, u32[]{:S(2)}) collective-permute-start(bf16[64,2048]{1,0:T(8,128)(2,1)S(1)} %get-tuple-element.34), channel_id=1, source_target_pairs={{0,128},{64,192},{128,256},{192,320},{256,384},{320,448},{384,512}... | collective-permute-start | bytes 786440 | tf_op jit(solution)/shard_map/ppermute | solution.py:370
  133.0 2.2 %collective-permute-start.8 = (bf16[64,2048]{1,0:T(8,128)(2,1)S(1)}, bf16[64,2048]{1,0:T(8,128)(2,1)S(1)}, u32[]{:S(2)}, u32[]{:S(2)}) collective-permute-start(bf16[64,2048]{1,0:T(8,128)(2,1)S(1)} %get-tuple-element.35), channel_id=1, source_target_pairs={{0,896},{64,960},{128,0},{192,64},{256,128},{320,192},{384,256},{4... | collective-permute-start | bytes 786440 | tf_op jit(solution)/shard_map/ppermute | solution.py:370
  135.2 2.4 %collective-permute-done.7.refs_2_ = bf16[64,2048]{1,0:T(8,128)(2,1)S(1)} collective-permute-done((bf16[64,2048]{1,0:T(8,128)(2,1)S(1)}, bf16[64,2048]{1,0:T(8,128)(2,1)S(1)}, u32[]{:S(2)}, u32[]{:S(2)}) %collective-permute-start.7) | collective-permute-done | bytes 262176 | tf_op jit(solution)/shard_map/ppermute | solution.py:370
  137.6 3.6 %collective-permute-done.8.refs_3_ = bf16[64,2048]{1,0:T(8,128)(2,1)S(1)} collective-permute-done((bf16[64,2048]{1,0:T(8,128)(2,1)S(1)}, bf16[64,2048]{1,0:T(8,128)(2,1)S(1)}, u32[]{:S(2)}, u32[]{:S(2)}) %collective-permute-start.8) | collective-permute-done | bytes 262176 | tf_op jit(solution)/shard_map/ppermute | solution.py:370
  (19 shorter events, 3.1 us)
Async XLA Ops:
  4.1 56.8 %all-to-all-start = ((bf16[64,8,1280]{2,1,0:T(8,128)(2,1)}), bf16[64,8,1280]{2,1,0:T(8,128)(2,1)S(1)}, u32[]{:S(2)}, u32[]{:S(2)}) async-start(bf16[64,8,1280]{2,1,0:T(8,128)(2,1)} %bitcast.17), calls=%async_computation | async-start | bytes 2621440 | tf_op jit(solution)/shard_map/all_to_all | solution.py:364
  60.9 1.1 copy-start.5
  72.0 24.6 %copy-start = (bf16[448,2048]{1,0:T(8,128)(2,1)S(1)}, bf16[448,2048]{1,0:T(8,128)(2,1)}, u32[]{:S(2)}) copy-start(bf16[448,2048]{1,0:T(8,128)(2,1)} %get-tuple-element.26.refs_0_.refs_3_) | copy-start | bytes 5505028
  72.0 12.9 %collective-permute-start.1 = (bf16[256,2048]{1,0:T(8,128)(2,1)}, bf16[256,2048]{1,0:T(8,128)(2,1)}, u32[]{:S(2)}, u32[]{:S(2)}) collective-permute-start(bf16[256,2048]{1,0:T(8,128)(2,1)} %get-tuple-element.28), channel_id=1, source_target_pairs={{0,64},{64,0},{128,192},{192,128},{256,320},{320,256},{384,448},{4... | collective-permute-start | bytes 3145736 | tf_op jit(solution)/shard_map/ppermute | solution.py:373
  74.1 46.5 %all-to-all-start.1 = ((bf16[64,8,768]{2,1,0:T(8,128)(2,1)}), bf16[64,8,768]{2,1,0:T(8,128)(2,1)}, u32[]{:S(2)}, u32[]{:S(2)}) async-start(bf16[64,8,768]{2,1,0:T(8,128)(2,1)} %bitcast.8), calls=%async_computation.1 | async-start | bytes 1572864 | tf_op jit(solution)/shard_map/all_to_all | solution.py:364
  83.0 21.7 %collective-permute-start = (bf16[256,2048]{1,0:T(8,128)(2,1)}, bf16[256,2048]{1,0:T(8,128)(2,1)S(1)}, u32[]{:S(2)}, u32[]{:S(2)}) collective-permute-start(bf16[256,2048]{1,0:T(8,128)(2,1)} %get-tuple-element.27), channel_id=1, source_target_pairs={{0,64},{64,0},{128,192},{192,128},{256,320},{320,256},{384,448},{4... | collective-permute-start | bytes 3145736 | tf_op jit(solution)/shard_map/ppermute | solution.py:373
  86.0 10.6 %collective-permute-start.2 = (bf16[64,2048]{1,0:T(8,128)(2,1)S(1)}, bf16[64,2048]{1,0:T(8,128)(2,1)S(1)}, u32[]{:S(2)}, u32[]{:S(2)}) collective-permute-start(bf16[64,2048]{1,0:T(8,128)(2,1)S(1)} %shard_map.96), channel_id=1, source_target_pairs={{0,128},{64,192},{128,256},{192,320},{256,384},{320,448},{384,512}... | collective-permute-start | bytes 786440 | tf_op jit(solution)/shard_map/ppermute | solution.py:370
  97.9 11.3 %collective-permute-start.3 = (bf16[64,2048]{1,0:T(8,128)(2,1)S(1)}, bf16[64,2048]{1,0:T(8,128)(2,1)S(1)}, u32[]{:S(2)}, u32[]{:S(2)}) collective-permute-start(bf16[64,2048]{1,0:T(8,128)(2,1)S(1)} %get-tuple-element.30), channel_id=1, source_target_pairs={{0,128},{64,192},{128,256},{192,320},{256,384},{320,448},{384,512}... | collective-permute-start | bytes 786440 | tf_op jit(solution)/shard_map/ppermute | solution.py:370
  101.5 19.1 %copy-start.3 = (bf16[128,2]{0,1:T(2,128)(2,1)S(1)}, bf16[128,2]{0,1:T(2,128)(2,1)}, u32[]{:S(2)}) copy-start(bf16[128,2]{0,1:T(2,128)(2,1)} %param.9) | copy-start | bytes 1540
  101.5 19.1 %copy-start.4 = (bf16[2,320,128]{2,1,0:T(8,128)(2,1)S(1)}, bf16[2,320,128]{2,1,0:T(8,128)(2,1)}, u32[]{:S(2)}) copy-start(bf16[2,320,128]{2,1,0:T(8,128)(2,1)} %get-tuple-element.23.s_ref) | copy-start | bytes 491524
  101.5 10.0 %collective-permute-start.4 = (bf16[64,2048]{1,0:T(8,128)(2,1)S(1)}, bf16[64,2048]{1,0:T(8,128)(2,1)S(1)}, u32[]{:S(2)}, u32[]{:S(2)}) collective-permute-start(bf16[64,2048]{1,0:T(8,128)(2,1)S(1)} %get-tuple-element.31), channel_id=1, source_target_pairs={{0,896},{64,960},{128,0},{192,64},{256,128},{320,192},{384,256},{4... | collective-permute-start | bytes 786440 | tf_op jit(solution)/shard_map/ppermute | solution.py:370
  112.9 10.7 %collective-permute-start.5 = (bf16[64,2048]{1,0:T(8,128)(2,1)S(1)}, bf16[64,2048]{1,0:T(8,128)(2,1)S(1)}, u32[]{:S(2)}, u32[]{:S(2)}) collective-permute-start(bf16[64,2048]{1,0:T(8,128)(2,1)S(1)} %get-tuple-element.32), channel_id=1, source_target_pairs={{0,128},{64,192},{128,256},{192,320},{256,384},{320,448},{384,512}... | collective-permute-start | bytes 786440 | tf_op jit(solution)/shard_map/ppermute | solution.py:370
  118.6 9.7 %collective-permute-start.6 = (bf16[64,2048]{1,0:T(8,128)(2,1)S(1)}, bf16[64,2048]{1,0:T(8,128)(2,1)S(1)}, u32[]{:S(2)}, u32[]{:S(2)}) collective-permute-start(bf16[64,2048]{1,0:T(8,128)(2,1)S(1)} %get-tuple-element.33), channel_id=1, source_target_pairs={{0,896},{64,960},{128,0},{192,64},{256,128},{320,192},{384,256},{4... | collective-permute-start | bytes 786440 | tf_op jit(solution)/shard_map/ppermute | solution.py:370
  120.6 7.7 %copy-start.1 = (bf16[448,2048]{1,0:T(8,128)(2,1)S(1)}, bf16[448,2048]{1,0:T(8,128)(2,1)}, u32[]{:S(2)}) copy-start(bf16[448,2048]{1,0:T(8,128)(2,1)} %get-tuple-element.26.refs_0_.refs_3_) | copy-start | bytes 5505028
  128.3 0.7 copy-start.2
  129.3 8.3 %collective-permute-start.7 = (bf16[64,2048]{1,0:T(8,128)(2,1)S(1)}, bf16[64,2048]{1,0:T(8,128)(2,1)S(1)}, u32[]{:S(2)}, u32[]{:S(2)}) collective-permute-start(bf16[64,2048]{1,0:T(8,128)(2,1)S(1)} %get-tuple-element.34), channel_id=1, source_target_pairs={{0,128},{64,192},{128,256},{192,320},{256,384},{320,448},{384,512}... | collective-permute-start | bytes 786440 | tf_op jit(solution)/shard_map/ppermute | solution.py:370
  133.0 8.3 %collective-permute-start.8 = (bf16[64,2048]{1,0:T(8,128)(2,1)S(1)}, bf16[64,2048]{1,0:T(8,128)(2,1)S(1)}, u32[]{:S(2)}, u32[]{:S(2)}) collective-permute-start(bf16[64,2048]{1,0:T(8,128)(2,1)S(1)} %get-tuple-element.35), channel_id=1, source_target_pairs={{0,896},{64,960},{128,0},{192,64},{256,128},{320,192},{384,256},{4... | collective-permute-start | bytes 786440 | tf_op jit(solution)/shard_map/ppermute | solution.py:370

commit v3 on v2

--- a/solution.py
+++ b/solution.py
@@ -115,18 +115,8 @@
             ]
 
 
-def expert_kernel(
-    order, place_ref, in_hbm, up_hbm, down_hbm, back_ref, *rest
-):
-    (mine_first, mine, *swapped_out), rest = rest[:4], rest[4:]
-    in_ref, feat, scal, hid, hg_ref, left_up, left_down, up_ref, down_ref, packed, back_v, *rest = rest
-    held, other, other_later, sems = rest
-    leaving = []
-
-    def leave(source, target):
-        leaving.append(pltpu.make_async_copy(source, target, sems.at[3 + len(leaving)]))
-        leaving[-1].start()
-
+def hidden_kernel(place_ref, in_hbm, up_hbm, down_hbm, *refs):
+    feat, scal, hid, hg_ref, part_ref, far_ref, in_ref, up_ref, down_ref, sems = refs
     pairs = ((in_hbm, in_ref), (up_hbm, up_ref), (down_hbm, down_ref))
     copies = [pltpu.make_async_copy(a, b, sems.at[i]) for i, (a, b) in enumerate(pairs)]
     for copy in copies:
@@ -146,44 +136,65 @@
     copies[2].wait()
     back = mm_tr(scal[...], down_ref[...])
     part = jnp.sum(hidden.astype(F32) * back, axis=1, keepdims=True)
+    part_ref[...] = jnp.broadcast_to(part, part_ref.shape).astype(BF16)
     hg_ref[...] = (back * (sig * (1.0 + pre * (1.0 - sig)))).astype(BF16)
-    piece = mm_tr(hg_ref[...], up_ref[...]).astype(BF16)
+    here = rows_of(place_ref, N_CHIP // 2, width)
+    far_ref[:, :width] = tr_mm(feat[:, here], hg_ref[...]).astype(BF16)
+    far_ref[:, width:] = tr_mm(hid[:, here], scal[...]).astype(BF16)
+
+
+def rows_of(place_ref, offset, width):
+    piece = width // N_CHIP
+    at = lax.rem(place_ref[0] + offset, N_CHIP) * piece
+    return pl.ds(pl.multiple_of(at, piece), piece)
+
+
+def blocks_kernel(place_ref, feat, scal, hid, hg_ref, part_ref, up_hbm, _, *refs):
+    back_ref, own_ref, other_ref, up_ref, packed, back_v, left, own, other, sems = refs
+    load = pltpu.make_async_copy(up_hbm, up_ref, sems.at[0])
+    load.start()
+    leaving = []
+
+    def leave(source, target):
+        leaving.append(pltpu.make_async_copy(source, target, sems.at[1 + len(leaving)]))
+        leaving[-1].start()
+
+    width = up_ref.shape[0]
+    piece = width // N_CHIP
+    half = piece // 2
+    first = place_ref[1] == 0
+    middle = N_CHIP // 2
+    for r in range(1, middle):
+        near = jnp.where(first, middle - r, middle + r)
+        rows = slice((r - 1) * piece, r * piece)
+        for a, (source, right) in enumerate(((feat, hg_ref), (hid, scal))):
+            left[:, :piece] = source[:, rows_of(place_ref, near, width)]
+            left[:, piece:] = source[:, rows_of(place_ref, N_CHIP - near, width)]
+            total = tr_mm(left[...], right[...]).astype(BF16)
+            lanes = slice(a * width, (a + 1) * width)
+            own[rows, lanes] = total[:piece]
+            other[rows, lanes] = total[piece:]
+    rows = slice((middle - 1) * piece, (middle - 1) * piece + half)
+    for a, (source, right) in enumerate(((feat, hg_ref), (hid, scal))):
+        total = tr_mm(source[:, rows_of(place_ref, 0, width)], right[...]).astype(BF16)
+        lanes = slice(a * width, (a + 1) * width)
+        own[rows, lanes] = jnp.where(first, total[:half], total[half:])
+        other[rows, lanes] = jnp.where(first, total[half:], total[:half])
+    leave(other, other_ref)
+    leave(own, own_ref)
+    load.wait()
+    peers = packed.shape[0] // ROWS8
+    sent = mm_tr(hg_ref[...], up_ref[...]).astype(BF16)
     for c in range(CAP):
         for j in range(width // LANE):
-            packed[j * peers : (j + 1) * peers, c * LANE : (c + 1) * LANE] = piece[
+            packed[j * peers : (j + 1) * peers, c * LANE : (c + 1) * LANE] = sent[
                 c * peers : (c + 1) * peers, j * LANE : (j + 1) * LANE
             ]
     rows = CAP * peers
-    packed[:rows, CAP * LANE :] = jnp.broadcast_to(part, (rows, LANE)).astype(BF16)
+    packed[:rows, CAP * LANE :] = part_ref[...]
     packed[rows:, CAP * LANE :] = jnp.zeros((packed.shape[0] - rows, LANE), BF16)
     back_v[...] = mm(by_peer(peers), packed[...]).astype(BF16)
     leave(back_v, back_ref)
-    first = place_ref[1] == 0
-    piece = width // N_CHIP
-    half = piece // 2
-    for i, p in enumerate(order):
-        at = pl.ds(pl.multiple_of(lax.rem(place_ref[0] + p, N_CHIP) * piece, piece), piece)
-        left_up[:, i * piece : (i + 1) * piece] = feat[:, at]
-        left_down[:, i * piece : (i + 1) * piece] = hid[:, at]
-    for i in range(0, N_CHIP, 2):
-        for a, (left, right) in enumerate(((left_up, hg_ref), (left_down, scal))):
-            total = tr_mm(left[:, i * piece : (i + 2) * piece], right[...]).astype(BF16)
-            lanes = slice(a * width, (a + 1) * width)
-            for h in range(2):
-                low = total[h * piece : h * piece + half]
-                high = total[h * piece + half : (h + 1) * piece]
-                held[(i + h) * half : (i + h + 1) * half, lanes] = jnp.where(first, low, high)
-                swapped, row = (other, i) if i < N_CHIP // 2 else (other_later, i - N_CHIP // 2)
-                row = (row + h) * half
-                swapped[row : row + half, lanes] = jnp.where(first, high, low)
-        if i == 0:
-            leave(held.at[pl.ds(0, half)], mine_first)
-            leave(held.at[pl.ds(half, half)], mine.at[pl.ds(0, half)])
-        else:
-            leave(held.at[pl.ds(i * half, 2 * half)], mine.at[pl.ds((i - 1) * half, 2 * half)])
-        if i == N_CHIP // 2 - 2:
-            leave(other, swapped_out[0])
-    leave(other_later, swapped_out[1])
     for copy in leaving:
         copy.wait()
 
@@ -199,21 +210,23 @@
         copy.wait()
 
 
-def step_kernel(rows, counts, *refs):
-    n_in, n_out = len(rows), len(counts)
-    outs, (held, sems) = refs[-2 - n_out : -2], refs[-2:]
-    fetch(refs, rows, held, sems)
-    at = 0
-    for out, count in zip(outs, counts):
-        total = held[at].astype(F32)
-        for i in range(at + 1, at + count):
-            total = total + held[i].astype(F32)
-        out[...] = total.astype(BF16)
-        at += count
+def step_kernel(rows, place_ref, *refs):
+    ins, outs, (held, sems) = refs[: len(rows)], refs[len(rows) : -2], refs[-2:]
+    fetch(ins, rows, held, sems)
+    total = held[0].astype(F32)
+    for i in range(1, len(rows)):
+        total = total + held[i].astype(F32)
+    total = total.astype(BF16)
+    if len(outs) == 1:
+        outs[0][...] = total
+    else:
+        first, half = place_ref[1] == 0, outs[0].shape[0]
+        outs[0][...] = jnp.where(first, total[:half], total[half:])
+        outs[1][...] = jnp.where(first, total[half:], total[:half])
 
 
 def last_kernel(width, rows, *refs):
-    ins, outs, (held, sems) = refs[: len(rows)], refs[len(rows) : -2], refs[-2:]
+    ins, outs, (held, sems) = refs[: len(rows)], refs[len(rows) + 1 : -2], refs[-2:]
     fetch(ins, rows, held, sems)
     for a, out in enumerate(outs):
         total = held[0, :, a * width : (a + 1) * width].astype(F32)
@@ -282,62 +295,78 @@
     )(layer_input, out_grad, ids, gates)
 
 
-def expert(place, received, w_up, w_down, order):
+def hidden_part(place, received, w_up, w_down):
     peers = received.shape[0] // ROWS8
     width = w_up.shape[0]
     rows = peers * CAP
-    half = width // N_CHIP // 2
-    back = (peers * ROWS8, (CAP + 1) * LANE)
-    out = call(
-        functools.partial(expert_kernel, order),
-        (shape(*back), shape(half, 2 * width), shape(width // 2 - half, 2 * width)) + (shape(width // 4, 2 * width),) * 2,
-        [SMEM, ANY, HBM, HBM],
-        [pltpu.VMEM(received.shape, BF16)]
-        + [pltpu.VMEM((rows, width), BF16)] * 6
-        + [
+    return call(
+        hidden_kernel,
+        (shape(rows, width),) * 4 + (shape(rows, LANE), shape(width // N_CHIP, 2 * width)),
+        [SMEM, VMEM, HBM, HBM],
+        [
+            pltpu.VMEM(received.shape, BF16),
             pltpu.VMEM(w_up.shape, BF16),
             pltpu.VMEM(w_down.shape, BF16),
-            pltpu.VMEM(back, BF16),
-            pltpu.VMEM(back, BF16),
-            pltpu.VMEM((N_CHIP * half, 2 * width), BF16),
-            pltpu.VMEM((width // 4, 2 * width), BF16),
-            pltpu.VMEM((width // 4, 2 * width), BF16),
-            pltpu.SemaphoreType.DMA((11,)),
+            pltpu.SemaphoreType.DMA((3,)),
         ],
         flops=3 * 10**9,
         moved=8 << 20,
+        limit=48,
+    )(place, received, w_up, w_down)
+
+
+def blocks(place, arrays, w_up, after):
+    rows, width = arrays[0].shape
+    peers = rows // CAP
+    back = (peers * ROWS8, (CAP + 1) * LANE)
+    kept = (width // 2 - width // N_CHIP // 2, 2 * width)
+    return call(
+        blocks_kernel,
+        (shape(*back), shape(*kept), shape(*kept)),
+        [SMEM] + [VMEM] * 5 + [HBM, ANY],
+        [
+            pltpu.VMEM(w_up.shape, BF16),
+            pltpu.VMEM(back, BF16),
+            pltpu.VMEM(back, BF16),
+            pltpu.VMEM((rows, 2 * width // N_CHIP), BF16),
+            pltpu.VMEM(kept, BF16),
+            pltpu.VMEM(kept, BF16),
+            pltpu.SemaphoreType.DMA((4,)),
+        ],
+        flops=4 * 10**9,
+        moved=8 << 20,
+        limit=50,
+        place=ANY,
+    )(place, *arrays, w_up, after)
+
+
+def ring_step(place, terms, parts):
+    arrays, starts = zip(*terms)
+    width = arrays[0].shape[1]
+    rows = width // 2 // N_CHIP
+    return call(
+        functools.partial(step_kernel, starts),
+        (shape(rows // parts, width),) * parts,
+        [SMEM] + [ANY] * len(arrays),
+        [pltpu.VMEM((len(arrays), rows, width), BF16), pltpu.SemaphoreType.DMA((len(arrays),))],
+        flops=10**6,
+        moved=1 << 20,
         limit=52,
-        place=ANY,
-    )(place, received, w_up, w_down)
-    return out
-
-
-def ring_step(half, groups, after=()):
-    arrays, rows = zip(*[term for group in groups for term in group])
+    )(place, *arrays)
+
+
+def finish(half, terms, after):
+    arrays, rows = zip(*terms)
     width = arrays[0].shape[1]
     return call(
-        functools.partial(step_kernel, rows, [len(group) for group in groups]),
-        (shape(half, width),) * len(groups),
-        [ANY] * (len(arrays) + len(after)),
+        functools.partial(last_kernel, width // 2, rows),
+        (shape(half, width // 2, dtype=F32),) * 2,
+        [ANY] * (len(arrays) + 1),
         [pltpu.VMEM((len(arrays), half, width), BF16), pltpu.SemaphoreType.DMA((len(arrays),))],
         flops=10**6,
         moved=1 << 20,
-        limit=50,
-    )(*arrays, *after)
-
-
-def finish(half, terms):
-    arrays, rows = zip(*terms)
-    width = arrays[0].shape[1]
-    return call(
-        functools.partial(last_kernel, width // 2, rows),
-        (shape(half, width // 2, dtype=F32),) * 2,
-        [ANY] * len(arrays),
-        [pltpu.VMEM((len(arrays), half, width), BF16), pltpu.SemaphoreType.DMA((len(arrays),))],
-        flops=10**6,
-        moved=1 << 20,
-        limit=50,
-    )(*arrays)
+        limit=52,
+    )(*arrays, after)
 
 
 def combine(returned, picks, gates, tokens, width):
@@ -366,39 +395,40 @@
         )
         return moved.reshape(array.shape)
 
-    def hop(array, step):
-        return lax.ppermute(array, "dp", [(i, (i + 2 * step) % n_dp) for i in range(n_dp)])
+    def along(array, first_only=False, cross=0):
+        pairs = []
+        for i in range(n_dp):
+            chip, core = i // 2, i % 2
+            if core == 0 or not first_only:
+                pairs.append((i, (chip + (1 - 2 * core)) % N_CHIP * 2 + (core ^ cross)))
+        return lax.ppermute(array, "dp", pairs)
 
     def swap(array):
         return lax.ppermute(array, "dp", [(i, i ^ 1) for i in range(n_dp)])
 
     sent, picks = dispatch(layer_input, out_grad, expert_ids.T, gates_t, peers)
     received = exchange(sent)
-    order = [N_CHIP // 2]
-    for far in range(N_CHIP // 2 - 1, 0, -1):
-        order += [N_CHIP - far, far]
-    order.append(0)
-    early = N_CHIP // 2
-    back, mine_first, mine, other, other_later = expert(place, received, w_up, w_down, order)
-    half = mine_first.shape[0]
-    got, got_later = swap(other), swap(other_later)
+    *arrays, far = hidden_part(place, received, w_up, w_down)
+    got_far = swap(far)
+    (total,) = ring_step(place, [(far, 0), (got_far, 0)], 1)
+    back, own, other = blocks(place, arrays, w_up, total)
+    got = swap(other)
     returned = exchange(back)
     input_grad, gate_grad = combine(returned, picks, gates_t, tokens, width)
-
-    def pair(offset):
-        i = order.index(offset)
-        own = (mine, (i - 1) * half) if i else (mine_first, 0)
-        return [own, (got, i * half) if i < early else (got_later, (i - early) * half)]
-
-    (up,) = ring_step(half, [pair(4)])
-    up = hop(up, 1)
-    up, down = ring_step(half, [pair(3) + [(up, 0)], pair(5)])
-    up, down = hop(up, 1), hop(down, -1)
-    up, down = ring_step(half, [pair(2) + [(up, 0)], pair(6) + [(down, 0)]])
-    up, down = hop(up, 1), hop(down, -1)
-    up, down = ring_step(half, [pair(1) + [(up, 0)], pair(7) + [(down, 0)]], [gate_grad])
-    up, down = hop(up, 1), hop(down, -1)
-    up_grad, down_grad = finish(half, pair(0) + [(up, 0), (down, 0)])
+    piece = far.shape[0]
+    total = along(total, first_only=True)
+    last = N_CHIP // 2 - 2
+    for r in range(last + 1):
+        terms = [(own, r * piece), (got, r * piece), (total, 0)]
+        if r < last:
+            (total,) = ring_step(place, terms, 1)
+            total = along(total)
+    same, crossed = ring_step(place, terms, 2)
+    same, crossed = along(same), along(crossed, cross=1)
+    row = (last + 1) * piece
+    up_grad, down_grad = finish(
+        piece // 2, [(own, row), (got, row), (same, 0), (crossed, 0)], gate_grad
+    )
     return (input_grad, gate_grad.T, up_grad[None], down_grad[None])
 
 

time: 143 us -> 141 us (0.986)
  the two profiles are of different devices: /device:TPU:30 before, /device:TPU:1 now
where the time goes in v3:
time: 141 us
  starting transfers between devices  64 us (45%)
  waiting for transfers between devices  49 us (35%)
  Pallas kernels  26 us (18%)
    all_to_all x2, waiting for transfers between devices, exchange(): lax.all_to_all(array.reshape(peers, ROWS8, -1), 'expert', split_axis=0, c...  32.1 us
    all_to_all x2, starting transfers between devices, exchange(): lax.all_to_all(array.reshape(peers, ROWS8, -1), 'expert', split_axis=0, c...  30.4 us
    ppermute x5, starting transfers between devices, along(): return lax.ppermute(array, 'dp', pairs)  25.4 us
    ppermute x5, waiting for transfers between devices, along(): return lax.ppermute(array, 'dp', pairs)  15.4 us
    ppermute x2, starting transfers between devices, swap(): return lax.ppermute(array, 'dp', [(i, i ^ 1) for i in range(n_dp)])  8.21 us
    pallas_call x1, Pallas kernels, blocks(): call(blocks_kernel, (shape(*back), shape(*kept), shape(*kept)), [SMEM] +...  7.61 us
    pallas_call x4, Pallas kernels, ring_step(): call(functools.partial(step_kernel, starts), (shape(rows // parts, width)...  6.66 us
    pallas_call x1, Pallas kernels, hidden_part(): call(hidden_kernel, (shape(rows, width),) * 4 + (shape(rows, LANE), shape...  4.65 us
  transfers between devices with their start and end apart: 9, of which 5 were waited for; matrix products, arithmetic and copies ran while one was open for 0% of the time, Pallas kernels for 5%

profile of v3, /device:TPU:1, one launch (start us, length us, event | category | flops | bytes accessed | tf_op | source)
XLA Modules:
  0.0 140.6 jit_solution(16969176704853573466)
XLA Ops:
  0.6 3.5 %shard_map.93 = (bf16[512,1280]{1,0:T(8,128)(2,1)}, bf16[2,320,128]{2,1,0:T(8,128)(2,1)}) custom-call(bf16[32,4096]{1,0:T(8,128)(2,1)} %x_hbm.1, bf16[32,4096]{1,0:T(8,128)(2,1)} %g_hbm.1, s32[2,128]{1,0:T(2,128)} %bitcast.24, bf16[2,128]{1,0:T(2,128)(2,1)} %bitcast.16), custom_call_target="tpu_custom_call" | custom-call | flops 1000000000 | bytes 4194304 | tf_op jit(solution)/shard_map/pallas_call | solution.py:278
  4.1 23.2 %all-to-all-start = ((bf16[64,8,1280]{2,1,0:T(8,128)(2,1)}), bf16[64,8,1280]{2,1,0:T(8,128)(2,1)S(1)}, u32[]{:S(2)}, u32[]{:S(2)}) async-start(bf16[64,8,1280]{2,1,0:T(8,128)(2,1)} %bitcast.18), calls=%async_computation | async-start | bytes 2621440 | tf_op jit(solution)/shard_map/all_to_all | solution.py:393
  27.4 32.1 %all-to-all-done = bf16[64,8,1280]{2,1,0:T(8,128)(2,1)S(1)} async-done(((bf16[64,8,1280]{2,1,0:T(8,128)(2,1)}), bf16[64,8,1280]{2,1,0:T(8,128)(2,1)S(1)}, u32[]{:S(2)}, u32[]{:S(2)}) %all-to-all-start) | async-done | bytes 1310752 | tf_op jit(solution)/shard_map/all_to_all | solution.py:393
  59.5 4.6 %shard_map.94 = (bf16[320,1024]{1,0:T(8,128)(2,1)S(1)}, bf16[320,1024]{1,0:T(8,128)(2,1)S(1)}, bf16[320,1024]{1,0:T(8,128)(2,1)S(1)}, bf16[320,1024]{1,0:T(8,128...) custom-call(s32[2]{0:T(128)S(1)} %pad_add_fusion.place_ref, bf16[512,1280]{1,0:T(8,128)(2,1)S(1)} %bitcast.13, ...), custom_call_target="tpu_custom_call" | custom-call | flops 3000000000 | bytes 8388608 | tf_op jit(solution)/shard_map/pallas_call | solution.py:302
  64.1 5.9 %collective-permute-start = (bf16[128,2048]{1,0:T(8,128)(2,1)S(1)}, bf16[128,2048]{1,0:T(8,128)(2,1)S(1)}, u32[]{:S(2)}, u32[]{:S(2)}) collective-permute-start(bf16[128,2048]{1,0:T(8,128)(2,1)S(1)} %get-tuple-element.27.refs_0_), channel_id=1, source_target_pairs={{0,64},{64,0},{128,192},{192,128},{256,320},{320,256},{384,448},{4... | collective-permute-start | bytes 1572872 | tf_op jit(solution)/shard_map/ppermute | solution.py:407
  70.1 1.5 %collective-permute-done.refs_1_ = bf16[128,2048]{1,0:T(8,128)(2,1)S(1)} collective-permute-done((bf16[128,2048]{1,0:T(8,128)(2,1)S(1)}, bf16[128,2048]{1,0:T(8,128)(2,1)S(1)}, u32[]{:S(2)}, u32[]{:S(2)}) %collective-permute-start) | collective-permute-done | bytes 524320 | tf_op jit(solution)/shard_map/ppermute | solution.py:407
  71.6 0.8 shard_map.95._
  72.3 7.6 %shard_map.96 = (bf16[512,768]{1,0:T(8,128)(2,1)}, bf16[448,2048]{1,0:T(8,128)(2,1)}, bf16[448,2048]{1,0:T(8,128)(2,1)}) custom-call(s32[2]{0:T(128)S(1)} %pad_add_fusion.place_ref, bf16[320,1024]{1,0:T(8,128)(2,1)S(1)} %get-tuple-element.22.feat, bf16[320,1024]{1,0:T(8,128)(2,1)S(1)} %get-tuple-element.23.scal, ...), custom_call_target="tpu_custom_call" | custom-call | flops 4000000000 | bytes 8388608 | tf_op jit(solution)/shard_map/pallas_call | solution.py:323
  79.9 2.3 %collective-permute-start.1 = (bf16[448,2048]{1,0:T(8,128)(2,1)}, bf16[448,2048]{1,0:T(8,128)(2,1)}, u32[]{:S(2)}, u32[]{:S(2)}) collective-permute-start(bf16[448,2048]{1,0:T(8,128)(2,1)} %get-tuple-element.33), channel_id=1, source_target_pairs={{0,64},{64,0},{128,192},{192,128},{256,320},{320,256},{384,448},{4... | collective-permute-start | bytes 5505032 | tf_op jit(solution)/shard_map/ppermute | solution.py:407
  82.2 0.7 collective-permute-start.2
  82.9 7.2 %all-to-all-start.1 = ((bf16[64,8,768]{2,1,0:T(8,128)(2,1)}), bf16[64,8,768]{2,1,0:T(8,128)(2,1)S(1)}, u32[]{:S(2)}, u32[]{:S(2)}) async-start(bf16[64,8,768]{2,1,0:T(8,128)(2,1)} %bitcast.8), calls=%async_computation.1 | async-start | bytes 1572864 | tf_op jit(solution)/shard_map/all_to_all | solution.py:393
  90.2 2.0 %shard_map.98 = bf16[128,2048]{1,0:T(8,128)(2,1)S(1)} custom-call(s32[2]{0:T(128)S(1)} %pad_add_fusion.place_ref, bf16[448,2048]{1,0:T(8,128)(2,1)} %get-tuple-element.32.refs_0_, bf16[448,2048]{1,0:T(8,128)(2,1)} %collective-permute-done.1.refs_1_, bf16[128,2048]{1,0:T(8,128)(2,1)S(1)} %collective-permute-done.2.refs_2_), custom_call_target="tpu_custom_call" | custom-call | flops 1000000 | bytes 1048576 | tf_op jit(solution)/shard_map/pallas_call | solution.py:347
  92.1 6.0 %collective-permute-start.3 = (bf16[128,2048]{1,0:T(8,128)(2,1)S(1)}, bf16[128,2048]{1,0:T(8,128)(2,1)S(1)}, u32[]{:S(2)}, u32[]{:S(2)}) collective-permute-start(bf16[128,2048]{1,0:T(8,128)(2,1)S(1)} %shard_map.98), channel_id=1, source_target_pairs={{0,128},{64,960},{128,256},{192,64},{256,384},{320,192},{384,512},... | collective-permute-start | bytes 1572872 | tf_op jit(solution)/shard_map/ppermute | solution.py:404
  98.1 6.1 %collective-permute-done.3.refs_2_ = bf16[128,2048]{1,0:T(8,128)(2,1)S(1)} collective-permute-done((bf16[128,2048]{1,0:T(8,128)(2,1)S(1)}, bf16[128,2048]{1,0:T(8,128)(2,1)S(1)}, u32[]{:S(2)}, u32[]{:S(2)}) %collective-permute-start.3) | collective-permute-done | bytes 524320 | tf_op jit(solution)/shard_map/ppermute | solution.py:404
  104.2 2.0 %shard_map.99 = bf16[128,2048]{1,0:T(8,128)(2,1)S(1)} custom-call(s32[2]{0:T(128)S(1)} %pad_add_fusion.place_ref, bf16[448,2048]{1,0:T(8,128)(2,1)} %get-tuple-element.32.refs_0_, bf16[448,2048]{1,0:T(8,128)(2,1)} %collective-permute-done.1.refs_1_, bf16[128,2048]{1,0:T(8,128)(2,1)S(1)} %collective-permute-done.3.refs_2_), custom_call_target="tpu_custom_call" | custom-call | flops 1000000 | bytes 1048576 | tf_op jit(solution)/shard_map/pallas_call | solution.py:347
  106.2 5.5 %collective-permute-start.4 = (bf16[128,2048]{1,0:T(8,128)(2,1)S(1)}, bf16[128,2048]{1,0:T(8,128)(2,1)S(1)}, u32[]{:S(2)}, u32[]{:S(2)}) collective-permute-start(bf16[128,2048]{1,0:T(8,128)(2,1)S(1)} %shard_map.99), channel_id=1, source_target_pairs={{0,128},{64,960},{128,256},{192,64},{256,384},{320,192},{384,512},... | collective-permute-start | bytes 1572872 | tf_op jit(solution)/shard_map/ppermute | solution.py:404
  111.7 6.1 %collective-permute-done.4.refs_2_ = bf16[128,2048]{1,0:T(8,128)(2,1)S(1)} collective-permute-done((bf16[128,2048]{1,0:T(8,128)(2,1)S(1)}, bf16[128,2048]{1,0:T(8,128)(2,1)S(1)}, u32[]{:S(2)}, u32[]{:S(2)}) %collective-permute-start.4) | collective-permute-done | bytes 524320 | tf_op jit(solution)/shard_map/ppermute | solution.py:404
  117.8 2.0 %shard_map.100 = (bf16[64,2048]{1,0:T(8,128)(2,1)S(1)}, bf16[64,2048]{1,0:T(8,128)(2,1)S(1)}) custom-call(s32[2]{0:T(128)S(1)} %pad_add_fusion.place_ref, bf16[448,2048]{1,0:T(8,128)(2,1)} %get-tuple-element.32.refs_0_, bf16[448,2048]{1,0:T(8,128)(2,1)} %collective-permute-done.1.refs_1_, bf16[128,2048]{1,0:T(8,128)(2,1)S(1)} %collective-permute-done.4.refs_2_), custom_call_target="tpu_custom_call" | custom-call | flops 1000000 | bytes 1048576 | tf_op jit(solution)/shard_map/pallas_call | solution.py:347
  119.8 5.0 %collective-permute-start.5 = (bf16[64,2048]{1,0:T(8,128)(2,1)S(1)}, bf16[64,2048]{1,0:T(8,128)(2,1)S(1)}, u32[]{:S(2)}, u32[]{:S(2)}) collective-permute-start(bf16[64,2048]{1,0:T(8,128)(2,1)S(1)} %get-tuple-element.34), channel_id=1, source_target_pairs={{0,128},{64,960},{128,256},{192,64},{256,384},{320,192},{384,512},... | collective-permute-start | bytes 786440 | tf_op jit(solution)/shard_map/ppermute | solution.py:404
  124.8 8.2 %collective-permute-start.6 = (bf16[64,2048]{1,0:T(8,128)(2,1)S(1)}, bf16[64,2048]{1,0:T(8,128)(2,1)S(1)}, u32[]{:S(2)}, u32[]{:S(2)}) collective-permute-start(bf16[64,2048]{1,0:T(8,128)(2,1)S(1)} %get-tuple-element.35), channel_id=1, source_target_pairs={{0,192},{64,896},{128,320},{192,0},{256,448},{320,128},{384,576},{... | collective-permute-start | bytes 786440 | tf_op jit(solution)/shard_map/ppermute | solution.py:404
  133.1 1.7 %shard_map.97 = (bf16[32,4096]{1,0:T(8,128)(2,1)}, bf16[2,128]{1,0:T(2,128)(2,1)}) custom-call(bf16[512,768]{1,0:T(8,128)(2,1)S(1)} %bitcast.14, bf16[2,320,128]{2,1,0:T(8,128)(2,1)S(1)} %copy-done.2, bf16[2,128]{1,0:T(2,128)(2,1)S(1)} %bitcast.17), custom_call_target="tpu_custom_call" | custom-call | flops 10000000000 | bytes 2097152 | tf_op jit(solution)/shard_map/pallas_call | solution.py:373
  134.8 3.2 %collective-permute-done.6.refs_3_ = bf16[64,2048]{1,0:T(8,128)(2,1)S(1)} collective-permute-done((bf16[64,2048]{1,0:T(8,128)(2,1)S(1)}, bf16[64,2048]{1,0:T(8,128)(2,1)S(1)}, u32[]{:S(2)}, u32[]{:S(2)}) %collective-permute-start.6) | collective-permute-done | bytes 262176 | tf_op jit(solution)/shard_map/ppermute | solution.py:404
  138.0 0.7 copy-done
  138.6 1.9 %shard_map.101 = (f32[64,1024]{1,0:T(8,128)}, f32[64,1024]{1,0:T(8,128)}) custom-call(bf16[448,2048]{1,0:T(8,128)(2,1)} %get-tuple-element.32.refs_0_, bf16[448,2048]{1,0:T(8,128)(2,1)} %collective-permute-done.1.refs_1_, bf16[64,2048]{1,0:T(8,128)(2,1)S(1)} %collective-permute-done.5.refs_2_, bf16[64,2048]{1,0:T(8,128)(2,1)S(1)} %collective-permute-done.6.refs_3_, ...), custom_call_target="tpu_custom_call" | custom-call | flops 1000000 | bytes 1048576 | tf_op jit(solution)/shard_map/pallas_call | solution.py:361
  (10 shorter events, 0.1 us)
Async XLA Ops:
  4.1 55.4 %all-to-all-start = ((bf16[64,8,1280]{2,1,0:T(8,128)(2,1)}), bf16[64,8,1280]{2,1,0:T(8,128)(2,1)S(1)}, u32[]{:S(2)}, u32[]{:S(2)}) async-start(bf16[64,8,1280]{2,1,0:T(8,128)(2,1)} %bitcast.18), calls=%async_computation | async-start | bytes 2621440 | tf_op jit(solution)/shard_map/all_to_all | solution.py:393
  64.1 7.5 %collective-permute-start = (bf16[128,2048]{1,0:T(8,128)(2,1)S(1)}, bf16[128,2048]{1,0:T(8,128)(2,1)S(1)}, u32[]{:S(2)}, u32[]{:S(2)}) collective-permute-start(bf16[128,2048]{1,0:T(8,128)(2,1)S(1)} %get-tuple-element.27.refs_0_), channel_id=1, source_target_pairs={{0,64},{64,0},{128,192},{192,128},{256,320},{320,256},{384,448},{4... | collective-permute-start | bytes 1572872 | tf_op jit(solution)/shard_map/ppermute | solution.py:407
  79.9 10.2 %collective-permute-start.1 = (bf16[448,2048]{1,0:T(8,128)(2,1)}, bf16[448,2048]{1,0:T(8,128)(2,1)}, u32[]{:S(2)}, u32[]{:S(2)}) collective-permute-start(bf16[448,2048]{1,0:T(8,128)(2,1)} %get-tuple-element.33), channel_id=1, source_target_pairs={{0,64},{64,0},{128,192},{192,128},{256,320},{320,256},{384,448},{4... | collective-permute-start | bytes 5505032 | tf_op jit(solution)/shard_map/ppermute | solution.py:407
  82.2 7.9 %collective-permute-start.2 = (bf16[128,2048]{1,0:T(8,128)(2,1)S(1)}, bf16[128,2048]{1,0:T(8,128)(2,1)S(1)}, u32[]{:S(2)}, u32[]{:S(2)}) collective-permute-start(bf16[128,2048]{1,0:T(8,128)(2,1)S(1)} %shard_map.95._), channel_id=1, source_target_pairs={{0,128},{128,256},{256,384},{384,512},{512,640},{640,768},{768,896... | collective-permute-start | bytes 1572872 | tf_op jit(solution)/shard_map/ppermute | solution.py:404
  82.9 50.1 %all-to-all-start.1 = ((bf16[64,8,768]{2,1,0:T(8,128)(2,1)}), bf16[64,8,768]{2,1,0:T(8,128)(2,1)S(1)}, u32[]{:S(2)}, u32[]{:S(2)}) async-start(bf16[64,8,768]{2,1,0:T(8,128)(2,1)} %bitcast.8), calls=%async_computation.1 | async-start | bytes 1572864 | tf_op jit(solution)/shard_map/all_to_all | solution.py:393
  92.1 12.1 %collective-permute-start.3 = (bf16[128,2048]{1,0:T(8,128)(2,1)S(1)}, bf16[128,2048]{1,0:T(8,128)(2,1)S(1)}, u32[]{:S(2)}, u32[]{:S(2)}) collective-permute-start(bf16[128,2048]{1,0:T(8,128)(2,1)S(1)} %shard_map.98), channel_id=1, source_target_pairs={{0,128},{64,960},{128,256},{192,64},{256,384},{320,192},{384,512},... | collective-permute-start | bytes 1572872 | tf_op jit(solution)/shard_map/ppermute | solution.py:404
  106.2 26.9 %copy-start.1 = (bf16[128,2]{0,1:T(2,128)(2,1)S(1)}, bf16[128,2]{0,1:T(2,128)(2,1)}, u32[]{:S(2)}) copy-start(bf16[128,2]{0,1:T(2,128)(2,1)} %param.9) | copy-start | bytes 1540
  106.2 26.9 %copy-start.2 = (bf16[2,320,128]{2,1,0:T(8,128)(2,1)S(1)}, bf16[2,320,128]{2,1,0:T(8,128)(2,1)}, u32[]{:S(2)}) copy-start(bf16[2,320,128]{2,1,0:T(8,128)(2,1)} %get-tuple-element.29.s_ref) | copy-start | bytes 491524
  106.2 11.6 %collective-permute-start.4 = (bf16[128,2048]{1,0:T(8,128)(2,1)S(1)}, bf16[128,2048]{1,0:T(8,128)(2,1)S(1)}, u32[]{:S(2)}, u32[]{:S(2)}) collective-permute-start(bf16[128,2048]{1,0:T(8,128)(2,1)S(1)} %shard_map.99), channel_id=1, source_target_pairs={{0,128},{64,960},{128,256},{192,64},{256,384},{320,192},{384,512},... | collective-permute-start | bytes 1572872 | tf_op jit(solution)/shard_map/ppermute | solution.py:404
  119.8 15.0 %collective-permute-start.5 = (bf16[64,2048]{1,0:T(8,128)(2,1)S(1)}, bf16[64,2048]{1,0:T(8,128)(2,1)S(1)}, u32[]{:S(2)}, u32[]{:S(2)}) collective-permute-start(bf16[64,2048]{1,0:T(8,128)(2,1)S(1)} %get-tuple-element.34), channel_id=1, source_target_pairs={{0,128},{64,960},{128,256},{192,64},{256,384},{320,192},{384,512},... | collective-permute-start | bytes 786440 | tf_op jit(solution)/shard_map/ppermute | solution.py:404
  124.8 13.2 %collective-permute-start.6 = (bf16[64,2048]{1,0:T(8,128)(2,1)S(1)}, bf16[64,2048]{1,0:T(8,128)(2,1)S(1)}, u32[]{:S(2)}, u32[]{:S(2)}) collective-permute-start(bf16[64,2048]{1,0:T(8,128)(2,1)S(1)} %get-tuple-element.35), channel_id=1, source_target_pairs={{0,192},{64,896},{128,320},{192,0},{256,448},{320,128},{384,576},{... | collective-permute-start | bytes 786440 | tf_op jit(solution)/shard_map/ppermute | solution.py:404
  138.0 0.7 copy-start

commit v4 on v3

--- a/solution.py
+++ b/solution.py
@@ -149,17 +149,48 @@
     return pl.ds(pl.multiple_of(at, piece), piece)
 
 
-def blocks_kernel(place_ref, feat, scal, hid, hg_ref, part_ref, up_hbm, _, *refs):
-    back_ref, own_ref, other_ref, up_ref, packed, back_v, left, own, other, sems = refs
-    load = pltpu.make_async_copy(up_hbm, up_ref, sems.at[0])
+def pieces_kernel(hg_ref, part_ref, up_hbm, _, out_ref, up_ref, packed, sem):
+    load = pltpu.make_async_copy(up_hbm, up_ref, sem)
     load.start()
+    peers = packed.shape[0] // ROWS8
+    rows = CAP * peers
+    packed[:rows, CAP * LANE :] = part_ref[...]
+    packed[rows:, CAP * LANE :] = jnp.zeros((packed.shape[0] - rows, LANE), BF16)
+    to_peer = by_peer(peers)
+    load.wait()
+    sent = mm_tr(hg_ref[...], up_ref[...]).astype(BF16)
+    for c in range(CAP):
+        for j in range(up_ref.shape[0] // LANE):
+            packed[j * peers : (j + 1) * peers, c * LANE : (c + 1) * LANE] = sent[
+                c * peers : (c + 1) * peers, j * LANE : (j + 1) * LANE
+            ]
+    out_ref[...] = mm(to_peer, packed[...]).astype(BF16)
+
+
+def presum_kernel(skip, own_hbm, got_hbm, _, out_ref, own, got, sems):
+    size = out_ref.shape[0] // 5
+    copies = []
+    for i in range(5):
+        for k, (a, b) in enumerate(((own_hbm, own), (got_hbm, got))):
+            source = a.at[pl.ds(skip + i * size, size)]
+            copies.append(pltpu.make_async_copy(source, b.at[pl.ds(i * size, size)], sems.at[2 * i + k]))
+            copies[-1].start()
+    for i in range(5):
+        here = slice(i * size, (i + 1) * size)
+        copies[2 * i].wait()
+        copies[2 * i + 1].wait()
+        out_ref[here, :] = (own[here, :].astype(F32) + got[here, :].astype(F32)).astype(BF16)
+
+
+def blocks_kernel(place_ref, feat, scal, hid, hg_ref, _, *refs):
+    own_ref, other_ref, mark_ref, left, own, other, sems = refs
     leaving = []
 
     def leave(source, target):
-        leaving.append(pltpu.make_async_copy(source, target, sems.at[1 + len(leaving)]))
+        leaving.append(pltpu.make_async_copy(source, target, sems.at[len(leaving)]))
         leaving[-1].start()
 
-    width = up_ref.shape[0]
+    width = feat.shape[1]
     piece = width // N_CHIP
     half = piece // 2
     first = place_ref[1] == 0
@@ -182,19 +213,7 @@
         other[rows, lanes] = jnp.where(first, total[half:], total[:half])
     leave(other, other_ref)
     leave(own, own_ref)
-    load.wait()
-    peers = packed.shape[0] // ROWS8
-    sent = mm_tr(hg_ref[...], up_ref[...]).astype(BF16)
-    for c in range(CAP):
-        for j in range(width // LANE):
-            packed[j * peers : (j + 1) * peers, c * LANE : (c + 1) * LANE] = sent[
-                c * peers : (c + 1) * peers, j * LANE : (j + 1) * LANE
-            ]
-    rows = CAP * peers
-    packed[:rows, CAP * LANE :] = part_ref[...]
-    packed[rows:, CAP * LANE :] = jnp.zeros((packed.shape[0] - rows, LANE), BF16)
-    back_v[...] = mm(by_peer(peers), packed[...]).astype(BF16)
-    leave(back_v, back_ref)
+    leave(left.at[pl.ds(0, 2 * ROWS8), pl.ds(0, LANE)], mark_ref)
     for copy in leaving:
         copy.wait()
 
@@ -226,7 +245,7 @@
 
 
 def last_kernel(width, rows, *refs):
-    ins, outs, (held, sems) = refs[: len(rows)], refs[len(rows) + 1 : -2], refs[-2:]
+    ins, outs, (held, sems) = refs[: len(rows)], refs[len(rows) : -2], refs[-2:]
     fetch(ins, rows, held, sems)
     for a, out in enumerate(outs):
         total = held[0, :, a * width : (a + 1) * width].astype(F32)
@@ -315,29 +334,51 @@
     )(place, received, w_up, w_down)
 
 
-def blocks(place, arrays, w_up, after):
+def blocks(place, arrays, after):
     rows, width = arrays[0].shape
-    peers = rows // CAP
-    back = (peers * ROWS8, (CAP + 1) * LANE)
     kept = (width // 2 - width // N_CHIP // 2, 2 * width)
     return call(
         blocks_kernel,
-        (shape(*back), shape(*kept), shape(*kept)),
-        [SMEM] + [VMEM] * 5 + [HBM, ANY],
+        (shape(*kept), shape(*kept), shape(2 * ROWS8, LANE)),
+        [SMEM] + [VMEM] * 4 + [ANY],
         [
-            pltpu.VMEM(w_up.shape, BF16),
-            pltpu.VMEM(back, BF16),
-            pltpu.VMEM(back, BF16),
             pltpu.VMEM((rows, 2 * width // N_CHIP), BF16),
             pltpu.VMEM(kept, BF16),
             pltpu.VMEM(kept, BF16),
-            pltpu.SemaphoreType.DMA((4,)),
+            pltpu.SemaphoreType.DMA((3,)),
         ],
-        flops=4 * 10**9,
+        flops=3 * 10**9,
         moved=8 << 20,
         limit=50,
         place=ANY,
-    )(place, *arrays, w_up, after)
+    )(place, *arrays, after)
+
+
+def pieces(hidden_grad, part, w_up, after):
+    rows, width = hidden_grad.shape
+    back = (rows // CAP * ROWS8, (CAP + 1) * LANE)
+    return call(
+        pieces_kernel,
+        shape(*back),
+        [VMEM, VMEM, HBM, ANY],
+        [pltpu.VMEM(w_up.shape, BF16), pltpu.VMEM(back, BF16), pltpu.SemaphoreType.DMA],
+        flops=2 * 10**9,
+        moved=4 << 20,
+        limit=50,
+    )(hidden_grad, part, w_up, after)
+
+
+def presum(own, got, skip, after):
+    size = (own.shape[0] - skip, own.shape[1])
+    return call(
+        functools.partial(presum_kernel, skip),
+        shape(*size),
+        [ANY] * 3,
+        [pltpu.VMEM(size, BF16)] * 2 + [pltpu.SemaphoreType.DMA((10,))],
+        flops=2 * 10**9,
+        moved=8 << 20,
+        limit=52,
+    )(own, got, after)
 
 
 def ring_step(place, terms, parts):
@@ -351,22 +392,22 @@
         [pltpu.VMEM((len(arrays), rows, width), BF16), pltpu.SemaphoreType.DMA((len(arrays),))],
         flops=10**6,
         moved=1 << 20,
-        limit=52,
+        limit=52 if len(arrays) > 2 else 49,
     )(place, *arrays)
 
 
-def finish(half, terms, after):
+def finish(half, terms):
     arrays, rows = zip(*terms)
     width = arrays[0].shape[1]
     return call(
         functools.partial(last_kernel, width // 2, rows),
         (shape(half, width // 2, dtype=F32),) * 2,
-        [ANY] * (len(arrays) + 1),
+        [ANY] * len(arrays),
         [pltpu.VMEM((len(arrays), half, width), BF16), pltpu.SemaphoreType.DMA((len(arrays),))],
         flops=10**6,
         moved=1 << 20,
-        limit=52,
-    )(*arrays, after)
+        limit=49,
+    )(*arrays)
 
 
 def combine(returned, picks, gates, tokens, width):
@@ -411,23 +452,23 @@
     *arrays, far = hidden_part(place, received, w_up, w_down)
     got_far = swap(far)
     (total,) = ring_step(place, [(far, 0), (got_far, 0)], 1)
-    back, own, other = blocks(place, arrays, w_up, total)
+    own, other, mark = blocks(place, arrays[:4], total)
     got = swap(other)
+    back = pieces(arrays[3], arrays[4], w_up, mark)
     returned = exchange(back)
     input_grad, gate_grad = combine(returned, picks, gates_t, tokens, width)
     piece = far.shape[0]
     total = along(total, first_only=True)
-    last = N_CHIP // 2 - 2
-    for r in range(last + 1):
-        terms = [(own, r * piece), (got, r * piece), (total, 0)]
-        if r < last:
-            (total,) = ring_step(place, terms, 1)
-            total = along(total)
-    same, crossed = ring_step(place, terms, 2)
+    (total,) = ring_step(place, [(own, 0), (got, 0), (total, 0)], 1)
+    summed = presum(own, got, piece, total)
+    total = along(total)
+    (total,) = ring_step(place, [(summed, 0), (total, 0)], 1)
+    total = along(total)
+    same, crossed = ring_step(place, [(summed, piece), (total, 0)], 2)
     same, crossed = along(same), along(crossed, cross=1)
-    row = (last + 1) * piece
+    row = 2 * piece
     up_grad, down_grad = finish(
-        piece // 2, [(own, row), (got, row), (same, 0), (crossed, 0)], gate_grad
+        piece // 2, [(summed, row), (same, 0), (crossed, 0)]
     )
     return (input_grad, gate_grad.T, up_grad[None], down_grad[None])
 

time: 141 us -> 134 us (0.950)
  starting transfers between devices: 64 us -> 61.7 us
  Pallas kernels: 26 us -> 24 us
  waiting for transfers between devices: 49 us -> 47.1 us
    pallas_call x4, Pallas kernels: 6.66 us -> 4.26 us  [ring_step(): call(functools.partial(step_kernel, starts), (shape(rows // parts, width)...]
    ppermute x5, starting transfers between devices: 25.4 us -> 23.1 us  [along(): return lax.ppermute(array, 'dp', pairs)]
    ppermute x5, waiting for transfers between devices: 15.4 us -> 13.5 us  [along(): return lax.ppermute(array, 'dp', pairs)]
    pallas_call x1 -> x3, Pallas kernels: 7.61 us -> 9.02 us  [the longest x1 4.62 us: blocks(): call(blocks_kernel, (shape(*kept), shape(*kept), shape(2 * ROWS8, LANE)),...]
  transfers between devices with their start and end apart: 9 -> 9, of which waited for: 5 -> 5; matrix products, arithmetic and copies ran while one was open for 0% -> 0% of each run, Pallas kernels for 5% -> 7%
where the time goes in v4:
time: 134 us
  starting transfers between devices  61.7 us (46%)
  waiting for transfers between devices  47.1 us (35%)
  Pallas kernels  24 us (18%)
    all_to_all x2, waiting for transfers between devices, exchange(): lax.all_to_all(array.reshape(peers, ROWS8, -1), 'expert', split_axis=0, c...  32.1 us
    all_to_all x2, starting transfers between devices, exchange(): lax.all_to_all(array.reshape(peers, ROWS8, -1), 'expert', split_axis=0, c...  30.4 us
    ppermute x5, starting transfers between devices, along(): return lax.ppermute(array, 'dp', pairs)  23.1 us
    ppermute x5, waiting for transfers between devices, along(): return lax.ppermute(array, 'dp', pairs)  13.5 us
    ppermute x2, starting transfers between devices, swap(): return lax.ppermute(array, 'dp', [(i, i ^ 1) for i in range(n_dp)])  8.2 us
    pallas_call x1, Pallas kernels, hidden_part(): call(hidden_kernel, (shape(rows, width),) * 4 + (shape(rows, LANE), shape...  4.65 us
    pallas_call x1, Pallas kernels, blocks(): call(blocks_kernel, (shape(*kept), shape(*kept), shape(2 * ROWS8, LANE)),...  4.62 us
    pallas_call x4, Pallas kernels, ring_step(): call(functools.partial(step_kernel, starts), (shape(rows // parts, width)...  4.26 us
  transfers between devices with their start and end apart: 9, of which 5 were waited for; matrix products, arithmetic and copies ran while one was open for 0% of the time, Pallas kernels for 7%

profile of v4, /device:TPU:1, one launch (start us, length us, event | category | flops | bytes accessed | tf_op | source)
XLA Modules:
  0.0 133.8 jit_solution(3381282354675467585)
XLA Ops:
  0.6 3.5 %shard_map.93 = (bf16[512,1280]{1,0:T(8,128)(2,1)}, bf16[2,320,128]{2,1,0:T(8,128)(2,1)}) custom-call(bf16[32,4096]{1,0:T(8,128)(2,1)} %x_hbm.1, bf16[32,4096]{1,0:T(8,128)(2,1)} %g_hbm.1, s32[2,128]{1,0:T(2,128)} %bitcast.23, bf16[2,128]{1,0:T(2,128)(2,1)} %bitcast.17), custom_call_target="tpu_custom_call" | custom-call | flops 1000000000 | bytes 4194304 | tf_op jit(solution)/shard_map/pallas_call | solution.py:297
  4.1 23.2 %all-to-all-start = ((bf16[64,8,1280]{2,1,0:T(8,128)(2,1)}), bf16[64,8,1280]{2,1,0:T(8,128)(2,1)S(1)}, u32[]{:S(2)}, u32[]{:S(2)}) async-start(bf16[64,8,1280]{2,1,0:T(8,128)(2,1)} %bitcast.19), calls=%async_computation | async-start | bytes 2621440 | tf_op jit(solution)/shard_map/all_to_all | solution.py:434
  27.4 32.1 %all-to-all-done = bf16[64,8,1280]{2,1,0:T(8,128)(2,1)S(1)} async-done(((bf16[64,8,1280]{2,1,0:T(8,128)(2,1)}), bf16[64,8,1280]{2,1,0:T(8,128)(2,1)S(1)}, u32[]{:S(2)}, u32[]{:S(2)}) %all-to-all-start) | async-done | bytes 1310752 | tf_op jit(solution)/shard_map/all_to_all | solution.py:434
  59.5 4.7 %shard_map.94 = (bf16[320,1024]{1,0:T(8,128)(2,1)S(1)}, bf16[320,1024]{1,0:T(8,128)(2,1)S(1)}, bf16[320,1024]{1,0:T(8,128)(2,1)S(1)}, bf16[320,1024]{1,0:T(8,128...) custom-call(s32[2]{0:T(128)S(1)} %pad_add_fusion.place_ref, bf16[512,1280]{1,0:T(8,128)(2,1)S(1)} %bitcast.13, ...), custom_call_target="tpu_custom_call" | custom-call | flops 3000000000 | bytes 8388608 | tf_op jit(solution)/shard_map/pallas_call | solution.py:321
  64.1 5.9 %collective-permute-start = (bf16[128,2048]{1,0:T(8,128)(2,1)S(1)}, bf16[128,2048]{1,0:T(8,128)(2,1)S(1)}, u32[]{:S(2)}, u32[]{:S(2)}) collective-permute-start(bf16[128,2048]{1,0:T(8,128)(2,1)S(1)} %get-tuple-element.27.refs_0_), channel_id=1, source_target_pairs={{0,64},{64,0},{128,192},{192,128},{256,320},{320,256},{384,448},{4... | collective-permute-start | bytes 1572872 | tf_op jit(solution)/shard_map/ppermute | solution.py:448
  70.1 1.5 %collective-permute-done.refs_1_ = bf16[128,2048]{1,0:T(8,128)(2,1)S(1)} collective-permute-done((bf16[128,2048]{1,0:T(8,128)(2,1)S(1)}, bf16[128,2048]{1,0:T(8,128)(2,1)S(1)}, u32[]{:S(2)}, u32[]{:S(2)}) %collective-permute-start) | collective-permute-done | bytes 524320 | tf_op jit(solution)/shard_map/ppermute | solution.py:448
  71.6 0.8 shard_map.95._
  72.3 4.6 %shard_map.96 = (bf16[448,2048]{1,0:T(8,128)(2,1)}, bf16[448,2048]{1,0:T(8,128)(2,1)}, bf16[16,128]{1,0:T(8,128)(2,1)S(1)}) custom-call(s32[2]{0:T(128)S(1)} %pad_add_fusion.place_ref, bf16[320,1024]{1,0:T(8,128)(2,1)S(1)} %get-tuple-element.24.feat, bf16[320,1024]{1,0:T(8,128)(2,1)S(1)} %get-tuple-element.25.scal, ...), custom_call_target="tpu_custom_call" | custom-call | flops 3000000000 | bytes 8388608 | tf_op jit(solution)/shard_map/pallas_call | solution.py:340
  77.0 2.3 %collective-permute-start.1 = (bf16[448,2048]{1,0:T(8,128)(2,1)}, bf16[448,2048]{1,0:T(8,128)(2,1)}, u32[]{:S(2)}, u32[]{:S(2)}) collective-permute-start(bf16[448,2048]{1,0:T(8,128)(2,1)} %get-tuple-element.33), channel_id=1, source_target_pairs={{0,64},{64,0},{128,192},{192,128},{256,320},{320,256},{384,448},{4... | collective-permute-start | bytes 5505032 | tf_op jit(solution)/shard_map/ppermute | solution.py:448
  80.0 2.6 %shard_map.97 = bf16[512,768]{1,0:T(8,128)(2,1)} custom-call(bf16[320,1024]{1,0:T(8,128)(2,1)S(1)} %get-tuple-element.22.hg_ref, bf16[320,128]{1,0:T(8,128)(2,1)S(1)} %get-tuple-element.23.part_ref, bf16[1024,1024]{1,0:T(8,128)(2,1)S(1)} %bitcast.16, bf16[16,128]{1,0:T(8,128)(2,1)S(1)} %get-tuple-element.28._), custom_call_target="tpu_custom_call" | custom-call | flops 2000000000 | bytes 4194304 | tf_op jit(solution)/shard_map/pallas_call | solution.py:360
  82.6 7.2 %all-to-all-start.1 = ((bf16[64,8,768]{2,1,0:T(8,128)(2,1)}), bf16[64,8,768]{2,1,0:T(8,128)(2,1)S(1)}, u32[]{:S(2)}, u32[]{:S(2)}) async-start(bf16[64,8,768]{2,1,0:T(8,128)(2,1)} %bitcast.8), calls=%async_computation.1 | async-start | bytes 1572864 | tf_op jit(solution)/shard_map/all_to_all | solution.py:434
  89.8 2.0 %shard_map.99._ = bf16[128,2048]{1,0:T(8,128)(2,1)S(1)} custom-call(s32[2]{0:T(128)S(1)} %pad_add_fusion.place_ref, bf16[448,2048]{1,0:T(8,128)(2,1)} %get-tuple-element.32.refs_0_.own_hbm, bf16[448,2048]{1,0:T(8,128)(2,1)} %collective-permute-done.1.refs_1_.got_hbm, bf16[128,2048]{1,0:T(8,128)(2,1)S(1)} %collective-permute-done.2.refs_2_), custom_call_target="tpu_custom_call" | custom-call | flops 1000000 | bytes 1048576 | tf_op jit(solution)/shard_map/pallas_call | solution.py:388
  91.7 6.0 %collective-permute-start.3 = (bf16[128,2048]{1,0:T(8,128)(2,1)S(1)}, bf16[128,2048]{1,0:T(8,128)(2,1)S(1)}, u32[]{:S(2)}, u32[]{:S(2)}) collective-permute-start(bf16[128,2048]{1,0:T(8,128)(2,1)S(1)} %shard_map.99._), channel_id=1, source_target_pairs={{0,128},{64,960},{128,256},{192,64},{256,384},{320,192},{384,512},... | collective-permute-start | bytes 1572872 | tf_op jit(solution)/shard_map/ppermute | solution.py:445
  97.8 1.8 %shard_map.100.refs_0_ = bf16[320,2048]{1,0:T(8,128)(2,1)S(1)} custom-call(bf16[448,2048]{1,0:T(8,128)(2,1)} %get-tuple-element.32.refs_0_.own_hbm, bf16[448,2048]{1,0:T(8,128)(2,1)} %collective-permute-done.1.refs_1_.got_hbm, bf16[128,2048]{1,0:T(8,128)(2,1)S(1)} %shard_map.99._), custom_call_target="tpu_custom_call" | custom-call | flops 2000000000 | bytes 8388608 | tf_op jit(solution)/shard_map/pallas_call | solution.py:373
  99.6 4.3 %collective-permute-done.3.refs_1_ = bf16[128,2048]{1,0:T(8,128)(2,1)S(1)} collective-permute-done((bf16[128,2048]{1,0:T(8,128)(2,1)S(1)}, bf16[128,2048]{1,0:T(8,128)(2,1)S(1)}, u32[]{:S(2)}, u32[]{:S(2)}) %collective-permute-start.3) | collective-permute-done | bytes 524320 | tf_op jit(solution)/shard_map/ppermute | solution.py:445
  103.9 0.8 shard_map.101
  104.6 5.3 %collective-permute-start.4 = (bf16[128,2048]{1,0:T(8,128)(2,1)S(1)}, bf16[128,2048]{1,0:T(8,128)(2,1)S(1)}, u32[]{:S(2)}, u32[]{:S(2)}) collective-permute-start(bf16[128,2048]{1,0:T(8,128)(2,1)S(1)} %shard_map.101), channel_id=1, source_target_pairs={{0,128},{64,960},{128,256},{192,64},{256,384},{320,192},{384,512},... | collective-permute-start | bytes 1572872 | tf_op jit(solution)/shard_map/ppermute | solution.py:445
  109.9 6.1 %collective-permute-done.4.refs_1_ = bf16[128,2048]{1,0:T(8,128)(2,1)S(1)} collective-permute-done((bf16[128,2048]{1,0:T(8,128)(2,1)S(1)}, bf16[128,2048]{1,0:T(8,128)(2,1)S(1)}, u32[]{:S(2)}, u32[]{:S(2)}) %collective-permute-start.4) | collective-permute-done | bytes 524320 | tf_op jit(solution)/shard_map/ppermute | solution.py:445
  116.1 0.8 shard_map.102
  116.9 5.0 %collective-permute-start.5 = (bf16[64,2048]{1,0:T(8,128)(2,1)S(1)}, bf16[64,2048]{1,0:T(8,128)(2,1)S(1)}, u32[]{:S(2)}, u32[]{:S(2)}) collective-permute-start(bf16[64,2048]{1,0:T(8,128)(2,1)S(1)} %get-tuple-element.34), channel_id=1, source_target_pairs={{0,128},{64,960},{128,256},{192,64},{256,384},{320,192},{384,512},... | collective-permute-start | bytes 786440 | tf_op jit(solution)/shard_map/ppermute | solution.py:445
  121.9 6.1 %collective-permute-start.6 = (bf16[64,2048]{1,0:T(8,128)(2,1)S(1)}, bf16[64,2048]{1,0:T(8,128)(2,1)S(1)}, u32[]{:S(2)}, u32[]{:S(2)}) collective-permute-start(bf16[64,2048]{1,0:T(8,128)(2,1)S(1)} %get-tuple-element.35), channel_id=1, source_target_pairs={{0,192},{64,896},{128,320},{192,0},{256,448},{320,128},{384,576},{... | collective-permute-start | bytes 786440 | tf_op jit(solution)/shard_map/ppermute | solution.py:445
  128.0 1.7 %shard_map.98 = (bf16[32,4096]{1,0:T(8,128)(2,1)}, bf16[2,128]{1,0:T(2,128)(2,1)}) custom-call(bf16[512,768]{1,0:T(8,128)(2,1)S(1)} %bitcast.14, bf16[2,320,128]{2,1,0:T(8,128)(2,1)S(1)} %copy-done.2, bf16[2,128]{1,0:T(2,128)(2,1)S(1)} %bitcast.18), custom_call_target="tpu_custom_call" | custom-call | flops 10000000000 | bytes 2097152 | tf_op jit(solution)/shard_map/pallas_call | solution.py:414
  129.7 3.2 %collective-permute-done.6.refs_2_ = bf16[64,2048]{1,0:T(8,128)(2,1)S(1)} collective-permute-done((bf16[64,2048]{1,0:T(8,128)(2,1)S(1)}, bf16[64,2048]{1,0:T(8,128)(2,1)S(1)}, u32[]{:S(2)}, u32[]{:S(2)}) %collective-permute-start.6) | collective-permute-done | bytes 262176 | tf_op jit(solution)/shard_map/ppermute | solution.py:445
  132.9 0.9 shard_map.103
  (12 shorter events, 0.8 us)
Async XLA Ops:
  4.1 55.4 %all-to-all-start = ((bf16[64,8,1280]{2,1,0:T(8,128)(2,1)}), bf16[64,8,1280]{2,1,0:T(8,128)(2,1)S(1)}, u32[]{:S(2)}, u32[]{:S(2)}) async-start(bf16[64,8,1280]{2,1,0:T(8,128)(2,1)} %bitcast.19), calls=%async_computation | async-start | bytes 2621440 | tf_op jit(solution)/shard_map/all_to_all | solution.py:434
  64.1 7.5 %collective-permute-start = (bf16[128,2048]{1,0:T(8,128)(2,1)S(1)}, bf16[128,2048]{1,0:T(8,128)(2,1)S(1)}, u32[]{:S(2)}, u32[]{:S(2)}) collective-permute-start(bf16[128,2048]{1,0:T(8,128)(2,1)S(1)} %get-tuple-element.27.refs_0_), channel_id=1, source_target_pairs={{0,64},{64,0},{128,192},{192,128},{256,320},{320,256},{384,448},{4... | collective-permute-start | bytes 1572872 | tf_op jit(solution)/shard_map/ppermute | solution.py:448
  72.3 7.6 %copy-start = (bf16[1,1024,1024]{2,1,0:T(8,128)(2,1)S(1)}, bf16[1,1024,1024]{2,1,0:T(8,128)(2,1)}, u32[]{:S(2)}) copy-start(bf16[1,1024,1024]{2,1,0:T(8,128)(2,1)} %param.10) | copy-start | bytes 6291460
  77.0 12.8 %collective-permute-start.1 = (bf16[448,2048]{1,0:T(8,128)(2,1)}, bf16[448,2048]{1,0:T(8,128)(2,1)}, u32[]{:S(2)}, u32[]{:S(2)}) collective-permute-start(bf16[448,2048]{1,0:T(8,128)(2,1)} %get-tuple-element.33), channel_id=1, source_target_pairs={{0,64},{64,0},{128,192},{192,128},{256,320},{320,256},{384,448},{4... | collective-permute-start | bytes 5505032 | tf_op jit(solution)/shard_map/ppermute | solution.py:448
  79.2 10.5 %collective-permute-start.2 = (bf16[128,2048]{1,0:T(8,128)(2,1)S(1)}, bf16[128,2048]{1,0:T(8,128)(2,1)S(1)}, u32[]{:S(2)}, u32[]{:S(2)}) collective-permute-start(bf16[128,2048]{1,0:T(8,128)(2,1)S(1)} %shard_map.95._), channel_id=1, source_target_pairs={{0,128},{128,256},{256,384},{384,512},{512,640},{640,768},{768,896... | collective-permute-start | bytes 1572872 | tf_op jit(solution)/shard_map/ppermute | solution.py:445
  82.6 45.4 %all-to-all-start.1 = ((bf16[64,8,768]{2,1,0:T(8,128)(2,1)}), bf16[64,8,768]{2,1,0:T(8,128)(2,1)S(1)}, u32[]{:S(2)}, u32[]{:S(2)}) async-start(bf16[64,8,768]{2,1,0:T(8,128)(2,1)} %bitcast.8), calls=%async_computation.1 | async-start | bytes 1572864 | tf_op jit(solution)/shard_map/all_to_all | solution.py:434
  91.7 12.1 %collective-permute-start.3 = (bf16[128,2048]{1,0:T(8,128)(2,1)S(1)}, bf16[128,2048]{1,0:T(8,128)(2,1)S(1)}, u32[]{:S(2)}, u32[]{:S(2)}) collective-permute-start(bf16[128,2048]{1,0:T(8,128)(2,1)S(1)} %shard_map.99._), channel_id=1, source_target_pairs={{0,128},{64,960},{128,256},{192,64},{256,384},{320,192},{384,512},... | collective-permute-start | bytes 1572872 | tf_op jit(solution)/shard_map/ppermute | solution.py:445
  99.6 28.4 %copy-start.1 = (bf16[128,2]{0,1:T(2,128)(2,1)S(1)}, bf16[128,2]{0,1:T(2,128)(2,1)}, u32[]{:S(2)}) copy-start(bf16[128,2]{0,1:T(2,128)(2,1)} %param.9) | copy-start | bytes 1540
  99.6 28.4 %copy-start.2 = (bf16[2,320,128]{2,1,0:T(8,128)(2,1)S(1)}, bf16[2,320,128]{2,1,0:T(8,128)(2,1)}, u32[]{:S(2)}) copy-start(bf16[2,320,128]{2,1,0:T(8,128)(2,1)} %get-tuple-element.29.s_ref) | copy-start | bytes 491524
  104.6 11.4 %collective-permute-start.4 = (bf16[128,2048]{1,0:T(8,128)(2,1)S(1)}, bf16[128,2048]{1,0:T(8,128)(2,1)S(1)}, u32[]{:S(2)}, u32[]{:S(2)}) collective-permute-start(bf16[128,2048]{1,0:T(8,128)(2,1)S(1)} %shard_map.101), channel_id=1, source_target_pairs={{0,128},{64,960},{128,256},{192,64},{256,384},{320,192},{384,512},... | collective-permute-start | bytes 1572872 | tf_op jit(solution)/shard_map/ppermute | solution.py:445
  116.9 12.9 %collective-permute-start.5 = (bf16[64,2048]{1,0:T(8,128)(2,1)S(1)}, bf16[64,2048]{1,0:T(8,128)(2,1)S(1)}, u32[]{:S(2)}, u32[]{:S(2)}) collective-permute-start(bf16[64,2048]{1,0:T(8,128)(2,1)S(1)} %get-tuple-element.34), channel_id=1, source_target_pairs={{0,128},{64,960},{128,256},{192,64},{256,384},{320,192},{384,512},... | collective-permute-start | bytes 786440 | tf_op jit(solution)/shard_map/ppermute | solution.py:445
  121.9 11.0 %collective-permute-start.6 = (bf16[64,2048]{1,0:T(8,128)(2,1)S(1)}, bf16[64,2048]{1,0:T(8,128)(2,1)S(1)}, u32[]{:S(2)}, u32[]{:S(2)}) collective-permute-start(bf16[64,2048]{1,0:T(8,128)(2,1)S(1)} %get-tuple-element.35), channel_id=1, source_target_pairs={{0,192},{64,896},{128,320},{192,0},{256,448},{320,128},{384,576},{... | collective-permute-start | bytes 786440 | tf_op jit(solution)/shard_map/ppermute | solution.py:445

commit v5 on v4

--- a/solution.py
+++ b/solution.py
@@ -13,6 +13,7 @@
 LANE = 128
 ROWS8 = 8
 N_CHIP = 8
+CUTS = 4
 F32 = jnp.float32
 BF16 = jnp.bfloat16
 VMEM = pl.BlockSpec(memory_space=pltpu.VMEM)
@@ -70,6 +71,8 @@
     copies = [pltpu.make_async_copy(a, b, sems.at[i]) for i, (a, b) in enumerate(pairs)]
     for copy in copies:
         copy.start()
+    in_order = natural_order(ids_ref.shape[1])
+    to_peer = by_peer(out_ref.shape[0] // ROWS8)
     copies[0].wait()
     copies[1].wait()
     block = ids_ref.shape[1]
@@ -79,7 +82,7 @@
     top = jnp.concatenate(
         [ids_ref[...].astype(F32), gates_ref[...].astype(F32), jnp.zeros((4, block), F32)], axis=0
     ).astype(BF16)
-    top = mm(top, natural_order(block))
+    top = mm(top, in_order)
     expert = iota((peers, block), 0).astype(F32)
     hot = [expert == top[k : k + 1] for k in range(TOP)]
     chosen = one_hot(hot[0] | hot[1])
@@ -103,7 +106,7 @@
                 packed[j * peers : (j + 1) * peers, (a * CAP + c) * LANE : (a * CAP + c + 1) * LANE] = (
                     sent[c * peers : (c + 1) * peers, j * LANE : (j + 1) * LANE]
                 )
-    out_ref[...] = mm(by_peer(peers), packed[...]).astype(BF16)
+    out_ref[...] = mm(to_peer, packed[...]).astype(BF16)
 
 
 def unpack(source, target, peers, base):
@@ -205,14 +208,18 @@
             lanes = slice(a * width, (a + 1) * width)
             own[rows, lanes] = total[:piece]
             other[rows, lanes] = total[piece:]
+        at = pl.ds((r - 1) * piece, piece)
+        leave(other.at[at], other_ref.at[at])
+        leave(own.at[at], own_ref.at[at])
     rows = slice((middle - 1) * piece, (middle - 1) * piece + half)
     for a, (source, right) in enumerate(((feat, hg_ref), (hid, scal))):
         total = tr_mm(source[:, rows_of(place_ref, 0, width)], right[...]).astype(BF16)
         lanes = slice(a * width, (a + 1) * width)
         own[rows, lanes] = jnp.where(first, total[:half], total[half:])
         other[rows, lanes] = jnp.where(first, total[half:], total[:half])
-    leave(other, other_ref)
-    leave(own, own_ref)
+    at = pl.ds((middle - 1) * piece, half)
+    leave(other.at[at], other_ref.at[at])
+    leave(own.at[at], own_ref.at[at])
     leave(left.at[pl.ds(0, 2 * ROWS8), pl.ds(0, LANE)], mark_ref)
     for copy in leaving:
         copy.wait()
@@ -231,17 +238,32 @@
 
 def step_kernel(rows, place_ref, *refs):
     ins, outs, (held, sems) = refs[: len(rows)], refs[len(rows) : -2], refs[-2:]
-    fetch(ins, rows, held, sems)
-    total = held[0].astype(F32)
-    for i in range(1, len(rows)):
-        total = total + held[i].astype(F32)
-    total = total.astype(BF16)
-    if len(outs) == 1:
-        outs[0][...] = total
-    else:
-        first, half = place_ref[1] == 0, outs[0].shape[0]
-        outs[0][...] = jnp.where(first, total[:half], total[half:])
-        outs[1][...] = jnp.where(first, total[half:], total[:half])
+    size = held.shape[1] // CUTS
+    copies = []
+    for at in range(CUTS):
+        for i, (ref, row) in enumerate(zip(ins, rows)):
+            source = ref.at[pl.ds(row + at * size, size)]
+            target = held.at[i, pl.ds(at * size, size)]
+            copies.append(pltpu.make_async_copy(source, target, sems.at[len(copies)]))
+            copies[-1].start()
+    sums = []
+    for at in range(CUTS):
+        here = slice(at * size, (at + 1) * size)
+        total = None
+        for i in range(len(rows)):
+            copies[at * len(rows) + i].wait()
+            term = held[i, here, :].astype(F32)
+            total = term if total is None else total + term
+        sums.append(total.astype(BF16))
+        if len(outs) == 1:
+            outs[0][here, :] = sums[-1]
+    if len(outs) == 2:
+        first = place_ref[1] == 0
+        for at in range(CUTS // 2):
+            here = slice(at * size, (at + 1) * size)
+            low, high = sums[at], sums[at + CUTS // 2]
+            outs[0][here, :] = jnp.where(first, low, high)
+            outs[1][here, :] = jnp.where(first, high, low)
 
 
 def last_kernel(width, rows, *refs):
@@ -345,7 +367,7 @@
             pltpu.VMEM((rows, 2 * width // N_CHIP), BF16),
             pltpu.VMEM(kept, BF16),
             pltpu.VMEM(kept, BF16),
-            pltpu.SemaphoreType.DMA((3,)),
+            pltpu.SemaphoreType.DMA((9,)),
         ],
         flops=3 * 10**9,
         moved=8 << 20,
@@ -389,7 +411,7 @@
         functools.partial(step_kernel, starts),
         (shape(rows // parts, width),) * parts,
         [SMEM] + [ANY] * len(arrays),
-        [pltpu.VMEM((len(arrays), rows, width), BF16), pltpu.SemaphoreType.DMA((len(arrays),))],
+        [pltpu.VMEM((len(arrays), rows, width), BF16), pltpu.SemaphoreType.DMA((CUTS * len(arrays),))],
         flops=10**6,
         moved=1 << 20,
         limit=52 if len(arrays) > 2 else 49,

time: 134 us -> 138 us (1.030)
  Pallas kernels: 24 us -> 27.5 us
    pallas_call x4, Pallas kernels: 4.26 us -> 8.67 us  [ring_step(): call(functools.partial(step_kernel, starts), (shape(rows // parts, width)...]
  transfers between devices with their start and end apart: 9 -> 9, of which waited for: 5 -> 5; matrix products, arithmetic and copies ran while one was open for 0% -> 0% of each run, Pallas kernels for 7% -> 9%
where the time goes in v5:
time: 138 us; the launch traced here: 137 us
  starting transfers between devices  61.7 us (45%)
  waiting for transfers between devices  47.1 us (34%)
  Pallas kernels  27.5 us (20%)
    all_to_all x2, waiting for transfers between devices, exchange(): lax.all_to_all(array.reshape(peers, ROWS8, -1), 'expert', split_axis=0, c...  32.1 us
    all_to_all x2, starting transfers between devices, exchange(): lax.all_to_all(array.reshape(peers, ROWS8, -1), 'expert', split_axis=0, c...  30.4 us
    ppermute x5, starting transfers between devices, along(): return lax.ppermute(array, 'dp', pairs)  23 us
    ppermute x5, waiting for transfers between devices, along(): return lax.ppermute(array, 'dp', pairs)  13.5 us
    pallas_call x4, Pallas kernels, ring_step(): call(functools.partial(step_kernel, starts), (shape(rows // parts, width)...  8.67 us
    ppermute x2, starting transfers between devices, swap(): return lax.ppermute(array, 'dp', [(i, i ^ 1) for i in range(n_dp)])  8.22 us
    pallas_call x1, Pallas kernels, hidden_part(): call(hidden_kernel, (shape(rows, width),) * 4 + (shape(rows, LANE), shape...  4.66 us
    pallas_call x1, Pallas kernels, blocks(): call(blocks_kernel, (shape(*kept), shape(*kept), shape(2 * ROWS8, LANE)),...  3.73 us
  transfers between devices with their start and end apart: 9, of which 5 were waited for; matrix products, arithmetic and copies ran while one was open for 0% of the time, Pallas kernels for 9%

profile of v5, /device:TPU:1, one launch (start us, length us, event | category | flops | bytes accessed | tf_op | source)
XLA Modules:
  0.0 137.3 jit_solution(1709070197016806037)
XLA Ops:
  0.6 3.4 %shard_map.93 = (bf16[512,1280]{1,0:T(8,128)(2,1)}, bf16[2,320,128]{2,1,0:T(8,128)(2,1)}) custom-call(bf16[32,4096]{1,0:T(8,128)(2,1)} %x_hbm.1, bf16[32,4096]{1,0:T(8,128)(2,1)} %g_hbm.1, s32[2,128]{1,0:T(2,128)} %bitcast.23, bf16[2,128]{1,0:T(2,128)(2,1)} %bitcast.17), custom_call_target="tpu_custom_call" | custom-call | flops 1000000000 | bytes 4194304 | tf_op jit(solution)/shard_map/pallas_call | solution.py:319
  4.1 23.2 %all-to-all-start = ((bf16[64,8,1280]{2,1,0:T(8,128)(2,1)}), bf16[64,8,1280]{2,1,0:T(8,128)(2,1)S(1)}, u32[]{:S(2)}, u32[]{:S(2)}) async-start(bf16[64,8,1280]{2,1,0:T(8,128)(2,1)} %bitcast.19), calls=%async_computation | async-start | bytes 2621440 | tf_op jit(solution)/shard_map/all_to_all | solution.py:456
  27.3 32.1 %all-to-all-done = bf16[64,8,1280]{2,1,0:T(8,128)(2,1)S(1)} async-done(((bf16[64,8,1280]{2,1,0:T(8,128)(2,1)}), bf16[64,8,1280]{2,1,0:T(8,128)(2,1)S(1)}, u32[]{:S(2)}, u32[]{:S(2)}) %all-to-all-start) | async-done | bytes 1310752 | tf_op jit(solution)/shard_map/all_to_all | solution.py:456
  59.4 4.7 %shard_map.94 = (bf16[320,1024]{1,0:T(8,128)(2,1)S(1)}, bf16[320,1024]{1,0:T(8,128)(2,1)S(1)}, bf16[320,1024]{1,0:T(8,128)(2,1)S(1)}, bf16[320,1024]{1,0:T(8,128...) custom-call(s32[2]{0:T(128)S(1)} %pad_add_fusion.place_ref, bf16[512,1280]{1,0:T(8,128)(2,1)S(1)} %bitcast.13, ...), custom_call_target="tpu_custom_call" | custom-call | flops 3000000000 | bytes 8388608 | tf_op jit(solution)/shard_map/pallas_call | solution.py:343
  64.1 5.9 %collective-permute-start = (bf16[128,2048]{1,0:T(8,128)(2,1)S(1)}, bf16[128,2048]{1,0:T(8,128)(2,1)S(1)}, u32[]{:S(2)}, u32[]{:S(2)}) collective-permute-start(bf16[128,2048]{1,0:T(8,128)(2,1)S(1)} %get-tuple-element.27.refs_0_), channel_id=1, source_target_pairs={{0,64},{64,0},{128,192},{192,128},{256,320},{320,256},{384,448},{4... | collective-permute-start | bytes 1572872 | tf_op jit(solution)/shard_map/ppermute | solution.py:470
  70.0 1.5 %collective-permute-done.refs_1_ = bf16[128,2048]{1,0:T(8,128)(2,1)S(1)} collective-permute-done((bf16[128,2048]{1,0:T(8,128)(2,1)S(1)}, bf16[128,2048]{1,0:T(8,128)(2,1)S(1)}, u32[]{:S(2)}, u32[]{:S(2)}) %collective-permute-start) | collective-permute-done | bytes 524320 | tf_op jit(solution)/shard_map/ppermute | solution.py:470
  71.6 2.1 %shard_map.95._ = bf16[128,2048]{1,0:T(8,128)(2,1)S(1)} custom-call(s32[2]{0:T(128)S(1)} %pad_add_fusion.place_ref, bf16[128,2048]{1,0:T(8,128)(2,1)S(1)} %get-tuple-element.27.refs_0_, bf16[128,2048]{1,0:T(8,128)(2,1)S(1)} %collective-permute-done.refs_1_), custom_call_target="tpu_custom_call" | custom-call | flops 1000000 | bytes 1048576 | tf_op jit(solution)/shard_map/pallas_call | solution.py:410
  73.7 3.7 %shard_map.96 = (bf16[448,2048]{1,0:T(8,128)(2,1)}, bf16[448,2048]{1,0:T(8,128)(2,1)}, bf16[16,128]{1,0:T(8,128)(2,1)S(1)}) custom-call(s32[2]{0:T(128)S(1)} %pad_add_fusion.place_ref, bf16[320,1024]{1,0:T(8,128)(2,1)S(1)} %get-tuple-element.24.feat, bf16[320,1024]{1,0:T(8,128)(2,1)S(1)} %get-tuple-element.25.scal, ...), custom_call_target="tpu_custom_call" | custom-call | flops 3000000000 | bytes 8388608 | tf_op jit(solution)/shard_map/pallas_call | solution.py:362
  77.4 2.3 %collective-permute-start.1 = (bf16[448,2048]{1,0:T(8,128)(2,1)}, bf16[448,2048]{1,0:T(8,128)(2,1)}, u32[]{:S(2)}, u32[]{:S(2)}) collective-permute-start(bf16[448,2048]{1,0:T(8,128)(2,1)} %get-tuple-element.33), channel_id=1, source_target_pairs={{0,64},{64,0},{128,192},{192,128},{256,320},{320,256},{384,448},{4... | collective-permute-start | bytes 5505032 | tf_op jit(solution)/shard_map/ppermute | solution.py:470
  80.4 2.6 %shard_map.97 = bf16[512,768]{1,0:T(8,128)(2,1)} custom-call(bf16[320,1024]{1,0:T(8,128)(2,1)S(1)} %get-tuple-element.22.hg_ref, bf16[320,128]{1,0:T(8,128)(2,1)S(1)} %get-tuple-element.23.part_ref, bf16[1024,1024]{1,0:T(8,128)(2,1)S(1)} %bitcast.16, bf16[16,128]{1,0:T(8,128)(2,1)S(1)} %get-tuple-element.28._), custom_call_target="tpu_custom_call" | custom-call | flops 2000000000 | bytes 4194304 | tf_op jit(solution)/shard_map/pallas_call | solution.py:382
  83.0 7.3 %all-to-all-start.1 = ((bf16[64,8,768]{2,1,0:T(8,128)(2,1)}), bf16[64,8,768]{2,1,0:T(8,128)(2,1)S(1)}, u32[]{:S(2)}, u32[]{:S(2)}) async-start(bf16[64,8,768]{2,1,0:T(8,128)(2,1)} %bitcast.8), calls=%async_computation.1 | async-start | bytes 1572864 | tf_op jit(solution)/shard_map/all_to_all | solution.py:456
  90.3 2.2 %shard_map.99._ = bf16[128,2048]{1,0:T(8,128)(2,1)S(1)} custom-call(s32[2]{0:T(128)S(1)} %pad_add_fusion.place_ref, bf16[448,2048]{1,0:T(8,128)(2,1)} %get-tuple-element.32.refs_0_.own_hbm, bf16[448,2048]{1,0:T(8,128)(2,1)} %collective-permute-done.1.refs_1_.got_hbm, bf16[128,2048]{1,0:T(8,128)(2,1)S(1)} %collective-permute-done.2.refs_2_), custom_call_target="tpu_custom_call" | custom-call | flops 1000000 | bytes 1048576 | tf_op jit(solution)/shard_map/pallas_call | solution.py:410
  92.6 5.9 %collective-permute-start.3 = (bf16[128,2048]{1,0:T(8,128)(2,1)S(1)}, bf16[128,2048]{1,0:T(8,128)(2,1)S(1)}, u32[]{:S(2)}, u32[]{:S(2)}) collective-permute-start(bf16[128,2048]{1,0:T(8,128)(2,1)S(1)} %shard_map.99._), channel_id=1, source_target_pairs={{0,128},{64,960},{128,256},{192,64},{256,384},{320,192},{384,512},... | collective-permute-start | bytes 1572872 | tf_op jit(solution)/shard_map/ppermute | solution.py:467
  98.5 1.8 %shard_map.100.refs_0_ = bf16[320,2048]{1,0:T(8,128)(2,1)S(1)} custom-call(bf16[448,2048]{1,0:T(8,128)(2,1)} %get-tuple-element.32.refs_0_.own_hbm, bf16[448,2048]{1,0:T(8,128)(2,1)} %collective-permute-done.1.refs_1_.got_hbm, bf16[128,2048]{1,0:T(8,128)(2,1)S(1)} %shard_map.99._), custom_call_target="tpu_custom_call" | custom-call | flops 2000000000 | bytes 8388608 | tf_op jit(solution)/shard_map/pallas_call | solution.py:395
  100.3 4.3 %collective-permute-done.3.refs_1_ = bf16[128,2048]{1,0:T(8,128)(2,1)S(1)} collective-permute-done((bf16[128,2048]{1,0:T(8,128)(2,1)S(1)}, bf16[128,2048]{1,0:T(8,128)(2,1)S(1)}, u32[]{:S(2)}, u32[]{:S(2)}) %collective-permute-start.3) | collective-permute-done | bytes 524320 | tf_op jit(solution)/shard_map/ppermute | solution.py:467
  104.6 2.1 %shard_map.101 = bf16[128,2048]{1,0:T(8,128)(2,1)S(1)} custom-call(s32[2]{0:T(128)S(1)} %pad_add_fusion.place_ref, bf16[320,2048]{1,0:T(8,128)(2,1)S(1)} %shard_map.100.refs_0_, bf16[128,2048]{1,0:T(8,128)(2,1)S(1)} %collective-permute-done.3.refs_1_), custom_call_target="tpu_custom_call" | custom-call | flops 1000000 | bytes 1048576 | tf_op jit(solution)/shard_map/pallas_call | solution.py:410
  106.7 5.3 %collective-permute-start.4 = (bf16[128,2048]{1,0:T(8,128)(2,1)S(1)}, bf16[128,2048]{1,0:T(8,128)(2,1)S(1)}, u32[]{:S(2)}, u32[]{:S(2)}) collective-permute-start(bf16[128,2048]{1,0:T(8,128)(2,1)S(1)} %shard_map.101), channel_id=1, source_target_pairs={{0,128},{64,960},{128,256},{192,64},{256,384},{320,192},{384,512},... | collective-permute-start | bytes 1572872 | tf_op jit(solution)/shard_map/ppermute | solution.py:467
  112.0 6.1 %collective-permute-done.4.refs_1_ = bf16[128,2048]{1,0:T(8,128)(2,1)S(1)} collective-permute-done((bf16[128,2048]{1,0:T(8,128)(2,1)S(1)}, bf16[128,2048]{1,0:T(8,128)(2,1)S(1)}, u32[]{:S(2)}, u32[]{:S(2)}) %collective-permute-start.4) | collective-permute-done | bytes 524320 | tf_op jit(solution)/shard_map/ppermute | solution.py:467
  118.1 2.2 %shard_map.102 = (bf16[64,2048]{1,0:T(8,128)(2,1)S(1)}, bf16[64,2048]{1,0:T(8,128)(2,1)S(1)}) custom-call(s32[2]{0:T(128)S(1)} %pad_add_fusion.place_ref, bf16[320,2048]{1,0:T(8,128)(2,1)S(1)} %shard_map.100.refs_0_, bf16[128,2048]{1,0:T(8,128)(2,1)S(1)} %collective-permute-done.4.refs_1_), custom_call_target="tpu_custom_call" | custom-call | flops 1000000 | bytes 1048576 | tf_op jit(solution)/shard_map/pallas_call | solution.py:410
  120.3 5.0 %collective-permute-start.5 = (bf16[64,2048]{1,0:T(8,128)(2,1)S(1)}, bf16[64,2048]{1,0:T(8,128)(2,1)S(1)}, u32[]{:S(2)}, u32[]{:S(2)}) collective-permute-start(bf16[64,2048]{1,0:T(8,128)(2,1)S(1)} %get-tuple-element.34), channel_id=1, source_target_pairs={{0,128},{64,960},{128,256},{192,64},{256,384},{320,192},{384,512},... | collective-permute-start | bytes 786440 | tf_op jit(solution)/shard_map/ppermute | solution.py:467
  125.4 6.1 %collective-permute-start.6 = (bf16[64,2048]{1,0:T(8,128)(2,1)S(1)}, bf16[64,2048]{1,0:T(8,128)(2,1)S(1)}, u32[]{:S(2)}, u32[]{:S(2)}) collective-permute-start(bf16[64,2048]{1,0:T(8,128)(2,1)S(1)} %get-tuple-element.35), channel_id=1, source_target_pairs={{0,192},{64,896},{128,320},{192,0},{256,448},{320,128},{384,576},{... | collective-permute-start | bytes 786440 | tf_op jit(solution)/shard_map/ppermute | solution.py:467
  131.5 1.7 %shard_map.98 = (bf16[32,4096]{1,0:T(8,128)(2,1)}, bf16[2,128]{1,0:T(2,128)(2,1)}) custom-call(bf16[512,768]{1,0:T(8,128)(2,1)S(1)} %bitcast.14, bf16[2,320,128]{2,1,0:T(8,128)(2,1)S(1)} %copy-done.2, bf16[2,128]{1,0:T(2,128)(2,1)S(1)} %bitcast.18), custom_call_target="tpu_custom_call" | custom-call | flops 10000000000 | bytes 2097152 | tf_op jit(solution)/shard_map/pallas_call | solution.py:436
  133.2 3.2 %collective-permute-done.6.refs_2_ = bf16[64,2048]{1,0:T(8,128)(2,1)S(1)} collective-permute-done((bf16[64,2048]{1,0:T(8,128)(2,1)S(1)}, bf16[64,2048]{1,0:T(8,128)(2,1)S(1)}, u32[]{:S(2)}, u32[]{:S(2)}) %collective-permute-start.6) | collective-permute-done | bytes 262176 | tf_op jit(solution)/shard_map/ppermute | solution.py:467
  136.4 0.9 shard_map.103
  (12 shorter events, 0.8 us)
Async XLA Ops:
  4.1 55.4 %all-to-all-start = ((bf16[64,8,1280]{2,1,0:T(8,128)(2,1)}), bf16[64,8,1280]{2,1,0:T(8,128)(2,1)S(1)}, u32[]{:S(2)}, u32[]{:S(2)}) async-start(bf16[64,8,1280]{2,1,0:T(8,128)(2,1)} %bitcast.19), calls=%async_computation | async-start | bytes 2621440 | tf_op jit(solution)/shard_map/all_to_all | solution.py:456
  64.1 7.5 %collective-permute-start = (bf16[128,2048]{1,0:T(8,128)(2,1)S(1)}, bf16[128,2048]{1,0:T(8,128)(2,1)S(1)}, u32[]{:S(2)}, u32[]{:S(2)}) collective-permute-start(bf16[128,2048]{1,0:T(8,128)(2,1)S(1)} %get-tuple-element.27.refs_0_), channel_id=1, source_target_pairs={{0,64},{64,0},{128,192},{192,128},{256,320},{320,256},{384,448},{4... | collective-permute-start | bytes 1572872 | tf_op jit(solution)/shard_map/ppermute | solution.py:470
  73.7 6.7 %copy-start = (bf16[1,1024,1024]{2,1,0:T(8,128)(2,1)S(1)}, bf16[1,1024,1024]{2,1,0:T(8,128)(2,1)}, u32[]{:S(2)}) copy-start(bf16[1,1024,1024]{2,1,0:T(8,128)(2,1)} %param.10) | copy-start | bytes 6291460
  77.4 12.9 %collective-permute-start.1 = (bf16[448,2048]{1,0:T(8,128)(2,1)}, bf16[448,2048]{1,0:T(8,128)(2,1)}, u32[]{:S(2)}, u32[]{:S(2)}) collective-permute-start(bf16[448,2048]{1,0:T(8,128)(2,1)} %get-tuple-element.33), channel_id=1, source_target_pairs={{0,64},{64,0},{128,192},{192,128},{256,320},{320,256},{384,448},{4... | collective-permute-start | bytes 5505032 | tf_op jit(solution)/shard_map/ppermute | solution.py:470
  79.7 10.6 %collective-permute-start.2 = (bf16[128,2048]{1,0:T(8,128)(2,1)S(1)}, bf16[128,2048]{1,0:T(8,128)(2,1)S(1)}, u32[]{:S(2)}, u32[]{:S(2)}) collective-permute-start(bf16[128,2048]{1,0:T(8,128)(2,1)S(1)} %shard_map.95._), channel_id=1, source_target_pairs={{0,128},{128,256},{256,384},{384,512},{512,640},{640,768},{768,896... | collective-permute-start | bytes 1572872 | tf_op jit(solution)/shard_map/ppermute | solution.py:467
  83.0 48.4 %all-to-all-start.1 = ((bf16[64,8,768]{2,1,0:T(8,128)(2,1)}), bf16[64,8,768]{2,1,0:T(8,128)(2,1)S(1)}, u32[]{:S(2)}, u32[]{:S(2)}) async-start(bf16[64,8,768]{2,1,0:T(8,128)(2,1)} %bitcast.8), calls=%async_computation.1 | async-start | bytes 1572864 | tf_op jit(solution)/shard_map/all_to_all | solution.py:456
  92.6 12.0 %collective-permute-start.3 = (bf16[128,2048]{1,0:T(8,128)(2,1)S(1)}, bf16[128,2048]{1,0:T(8,128)(2,1)S(1)}, u32[]{:S(2)}, u32[]{:S(2)}) collective-permute-start(bf16[128,2048]{1,0:T(8,128)(2,1)S(1)} %shard_map.99._), channel_id=1, source_target_pairs={{0,128},{64,960},{128,256},{192,64},{256,384},{320,192},{384,512},... | collective-permute-start | bytes 1572872 | tf_op jit(solution)/shard_map/ppermute | solution.py:467
  100.3 31.2 %copy-start.1 = (bf16[128,2]{0,1:T(2,128)(2,1)S(1)}, bf16[128,2]{0,1:T(2,128)(2,1)}, u32[]{:S(2)}) copy-start(bf16[128,2]{0,1:T(2,128)(2,1)} %param.9) | copy-start | bytes 1540
  100.3 31.2 %copy-start.2 = (bf16[2,320,128]{2,1,0:T(8,128)(2,1)S(1)}, bf16[2,320,128]{2,1,0:T(8,128)(2,1)}, u32[]{:S(2)}) copy-start(bf16[2,320,128]{2,1,0:T(8,128)(2,1)} %get-tuple-element.29.s_ref) | copy-start | bytes 491524
  106.7 11.4 %collective-permute-start.4 = (bf16[128,2048]{1,0:T(8,128)(2,1)S(1)}, bf16[128,2048]{1,0:T(8,128)(2,1)S(1)}, u32[]{:S(2)}, u32[]{:S(2)}) collective-permute-start(bf16[128,2048]{1,0:T(8,128)(2,1)S(1)} %shard_map.101), channel_id=1, source_target_pairs={{0,128},{64,960},{128,256},{192,64},{256,384},{320,192},{384,512},... | collective-permute-start | bytes 1572872 | tf_op jit(solution)/shard_map/ppermute | solution.py:467
  120.3 12.9 %collective-permute-start.5 = (bf16[64,2048]{1,0:T(8,128)(2,1)S(1)}, bf16[64,2048]{1,0:T(8,128)(2,1)S(1)}, u32[]{:S(2)}, u32[]{:S(2)}) collective-permute-start(bf16[64,2048]{1,0:T(8,128)(2,1)S(1)} %get-tuple-element.34), channel_id=1, source_target_pairs={{0,128},{64,960},{128,256},{192,64},{256,384},{320,192},{384,512},... | collective-permute-start | bytes 786440 | tf_op jit(solution)/shard_map/ppermute | solution.py:467
  125.4 11.0 %collective-permute-start.6 = (bf16[64,2048]{1,0:T(8,128)(2,1)S(1)}, bf16[64,2048]{1,0:T(8,128)(2,1)S(1)}, u32[]{:S(2)}, u32[]{:S(2)}) collective-permute-start(bf16[64,2048]{1,0:T(8,128)(2,1)S(1)} %get-tuple-element.35), channel_id=1, source_target_pairs={{0,192},{64,896},{128,320},{192,0},{256,448},{320,128},{384,576},{... | collective-permute-start | bytes 786440 | tf_op jit(solution)/shard_map/ppermute | solution.py:467

commit v6 on v4

--- a/solution.py
+++ b/solution.py
@@ -70,6 +70,8 @@
     copies = [pltpu.make_async_copy(a, b, sems.at[i]) for i, (a, b) in enumerate(pairs)]
     for copy in copies:
         copy.start()
+    in_order = natural_order(ids_ref.shape[1])
+    to_peer = by_peer(out_ref.shape[0] // ROWS8)
     copies[0].wait()
     copies[1].wait()
     block = ids_ref.shape[1]
@@ -79,7 +81,7 @@
     top = jnp.concatenate(
         [ids_ref[...].astype(F32), gates_ref[...].astype(F32), jnp.zeros((4, block), F32)], axis=0
     ).astype(BF16)
-    top = mm(top, natural_order(block))
+    top = mm(top, in_order)
     expert = iota((peers, block), 0).astype(F32)
     hot = [expert == top[k : k + 1] for k in range(TOP)]
     chosen = one_hot(hot[0] | hot[1])
@@ -103,7 +105,7 @@
                 packed[j * peers : (j + 1) * peers, (a * CAP + c) * LANE : (a * CAP + c + 1) * LANE] = (
                     sent[c * peers : (c + 1) * peers, j * LANE : (j + 1) * LANE]
                 )
-    out_ref[...] = mm(by_peer(peers), packed[...]).astype(BF16)
+    out_ref[...] = mm(to_peer, packed[...]).astype(BF16)
 
 
 def unpack(source, target, peers, base):
@@ -205,14 +207,18 @@
             lanes = slice(a * width, (a + 1) * width)
             own[rows, lanes] = total[:piece]
             other[rows, lanes] = total[piece:]
+        at = pl.ds((r - 1) * piece, piece)
+        leave(other.at[at], other_ref.at[at])
+        leave(own.at[at], own_ref.at[at])
     rows = slice((middle - 1) * piece, (middle - 1) * piece + half)
     for a, (source, right) in enumerate(((feat, hg_ref), (hid, scal))):
         total = tr_mm(source[:, rows_of(place_ref, 0, width)], right[...]).astype(BF16)
         lanes = slice(a * width, (a + 1) * width)
         own[rows, lanes] = jnp.where(first, total[:half], total[half:])
         other[rows, lanes] = jnp.where(first, total[half:], total[:half])
-    leave(other, other_ref)
-    leave(own, own_ref)
+    at = pl.ds((middle - 1) * piece, half)
+    leave(other.at[at], other_ref.at[at])
+    leave(own.at[at], own_ref.at[at])
     leave(left.at[pl.ds(0, 2 * ROWS8), pl.ds(0, LANE)], mark_ref)
     for copy in leaving:
         copy.wait()
@@ -230,12 +236,16 @@
 
 
 def step_kernel(rows, place_ref, *refs):
-    ins, outs, (held, sems) = refs[: len(rows)], refs[len(rows) : -2], refs[-2:]
-    fetch(ins, rows, held, sems)
-    total = held[0].astype(F32)
-    for i in range(1, len(rows)):
-        total = total + held[i].astype(F32)
-    total = total.astype(BF16)
+    ins, rest = refs[: len(rows)], refs[len(rows) :]
+    if len(rows) > 2:
+        *outs, held, sems = rest
+        fetch(ins, rows, held, sems)
+        terms = [held[i].astype(F32) for i in range(len(rows))]
+    else:
+        outs = rest
+        size = outs[0].shape[0] * len(outs)
+        terms = [ref[row : row + size, :].astype(F32) for ref, row in zip(ins, rows)]
+    total = functools.reduce(jnp.add, terms).astype(BF16)
     if len(outs) == 1:
         outs[0][...] = total
     else:
@@ -345,7 +355,7 @@
             pltpu.VMEM((rows, 2 * width // N_CHIP), BF16),
             pltpu.VMEM(kept, BF16),
             pltpu.VMEM(kept, BF16),
-            pltpu.SemaphoreType.DMA((3,)),
+            pltpu.SemaphoreType.DMA((9,)),
         ],
         flops=3 * 10**9,
         moved=8 << 20,
@@ -385,14 +395,16 @@
     arrays, starts = zip(*terms)
     width = arrays[0].shape[1]
     rows = width // 2 // N_CHIP
+    near = len(arrays) <= 2
+    held = [pltpu.VMEM((len(arrays), rows, width), BF16), pltpu.SemaphoreType.DMA((len(arrays),))]
     return call(
         functools.partial(step_kernel, starts),
         (shape(rows // parts, width),) * parts,
-        [SMEM] + [ANY] * len(arrays),
-        [pltpu.VMEM((len(arrays), rows, width), BF16), pltpu.SemaphoreType.DMA((len(arrays),))],
+        [SMEM] + [VMEM if near else ANY] * len(arrays),
+        [] if near else held,
         flops=10**6,
         moved=1 << 20,
-        limit=52 if len(arrays) > 2 else 49,
+        limit=49 if near else 52,
     )(place, *arrays)
 
 

time: 134 us -> 133 us (level)
  no operation moved by 1% of the time
where the time goes in v6:
time: 133 us
  starting transfers between devices  61.7 us (46%)
  waiting for transfers between devices  47.1 us (35%)
  Pallas kernels  22.8 us (17%)
    all_to_all x2, waiting for transfers between devices, exchange(): lax.all_to_all(array.reshape(peers, ROWS8, -1), 'expert', split_axis=0, c...  32.1 us
    all_to_all x2, starting transfers between devices, exchange(): lax.all_to_all(array.reshape(peers, ROWS8, -1), 'expert', split_axis=0, c...  30.4 us
    ppermute x5, starting transfers between devices, along(): return lax.ppermute(array, 'dp', pairs)  23 us
    ppermute x5, waiting for transfers between devices, along(): return lax.ppermute(array, 'dp', pairs)  13.5 us
    ppermute x2, starting transfers between devices, swap(): return lax.ppermute(array, 'dp', [(i, i ^ 1) for i in range(n_dp)])  8.22 us
    pallas_call x1, Pallas kernels, hidden_part(): call(hidden_kernel, (shape(rows, width),) * 4 + (shape(rows, LANE), shape...  4.66 us
    pallas_call x4, Pallas kernels, ring_step(): call(functools.partial(step_kernel, starts), (shape(rows // parts, width)...  3.98 us
    pallas_call x1, Pallas kernels, blocks(): call(blocks_kernel, (shape(*kept), shape(*kept), shape(2 * ROWS8, LANE)),...  3.73 us
  transfers between devices with their start and end apart: 9, of which 5 were waited for; matrix products, arithmetic and copies ran while one was open for 0% of the time, Pallas kernels for 7%

profile of v6, /device:TPU:1, one launch (start us, length us, event | category | flops | bytes accessed | tf_op | source)
XLA Modules:
  0.0 132.6 jit_solution(10688603096025047453)
XLA Ops:
  0.6 3.4 %shard_map.93 = (bf16[512,1280]{1,0:T(8,128)(2,1)}, bf16[2,320,128]{2,1,0:T(8,128)(2,1)}) custom-call(bf16[32,4096]{1,0:T(8,128)(2,1)} %x_hbm.1, bf16[32,4096]{1,0:T(8,128)(2,1)} %g_hbm.1, s32[2,128]{1,0:T(2,128)} %bitcast.23, bf16[2,128]{1,0:T(2,128)(2,1)} %bitcast.17), custom_call_target="tpu_custom_call" | custom-call | flops 1000000000 | bytes 4194304 | tf_op jit(solution)/shard_map/pallas_call | solution.py:307
  4.1 23.2 %all-to-all-start = ((bf16[64,8,1280]{2,1,0:T(8,128)(2,1)}), bf16[64,8,1280]{2,1,0:T(8,128)(2,1)S(1)}, u32[]{:S(2)}, u32[]{:S(2)}) async-start(bf16[64,8,1280]{2,1,0:T(8,128)(2,1)} %bitcast.19), calls=%async_computation | async-start | bytes 2621440 | tf_op jit(solution)/shard_map/all_to_all | solution.py:446
  27.3 32.1 %all-to-all-done = bf16[64,8,1280]{2,1,0:T(8,128)(2,1)S(1)} async-done(((bf16[64,8,1280]{2,1,0:T(8,128)(2,1)}), bf16[64,8,1280]{2,1,0:T(8,128)(2,1)S(1)}, u32[]{:S(2)}, u32[]{:S(2)}) %all-to-all-start) | async-done | bytes 1310752 | tf_op jit(solution)/shard_map/all_to_all | solution.py:446
  59.4 4.7 %shard_map.94 = (bf16[320,1024]{1,0:T(8,128)(2,1)S(1)}, bf16[320,1024]{1,0:T(8,128)(2,1)S(1)}, bf16[320,1024]{1,0:T(8,128)(2,1)S(1)}, bf16[320,1024]{1,0:T(8,128...) custom-call(s32[2]{0:T(128)S(1)} %pad_add_fusion.place_ref, bf16[512,1280]{1,0:T(8,128)(2,1)S(1)} %bitcast.13, ...), custom_call_target="tpu_custom_call" | custom-call | flops 3000000000 | bytes 8388608 | tf_op jit(solution)/shard_map/pallas_call | solution.py:331
  64.1 5.9 %collective-permute-start = (bf16[128,2048]{1,0:T(8,128)(2,1)S(1)}, bf16[128,2048]{1,0:T(8,128)(2,1)S(1)}, u32[]{:S(2)}, u32[]{:S(2)}) collective-permute-start(bf16[128,2048]{1,0:T(8,128)(2,1)S(1)} %get-tuple-element.27.refs_0_), channel_id=1, source_target_pairs={{0,64},{64,0},{128,192},{192,128},{256,320},{320,256},{384,448},{4... | collective-permute-start | bytes 1572872 | tf_op jit(solution)/shard_map/ppermute | solution.py:460
  70.0 1.5 %collective-permute-done.refs_1_ = bf16[128,2048]{1,0:T(8,128)(2,1)S(1)} collective-permute-done((bf16[128,2048]{1,0:T(8,128)(2,1)S(1)}, bf16[128,2048]{1,0:T(8,128)(2,1)S(1)}, u32[]{:S(2)}, u32[]{:S(2)}) %collective-permute-start) | collective-permute-done | bytes 524320 | tf_op jit(solution)/shard_map/ppermute | solution.py:460
  71.6 0.7 shard_map.95._
  72.2 3.7 %shard_map.96 = (bf16[448,2048]{1,0:T(8,128)(2,1)}, bf16[448,2048]{1,0:T(8,128)(2,1)}, bf16[16,128]{1,0:T(8,128)(2,1)S(1)}) custom-call(s32[2]{0:T(128)S(1)} %pad_add_fusion.place_ref, bf16[320,1024]{1,0:T(8,128)(2,1)S(1)} %get-tuple-element.24.feat, bf16[320,1024]{1,0:T(8,128)(2,1)S(1)} %get-tuple-element.25.scal, ...), custom_call_target="tpu_custom_call" | custom-call | flops 3000000000 | bytes 8388608 | tf_op jit(solution)/shard_map/pallas_call | solution.py:350
  76.0 2.3 %collective-permute-start.1 = (bf16[448,2048]{1,0:T(8,128)(2,1)}, bf16[448,2048]{1,0:T(8,128)(2,1)}, u32[]{:S(2)}, u32[]{:S(2)}) collective-permute-start(bf16[448,2048]{1,0:T(8,128)(2,1)} %get-tuple-element.33), channel_id=1, source_target_pairs={{0,64},{64,0},{128,192},{192,128},{256,320},{320,256},{384,448},{4... | collective-permute-start | bytes 5505032 | tf_op jit(solution)/shard_map/ppermute | solution.py:460
  78.3 0.7 collective-permute-start.2
  79.0 2.6 %shard_map.97 = bf16[512,768]{1,0:T(8,128)(2,1)} custom-call(bf16[320,1024]{1,0:T(8,128)(2,1)S(1)} %get-tuple-element.22.hg_ref, bf16[320,128]{1,0:T(8,128)(2,1)S(1)} %get-tuple-element.23.part_ref, bf16[1024,1024]{1,0:T(8,128)(2,1)S(1)} %bitcast.16, bf16[16,128]{1,0:T(8,128)(2,1)S(1)} %get-tuple-element.28._), custom_call_target="tpu_custom_call" | custom-call | flops 2000000000 | bytes 4194304 | tf_op jit(solution)/shard_map/pallas_call | solution.py:370
  81.6 7.3 %all-to-all-start.1 = ((bf16[64,8,768]{2,1,0:T(8,128)(2,1)}), bf16[64,8,768]{2,1,0:T(8,128)(2,1)S(1)}, u32[]{:S(2)}, u32[]{:S(2)}) async-start(bf16[64,8,768]{2,1,0:T(8,128)(2,1)} %bitcast.8), calls=%async_computation.1 | async-start | bytes 1572864 | tf_op jit(solution)/shard_map/all_to_all | solution.py:446
  88.9 2.0 %shard_map.99._ = bf16[128,2048]{1,0:T(8,128)(2,1)S(1)} custom-call(s32[2]{0:T(128)S(1)} %pad_add_fusion.place_ref, bf16[448,2048]{1,0:T(8,128)(2,1)} %get-tuple-element.32.refs_0_.own_hbm, bf16[448,2048]{1,0:T(8,128)(2,1)} %collective-permute-done.1.refs_1_.got_hbm, bf16[128,2048]{1,0:T(8,128)(2,1)S(1)} %collective-permute-done.2.refs_2_), custom_call_target="tpu_custom_call" | custom-call | flops 1000000 | bytes 1048576 | tf_op jit(solution)/shard_map/pallas_call | solution.py:400
  90.8 5.9 %collective-permute-start.3 = (bf16[128,2048]{1,0:T(8,128)(2,1)S(1)}, bf16[128,2048]{1,0:T(8,128)(2,1)S(1)}, u32[]{:S(2)}, u32[]{:S(2)}) collective-permute-start(bf16[128,2048]{1,0:T(8,128)(2,1)S(1)} %shard_map.99._), channel_id=1, source_target_pairs={{0,128},{64,960},{128,256},{192,64},{256,384},{320,192},{384,512},... | collective-permute-start | bytes 1572872 | tf_op jit(solution)/shard_map/ppermute | solution.py:457
  96.7 1.8 %shard_map.100.refs_0_ = bf16[320,2048]{1,0:T(8,128)(2,1)S(1)} custom-call(bf16[448,2048]{1,0:T(8,128)(2,1)} %get-tuple-element.32.refs_0_.own_hbm, bf16[448,2048]{1,0:T(8,128)(2,1)} %collective-permute-done.1.refs_1_.got_hbm, bf16[128,2048]{1,0:T(8,128)(2,1)S(1)} %shard_map.99._), custom_call_target="tpu_custom_call" | custom-call | flops 2000000000 | bytes 8388608 | tf_op jit(solution)/shard_map/pallas_call | solution.py:383
  98.6 4.3 %collective-permute-done.3.refs_1_ = bf16[128,2048]{1,0:T(8,128)(2,1)S(1)} collective-permute-done((bf16[128,2048]{1,0:T(8,128)(2,1)S(1)}, bf16[128,2048]{1,0:T(8,128)(2,1)S(1)}, u32[]{:S(2)}, u32[]{:S(2)}) %collective-permute-start.3) | collective-permute-done | bytes 524320 | tf_op jit(solution)/shard_map/ppermute | solution.py:457
  103.5 5.3 %collective-permute-start.4 = (bf16[128,2048]{1,0:T(8,128)(2,1)S(1)}, bf16[128,2048]{1,0:T(8,128)(2,1)S(1)}, u32[]{:S(2)}, u32[]{:S(2)}) collective-permute-start(bf16[128,2048]{1,0:T(8,128)(2,1)S(1)} %shard_map.101), channel_id=1, source_target_pairs={{0,128},{64,960},{128,256},{192,64},{256,384},{320,192},{384,512},... | collective-permute-start | bytes 1572872 | tf_op jit(solution)/shard_map/ppermute | solution.py:457
  108.8 6.1 %collective-permute-done.4.refs_1_ = bf16[128,2048]{1,0:T(8,128)(2,1)S(1)} collective-permute-done((bf16[128,2048]{1,0:T(8,128)(2,1)S(1)}, bf16[128,2048]{1,0:T(8,128)(2,1)S(1)}, u32[]{:S(2)}, u32[]{:S(2)}) %collective-permute-start.4) | collective-permute-done | bytes 524320 | tf_op jit(solution)/shard_map/ppermute | solution.py:457
  114.9 0.7 shard_map.102
  115.6 5.0 %collective-permute-start.5 = (bf16[64,2048]{1,0:T(8,128)(2,1)S(1)}, bf16[64,2048]{1,0:T(8,128)(2,1)S(1)}, u32[]{:S(2)}, u32[]{:S(2)}) collective-permute-start(bf16[64,2048]{1,0:T(8,128)(2,1)S(1)} %get-tuple-element.34), channel_id=1, source_target_pairs={{0,128},{64,960},{128,256},{192,64},{256,384},{320,192},{384,512},... | collective-permute-start | bytes 786440 | tf_op jit(solution)/shard_map/ppermute | solution.py:457
  120.7 6.1 %collective-permute-start.6 = (bf16[64,2048]{1,0:T(8,128)(2,1)S(1)}, bf16[64,2048]{1,0:T(8,128)(2,1)S(1)}, u32[]{:S(2)}, u32[]{:S(2)}) collective-permute-start(bf16[64,2048]{1,0:T(8,128)(2,1)S(1)} %get-tuple-element.35), channel_id=1, source_target_pairs={{0,192},{64,896},{128,320},{192,0},{256,448},{320,128},{384,576},{... | collective-permute-start | bytes 786440 | tf_op jit(solution)/shard_map/ppermute | solution.py:457
  126.8 1.7 %shard_map.98 = (bf16[32,4096]{1,0:T(8,128)(2,1)}, bf16[2,128]{1,0:T(2,128)(2,1)}) custom-call(bf16[512,768]{1,0:T(8,128)(2,1)S(1)} %bitcast.14, bf16[2,320,128]{2,1,0:T(8,128)(2,1)S(1)} %copy-done.2, bf16[2,128]{1,0:T(2,128)(2,1)S(1)} %bitcast.18), custom_call_target="tpu_custom_call" | custom-call | flops 10000000000 | bytes 2097152 | tf_op jit(solution)/shard_map/pallas_call | solution.py:426
  128.5 3.2 %collective-permute-done.6.refs_2_ = bf16[64,2048]{1,0:T(8,128)(2,1)S(1)} collective-permute-done((bf16[64,2048]{1,0:T(8,128)(2,1)S(1)}, bf16[64,2048]{1,0:T(8,128)(2,1)S(1)}, u32[]{:S(2)}, u32[]{:S(2)}) %collective-permute-start.6) | collective-permute-done | bytes 262176 | tf_op jit(solution)/shard_map/ppermute | solution.py:457
  131.7 0.9 shard_map.103
  (12 shorter events, 0.8 us)
Async XLA Ops:
  4.1 55.4 %all-to-all-start = ((bf16[64,8,1280]{2,1,0:T(8,128)(2,1)}), bf16[64,8,1280]{2,1,0:T(8,128)(2,1)S(1)}, u32[]{:S(2)}, u32[]{:S(2)}) async-start(bf16[64,8,1280]{2,1,0:T(8,128)(2,1)} %bitcast.19), calls=%async_computation | async-start | bytes 2621440 | tf_op jit(solution)/shard_map/all_to_all | solution.py:446
  64.1 7.5 %collective-permute-start = (bf16[128,2048]{1,0:T(8,128)(2,1)S(1)}, bf16[128,2048]{1,0:T(8,128)(2,1)S(1)}, u32[]{:S(2)}, u32[]{:S(2)}) collective-permute-start(bf16[128,2048]{1,0:T(8,128)(2,1)S(1)} %get-tuple-element.27.refs_0_), channel_id=1, source_target_pairs={{0,64},{64,0},{128,192},{192,128},{256,320},{320,256},{384,448},{4... | collective-permute-start | bytes 1572872 | tf_op jit(solution)/shard_map/ppermute | solution.py:460
  72.2 6.7 %copy-start = (bf16[1,1024,1024]{2,1,0:T(8,128)(2,1)S(1)}, bf16[1,1024,1024]{2,1,0:T(8,128)(2,1)}, u32[]{:S(2)}) copy-start(bf16[1,1024,1024]{2,1,0:T(8,128)(2,1)} %param.10) | copy-start | bytes 6291460
  76.0 12.9 %collective-permute-start.1 = (bf16[448,2048]{1,0:T(8,128)(2,1)}, bf16[448,2048]{1,0:T(8,128)(2,1)}, u32[]{:S(2)}, u32[]{:S(2)}) collective-permute-start(bf16[448,2048]{1,0:T(8,128)(2,1)} %get-tuple-element.33), channel_id=1, source_target_pairs={{0,64},{64,0},{128,192},{192,128},{256,320},{320,256},{384,448},{4... | collective-permute-start | bytes 5505032 | tf_op jit(solution)/shard_map/ppermute | solution.py:460
  78.3 10.6 %collective-permute-start.2 = (bf16[128,2048]{1,0:T(8,128)(2,1)S(1)}, bf16[128,2048]{1,0:T(8,128)(2,1)S(1)}, u32[]{:S(2)}, u32[]{:S(2)}) collective-permute-start(bf16[128,2048]{1,0:T(8,128)(2,1)S(1)} %shard_map.95._), channel_id=1, source_target_pairs={{0,128},{128,256},{256,384},{384,512},{512,640},{640,768},{768,896... | collective-permute-start | bytes 1572872 | tf_op jit(solution)/shard_map/ppermute | solution.py:457
  81.6 45.2 %all-to-all-start.1 = ((bf16[64,8,768]{2,1,0:T(8,128)(2,1)}), bf16[64,8,768]{2,1,0:T(8,128)(2,1)S(1)}, u32[]{:S(2)}, u32[]{:S(2)}) async-start(bf16[64,8,768]{2,1,0:T(8,128)(2,1)} %bitcast.8), calls=%async_computation.1 | async-start | bytes 1572864 | tf_op jit(solution)/shard_map/all_to_all | solution.py:446
  90.8 12.0 %collective-permute-start.3 = (bf16[128,2048]{1,0:T(8,128)(2,1)S(1)}, bf16[128,2048]{1,0:T(8,128)(2,1)S(1)}, u32[]{:S(2)}, u32[]{:S(2)}) collective-permute-start(bf16[128,2048]{1,0:T(8,128)(2,1)S(1)} %shard_map.99._), channel_id=1, source_target_pairs={{0,128},{64,960},{128,256},{192,64},{256,384},{320,192},{384,512},... | collective-permute-start | bytes 1572872 | tf_op jit(solution)/shard_map/ppermute | solution.py:457
  98.5 28.2 %copy-start.1 = (bf16[128,2]{0,1:T(2,128)(2,1)S(1)}, bf16[128,2]{0,1:T(2,128)(2,1)}, u32[]{:S(2)}) copy-start(bf16[128,2]{0,1:T(2,128)(2,1)} %param.9) | copy-start | bytes 1540
  98.6 28.2 %copy-start.2 = (bf16[2,320,128]{2,1,0:T(8,128)(2,1)S(1)}, bf16[2,320,128]{2,1,0:T(8,128)(2,1)}, u32[]{:S(2)}) copy-start(bf16[2,320,128]{2,1,0:T(8,128)(2,1)} %get-tuple-element.29.s_ref) | copy-start | bytes 491524
  103.5 11.4 %collective-permute-start.4 = (bf16[128,2048]{1,0:T(8,128)(2,1)S(1)}, bf16[128,2048]{1,0:T(8,128)(2,1)S(1)}, u32[]{:S(2)}, u32[]{:S(2)}) collective-permute-start(bf16[128,2048]{1,0:T(8,128)(2,1)S(1)} %shard_map.101), channel_id=1, source_target_pairs={{0,128},{64,960},{128,256},{192,64},{256,384},{320,192},{384,512},... | collective-permute-start | bytes 1572872 | tf_op jit(solution)/shard_map/ppermute | solution.py:457
  115.6 12.9 %collective-permute-start.5 = (bf16[64,2048]{1,0:T(8,128)(2,1)S(1)}, bf16[64,2048]{1,0:T(8,128)(2,1)S(1)}, u32[]{:S(2)}, u32[]{:S(2)}) collective-permute-start(bf16[64,2048]{1,0:T(8,128)(2,1)S(1)} %get-tuple-element.34), channel_id=1, source_target_pairs={{0,128},{64,960},{128,256},{192,64},{256,384},{320,192},{384,512},... | collective-permute-start | bytes 786440 | tf_op jit(solution)/shard_map/ppermute | solution.py:457
  120.7 11.0 %collective-permute-start.6 = (bf16[64,2048]{1,0:T(8,128)(2,1)S(1)}, bf16[64,2048]{1,0:T(8,128)(2,1)S(1)}, u32[]{:S(2)}, u32[]{:S(2)}) collective-permute-start(bf16[64,2048]{1,0:T(8,128)(2,1)S(1)} %get-tuple-element.35), channel_id=1, source_target_pairs={{0,192},{64,896},{128,320},{192,0},{256,448},{320,128},{384,576},{... | collective-permute-start | bytes 786440 | tf_op jit(solution)/shard_map/ppermute | solution.py:457
